TPU v7x, 32 devices: a whole 2x2x4 slice. The times are simulated.
32 devices in a mesh: dp: 8 (over z, y), mp: 4 (over x, core).
Axes of the slice: x: 2, y: 2, z: 4, core: 2. Of those that a mesh axis runs over, the one named last changes fastest.
Arguments:
- pixels: bfloat16 [8192, 3072], P('dp', 'mp'), may hold values from -6 to 6
- lengths: int32 [8, 8], P('dp'), may hold values from 25 to 576, as said below
- valid_mask: int32 [8192], P('dp'), may hold values from 0 to 1, as said below
- teacher_logits: float32 [64, 1000], P('dp'), may hold values from -12 to 12
- teacher_map: int32 [8], replicated, may hold values from 0 to 7, each once
- attend_in: float32 [3, 3, 768, 768], P(None, None, 'dp', 'mp'), may hold values from -0.21875 to 0.21875
- attend_out: float32 [3, 768, 768], P(None, 'mp', 'dp'), may hold values from -0.625 to 0.625
- hidden_up: float32 [3, 768, 3072], P(None, 'dp', 'mp'), may hold values from -0.21875 to 0.21875
- hidden_down: float32 [3, 3072, 768], P(None, 'mp', 'dp'), may hold values from -0.109375 to 0.109375
- patch_embed: float32 [3072, 768], P('mp', 'dp'), may hold values from -0.109375 to 0.109375
- class_head: float32 [768, 1000], P('dp'), may hold values from -0.21875 to 0.21875
- norm_params: float32 [7, 2, 768], P(None, None, 'dp'), may hold values from -0.9 to 2.2
- attend_in_first: float32 [3, 3, 768, 768], P(None, None, 'dp', 'mp'), may hold values from -7.1525574e-07 to 7.1525574e-07
- attend_out_first: float32 [3, 768, 768], P(None, 'mp', 'dp'), may hold values from -7.1525574e-07 to 7.1525574e-07
- hidden_up_first: float32 [3, 768, 3072], P(None, 'dp', 'mp'), may hold values from -7.1525574e-07 to 7.1525574e-07
- hidden_down_first: float32 [3, 3072, 768], P(None, 'mp', 'dp'), may hold values from -7.1525574e-07 to 7.1525574e-07
- patch_embed_first: float32 [3072, 768], P('mp', 'dp'), may hold values from -7.1525574e-07 to 7.1525574e-07
- class_head_first: float32 [768, 1000], P('dp'), may hold values from -7.1525574e-07 to 7.1525574e-07
- norm_params_first: float32 [7, 2, 768], P(None, None, 'dp'), may hold values from -1.9073486e-06 to 1.9073486e-06
- attend_in_second: float32 [3, 3, 768, 768], P(None, None, 'dp', 'mp'), may hold values from 1.0262321e-15 to 4.1049283e-15
- attend_out_second: float32 [3, 768, 768], P(None, 'mp', 'dp'), may hold values from 1.0262321e-15 to 4.1049283e-15
- hidden_up_second: float32 [3, 768, 3072], P(None, 'dp', 'mp'), may hold values from 1.0262321e-15 to 4.1049283e-15
- hidden_down_second: float32 [3, 3072, 768], P(None, 'mp', 'dp'), may hold values from 1.0262321e-15 to 4.1049283e-15
- patch_embed_second: float32 [3072, 768], P('mp', 'dp'), may hold values from 1.0262321e-15 to 4.1049283e-15
- class_head_second: float32 [768, 1000], P('dp'), may hold values from 1.0262321e-15 to 4.1049283e-15
- norm_params_second: float32 [7, 2, 768], P(None, None, 'dp'), may hold values from 9.23609e-15 to 3.694436e-14
Outputs:
- loss: float32 [], replicated
- grad_norm: float32 [], replicated
- attend_in_first_next: float32 [3, 3, 768, 768], P(None, None, 'dp', 'mp')
- attend_out_first_next: float32 [3, 768, 768], P(None, 'mp', 'dp')
- hidden_up_first_next: float32 [3, 768, 3072], P(None, 'dp', 'mp')
- hidden_down_first_next: float32 [3, 3072, 768], P(None, 'mp', 'dp')
- patch_embed_first_next: float32 [3072, 768], P('mp', 'dp')
- class_head_first_next: float32 [768, 1000], P('dp')
- norm_params_first_next: float32 [7, 2, 768], P(None, None, 'dp')
- attend_in_second_next: float32 [3, 3, 768, 768], P(None, None, 'dp', 'mp')
- attend_out_second_next: float32 [3, 768, 768], P(None, 'mp', 'dp')
- hidden_up_second_next: float32 [3, 768, 3072], P(None, 'dp', 'mp')
- hidden_down_second_next: float32 [3, 3072, 768], P(None, 'mp', 'dp')
- patch_embed_second_next: float32 [3072, 768], P('mp', 'dp')
- class_head_second_next: float32 [768, 1000], P('dp')
- norm_params_second_next: float32 [7, 2, 768], P(None, None, 'dp')
- attend_in_next: float32 [3, 3, 768, 768], P(None, None, 'dp', 'mp')
- attend_out_next: float32 [3, 768, 768], P(None, 'mp', 'dp')
- hidden_up_next: float32 [3, 768, 3072], P(None, 'dp', 'mp')
- hidden_down_next: float32 [3, 3072, 768], P(None, 'mp', 'dp')
- patch_embed_next: float32 [3072, 768], P('mp', 'dp')
- class_head_next: float32 [768, 1000], P('dp')
- norm_params_next: float32 [7, 2, 768], P(None, None, 'dp')
Inputs may be any that keep to these rules, and one draw needn't show every extreme that they name: `lengths`: each row sums to 1024; one image of every device has exactly 576 tokens. `teacher_map`: a permutation of the dp indices. `valid_mask`: all tokens of one image of one device are 0.
All inputs are finite; a program needn't handle non-finite values.
Results may differ from a plain program's by a relative error of at most 0.018.
Values may be sent and summed in bfloat16 or wider, within the bound.
No kernel may reach another device: no remote copies, remote signals or barrier semaphores. Data moves between devices by JAX's collectives and lax.ppermute only.
A program may use at most 192 MiB of HBM per device.

v0:
```python
import jax
import jax.numpy as jnp
from jax import lax
from jax.sharding import PartitionSpec as P

HEAD_DIM = 64
LAYERS = 3
STEP = 10


EPSILON = 1e-06
MASKED = -30000.0
CLIP = 0.005
BETA_ONE = 0.9
BETA_TWO = 0.999
ADAM_EPS = 1e-08
RATES = (0.02, 0.06, 0.02, 0.02, 0.02, 0.02, 0.5)
DECAYS = (0.05, 0.05, 0.05, 0.05, 0.05, 0.05, 0.0)
SQRT_HALF = 0.7071067811865476
INV_ROOT = 0.3989422804014327
HIGH = lax.Precision.HIGHEST


def layer_norm(value, gain, bias):
    centred = value - jnp.mean(value, -1, keepdims=True)
    variance = jnp.mean(centred * centred, -1, keepdims=True)
    return centred * lax.rsqrt(variance + EPSILON) * gain + bias


def gather_rows(value):
    return lax.all_gather(value, "mp", axis=0, tiled=True)


def scatter_rows(left, right, rows):

    def term(start, count):
        return jnp.dot(left, right, preferred_element_type=jnp.float32)

    return lax.psum_scatter(
        term(jnp.int32(0), rows * lax.axis_size("mp")), "mp", scatter_dimension=0, tiled=True
    )


def gather_grad(value):
    return lax.all_gather(value.astype(jnp.bfloat16), "mp", axis=0, tiled=True)


def scatter_grad(term, rows):
    return lax.psum_scatter(
        term(jnp.int32(0), rows * lax.axis_size("mp")).astype(jnp.bfloat16),
        "mp",
        scatter_dimension=0,
        tiled=True,
    ).astype(jnp.float32)


def head_scores(item, keep):
    scores = jnp.einsum(
        "tc,sc->ts", item[0], item[1], preferred_element_type=jnp.float32
    ) * HEAD_DIM ** (-0.5)
    return jax.nn.softmax(jnp.where(keep, scores, MASKED), -1)


def head_forward(item, keep):
    probs = head_scores(item, keep)
    return jnp.dot(probs.astype(jnp.bfloat16), item[2], preferred_element_type=jnp.float32)


def head_backward(item, d_out, keep):
    probs = head_scores(item, keep)
    d_probs = jnp.einsum("tc,sc->ts", d_out, item[2], preferred_element_type=jnp.float32)
    delta = jnp.sum(probs * d_probs, -1, keepdims=True)
    d_scores = jnp.where(keep, probs * (d_probs - delta), 0.0).astype(jnp.bfloat16)
    scale = HEAD_DIM ** (-0.5)
    d_query = jnp.dot(d_scores, item[1], preferred_element_type=jnp.float32) * scale
    d_key = jnp.einsum("ts,tc->sc", d_scores, item[0], preferred_element_type=jnp.float32) * scale
    d_value = jnp.einsum(
        "ts,tc->sc", probs.astype(jnp.bfloat16), d_out, preferred_element_type=jnp.float32
    )
    return jnp.stack([d_query, d_key, d_value]).astype(jnp.bfloat16)


def layer_forward(x, layer_weights, norms, keep):
    attend_in, attend_out, hidden_up, hidden_down = layer_weights
    rows = x.shape[0]
    normed = gather_rows(layer_norm(x, norms[0, 0], norms[0, 1]).astype(jnp.bfloat16))
    tokens = normed.shape[0]
    mixed = jnp.einsum("td,jdc->jtc", normed, attend_in, preferred_element_type=jnp.float32).astype(
        jnp.bfloat16
    )
    per_head = mixed.reshape(3, tokens, -1, HEAD_DIM).transpose(2, 0, 1, 3)
    outputs = lax.map(lambda item: head_forward(item, keep), per_head)
    attended = outputs.transpose(1, 0, 2).reshape(tokens, -1).astype(jnp.bfloat16)
    middle = x + scatter_rows(attended, attend_out, rows)
    normed_two = gather_rows(layer_norm(middle, norms[1, 0], norms[1, 1]).astype(jnp.bfloat16))
    up_value = jnp.dot(normed_two, hidden_up, preferred_element_type=jnp.float32)
    active = jax.nn.gelu(up_value, approximate=False).astype(jnp.bfloat16)
    result = middle + scatter_rows(active, hidden_down, rows)
    return (result, (x, middle, normed, per_head, attended, normed_two, up_value, active))


def layer_backward(d_x, saved, layer_weights, norms, keep):
    x, middle, normed, per_head, attended, normed_two, up_value, active = saved
    attend_in, attend_out, hidden_up, hidden_down = layer_weights
    rows = x.shape[0]
    d_full = gather_grad(d_x)
    d_active = jnp.einsum("td,fd->tf", d_full, hidden_down, preferred_element_type=jnp.float32)
    g_down = jnp.einsum("tf,td->fd", active, d_full, preferred_element_type=jnp.float32)
    slope = (
        0.5 * (1.0 + lax.erf(up_value * SQRT_HALF))
        + up_value * jnp.exp(-0.5 * up_value * up_value) * INV_ROOT
    )
    d_up = (d_active * slope).astype(jnp.bfloat16)
    g_up = jnp.einsum("td,tf->df", normed_two, d_up, preferred_element_type=jnp.float32)

    def up_term(start, count):
        return jnp.einsum("tf,df->td", d_up, hidden_up, preferred_element_type=jnp.float32)

    d_normed_two = scatter_grad(up_term, rows)
    d_mid, g_gain_two, g_bias_two = jax.vjp(layer_norm, middle, norms[1, 0], norms[1, 1])[1](
        d_normed_two
    )
    d_mid = d_x + d_mid
    d_full = gather_grad(d_mid)
    tokens = d_full.shape[0]
    d_att = jnp.einsum("td,cd->tc", d_full, attend_out, preferred_element_type=jnp.float32).astype(
        jnp.bfloat16
    )
    g_out = jnp.einsum("tc,td->cd", attended, d_full, preferred_element_type=jnp.float32)
    d_heads = d_att.reshape(tokens, -1, HEAD_DIM).transpose(1, 0, 2)
    d_per_head = lax.map(lambda pair: head_backward(pair[0], pair[1], keep), (per_head, d_heads))
    d_mixed = d_per_head.transpose(1, 2, 0, 3).reshape(3, tokens, -1)
    g_in = jnp.einsum("td,jtc->jdc", normed, d_mixed, preferred_element_type=jnp.float32)

    def in_term(start, count):
        return jnp.einsum("jtc,jdc->td", d_mixed, attend_in, preferred_element_type=jnp.float32)

    d_normed = scatter_grad(in_term, rows)
    d_lower, g_gain_one, g_bias_one = jax.vjp(layer_norm, x, norms[0, 0], norms[0, 1])[1](d_normed)
    norm_grads = jnp.stack(
        [jnp.stack([g_gain_one, g_bias_one]), jnp.stack([g_gain_two, g_bias_two])]
    )
    return (d_mid + d_lower, (g_in, g_out, g_up, g_down), norm_grads)


def adam(weight, grad, first, second, rate, decay):
    first = BETA_ONE * first + (1.0 - BETA_ONE) * grad
    second = BETA_TWO * second + (1.0 - BETA_TWO) * grad * grad
    update = first / (1.0 - BETA_ONE**STEP) / (jnp.sqrt(second / (1.0 - BETA_TWO**STEP)) + ADAM_EPS)
    return (first, second, weight - rate * (update + decay * weight))


def body(
    pixels,
    lengths,
    valid_mask,
    teacher_logits,
    teacher_map,
    attend_in,
    attend_out,
    hidden_up,
    hidden_down,
    patch_embed,
    class_head,
    norm_params,
    attend_in_first,
    attend_out_first,
    hidden_up_first,
    hidden_down_first,
    patch_embed_first,
    class_head_first,
    norm_params_first,
    attend_in_second,
    attend_out_second,
    hidden_up_second,
    hidden_down_second,
    patch_embed_second,
    class_head_second,
    norm_params_second,
):
    in_all, out_all, up_all, down_all, patch_all, head_all, norms_all = (
        lax.all_gather(attend_in.astype(jnp.bfloat16), "dp", axis=2, tiled=True),
        lax.all_gather(attend_out.astype(jnp.bfloat16), "dp", axis=2, tiled=True),
        lax.all_gather(hidden_up.astype(jnp.bfloat16), "dp", axis=1, tiled=True),
        lax.all_gather(hidden_down.astype(jnp.bfloat16), "dp", axis=2, tiled=True),
        lax.all_gather(patch_embed.astype(jnp.bfloat16), "dp", axis=1, tiled=True),
        lax.all_gather(class_head.astype(jnp.bfloat16), "dp", axis=0, tiled=True),
        lax.all_gather(norm_params.astype(jnp.bfloat16), "dp", axis=2, tiled=True),
    )
    norms_all = norms_all.astype(jnp.float32)
    tokens = pixels.shape[0]
    rows = tokens // lax.axis_size("mp")
    offset = lax.axis_index("mp") * rows
    position = jnp.arange(tokens, dtype=jnp.int32)
    ends = jnp.cumsum(lengths[0])
    segment = jnp.sum((position[:, None] >= ends[None, :]).astype(jnp.int32), 1)
    keep = (segment[:, None] == segment[None, :]) & (valid_mask[None, :] > 0)
    images = lengths.shape[1]
    image_ids = jnp.arange(images, dtype=jnp.int32)[:, None]
    member_all = ((segment[None, :] == image_ids) & (valid_mask[None, :] > 0)).astype(jnp.float32)
    count = jnp.sum(member_all, 1)
    member = lax.dynamic_slice_in_dim(member_all, offset, rows, 1)
    x = scatter_rows(pixels, patch_all, rows)
    saved = []
    for layer in range(LAYERS):
        weights = (in_all[layer], out_all[layer], up_all[layer], down_all[layer])
        x, kept = layer_forward(x, weights, norms_all[2 * layer : 2 * layer + 2], keep)
        saved.append(kept)
    pooled_sum = lax.psum(jnp.dot(member, x, precision=HIGH), "mp")
    divisor = jnp.maximum(count, 1.0)[:, None]
    pooled = pooled_sum / divisor
    final_gain, final_bias = (norms_all[-1, 0], norms_all[-1, 1])
    pooled_normed = layer_norm(pooled, final_gain, final_bias).astype(jnp.bfloat16)
    logits = jnp.dot(pooled_normed, head_all, preferred_element_type=jnp.float32)
    me = lax.axis_index("dp")
    teacher_count = teacher_map.shape[0]
    piece = lax.all_gather(teacher_logits, "dp", axis=0, tiled=True)
    index = jnp.arange(piece.shape[0], dtype=jnp.int32)
    owner = index // images
    within = index % images
    target = jnp.sum(
        (owner[:, None] == jnp.arange(teacher_count, dtype=jnp.int32)[None, :])
        * teacher_map[None, :],
        1,
    )
    select = (
        (target == me)[None, :] & (within[None, :] == jnp.arange(images, dtype=jnp.int32)[:, None])
    ).astype(jnp.float32)
    teacher = jnp.dot(select, piece, precision=HIGH)
    teach_log = jax.nn.log_softmax(teacher, -1)
    student_log = jax.nn.log_softmax(logits, -1)
    total_images = images * lax.axis_size("dp")
    loss_local = jnp.sum(jnp.exp(teach_log) * (teach_log - student_log))
    d_logits = ((jnp.exp(student_log) - jnp.exp(teach_log)) / total_images).astype(jnp.bfloat16)
    g_head = jnp.einsum("id,ic->dc", pooled_normed, d_logits, preferred_element_type=jnp.float32)
    d_pooled_normed = jnp.einsum(
        "ic,dc->id", d_logits, head_all, preferred_element_type=jnp.float32
    )
    d_pooled, g_final_gain, g_final_bias = jax.vjp(layer_norm, pooled, final_gain, final_bias)[1](
        d_pooled_normed
    )
    d_x = jnp.einsum("is,id->sd", member, d_pooled / divisor, precision=HIGH)
    layer_grads = [None] * LAYERS
    norm_grads = [None] * LAYERS
    for layer in reversed(range(LAYERS)):
        weights = (in_all[layer], out_all[layer], up_all[layer], down_all[layer])
        d_x, grads, norm_grads[layer] = layer_backward(
            d_x, saved[layer], weights, norms_all[2 * layer : 2 * layer + 2], keep
        )
        layer_grads[layer] = grads
    d_full = gather_grad(d_x)
    g_patch = jnp.einsum("tp,td->pd", pixels, d_full, preferred_element_type=jnp.float32)
    stacked = [jnp.stack([grads[kind] for grads in layer_grads]) for kind in range(4)]
    reduced = (
        lax.psum_scatter(stacked[0], "dp", scatter_dimension=2, tiled=True),
        lax.psum_scatter(stacked[1], "dp", scatter_dimension=2, tiled=True),
        lax.psum_scatter(stacked[2], "dp", scatter_dimension=1, tiled=True),
        lax.psum_scatter(stacked[3], "dp", scatter_dimension=2, tiled=True),
        lax.psum_scatter(g_patch, "dp", scatter_dimension=1, tiled=True),
    )
    stacked = list(reduced[:4])
    g_patch = reduced[4]
    first_model = (lax.axis_index("mp") == 0).astype(jnp.float32)
    final_grads = first_model * jnp.stack([g_final_gain, g_final_bias])[None]
    norm_full = jnp.concatenate(norm_grads + [final_grads], 0)
    head_grad, norm_grad, loss = lax.psum(
        (first_model * g_head, norm_full, first_model * loss_local), ("dp", "mp")
    )
    width = class_head.shape[0]
    start = lax.axis_index("dp") * width
    head_grad = lax.dynamic_slice_in_dim(head_grad, start, width, 0)
    norm_grad = lax.dynamic_slice_in_dim(norm_grad, start, width, 2)
    big = (stacked[0], stacked[1], stacked[2], stacked[3], g_patch)
    squares = sum((jnp.sum(g * g) for g in big)) + first_model * (
        jnp.sum(head_grad * head_grad) + jnp.sum(norm_grad * norm_grad)
    )
    grad_norm = jnp.sqrt(lax.psum(squares, ("dp", "mp")))
    clip = jnp.minimum(1.0, CLIP / grad_norm)
    masters = (attend_in, attend_out, hidden_up, hidden_down, patch_embed, class_head, norm_params)
    firsts = (
        attend_in_first,
        attend_out_first,
        hidden_up_first,
        hidden_down_first,
        patch_embed_first,
        class_head_first,
        norm_params_first,
    )
    seconds = (
        attend_in_second,
        attend_out_second,
        hidden_up_second,
        hidden_down_second,
        patch_embed_second,
        class_head_second,
        norm_params_second,
    )
    all_grads = big + (head_grad, norm_grad)
    results = []
    for kind in range(7):
        results.append(
            adam(
                masters[kind],
                all_grads[kind] * clip,
                firsts[kind],
                seconds[kind],
                RATES[kind],
                DECAYS[kind],
            )
        )
    return (
        loss,
        grad_norm,
        results[0][0],
        results[1][0],
        results[2][0],
        results[3][0],
        results[4][0],
        results[5][0],
        results[6][0],
        results[0][1],
        results[1][1],
        results[2][1],
        results[3][1],
        results[4][1],
        results[5][1],
        results[6][1],
        results[0][2],
        results[1][2],
        results[2][2],
        results[3][2],
        results[4][2],
        results[5][2],
        results[6][2],
    )


def solution(mesh):
    placed = (
        P("dp", "mp"),
        P("dp", None),
        P("dp"),
        P("dp", None),
        P(),
        P(None, None, "dp", "mp"),
        P(None, "mp", "dp"),
        P(None, "dp", "mp"),
        P(None, "mp", "dp"),
        P("mp", "dp"),
        P("dp", None),
        P(None, None, "dp"),
        P(None, None, "dp", "mp"),
        P(None, "mp", "dp"),
        P(None, "dp", "mp"),
        P(None, "mp", "dp"),
        P("mp", "dp"),
        P("dp", None),
        P(None, None, "dp"),
        P(None, None, "dp", "mp"),
        P(None, "mp", "dp"),
        P(None, "dp", "mp"),
        P(None, "mp", "dp"),
        P("mp", "dp"),
        P("dp", None),
        P(None, None, "dp"),
    )
    return jax.shard_map(
        body,
        mesh=mesh,
        in_specs=placed,
        out_specs=(
            P(),
            P(),
            P(None, None, "dp", "mp"),
            P(None, "mp", "dp"),
            P(None, "dp", "mp"),
            P(None, "mp", "dp"),
            P("mp", "dp"),
            P("dp", None),
            P(None, None, "dp"),
            P(None, None, "dp", "mp"),
            P(None, "mp", "dp"),
            P(None, "dp", "mp"),
            P(None, "mp", "dp"),
            P("mp", "dp"),
            P("dp", None),
            P(None, None, "dp"),
            P(None, None, "dp", "mp"),
            P(None, "mp", "dp"),
            P(None, "dp", "mp"),
            P(None, "mp", "dp"),
            P("mp", "dp"),
            P("dp", None),
            P(None, None, "dp"),
        ),
        check_vma=False,
    )
```

profile of v0, /device:TPU:0, one launch (start us, length us, event | category | flops | bytes accessed | tf_op | source)
XLA Modules:
  0.0 2190.1 jit_solution(10618691995887647706)
XLA Ops:
  9.1 45.5 %all-gather.19.cloned.1.call-done = bf16[768,768]{0,1:T(8,128)(2,1)} async-done(((bf16[768,96]{0,1:T(8,128)(2,1)}), bf16[768,768]{0,1:T(8,128)(2,1)}) %all-gather.19.cloned.1.call-update) | async-done | bytes 1179664 | tf_op jit(solution)/shard_map/all_gather | solution.py:186
  61.6 31.0 %all_gather.65 = bf16[7,2,768]{0,1,2:T(2,128)(2,1)S(1)} all-gather(bf16[7,2,96]{0,1,2:T(2,128)(2,1)S(1)} %copy.187), channel_id=1, replica_groups=mesh['dp'=8,'mp'=4] {'dp'}, dimensions={2}, use_global_device_ids=true | all-gather | bytes 24192 | tf_op jit(solution)/shard_map/all_gather | solution.py:188
  92.9 39.8 %slice_reduce_fusion.3 = (f32[768]{0:T(1024)}, f32[768]{0:T(1024)}, f32[768]{0:T(1024)}, f32[768]{0:T(1024)}, f32[768]{0:T(1024)}, /*index=5*/f32[768]{0:T(1024)...) fusion(f32[7,2,768]{0,1,2:T(2,128)S(1)} %convert_element_type.248), kind=kLoop, calls=%fused_computation.373 | loop fusion | bytes 86016 | tf_op jit(solution)/shard_map/slice | solution.py:95
  138.2 45.0 %all_gather.68 = bf16[3,192,768]{1,0,2:T(4,128)(2,1)S(1)} all-gather(bf16[3,192,96]{1,0,2:T(4,128)(2,1)S(1)} %copy.191), channel_id=1, replica_groups=mesh['dp'=8,'mp'=4] {'dp'}, dimensions={2}, use_global_device_ids=true | all-gather | bytes 995328 | tf_op jit(solution)/shard_map/all_gather | solution.py:183
  265.8 37.2 %reduce-scatter.27.cloned.1.call-done = f32[256,768]{1,0:T(8,128)} async-done(((f32[1024,768]{1,0:T(8,128)}), f32[256,768]{1,0:T(8,128)}) %reduce-scatter.27.cloned.1.call-update) | async-done | bytes 786448 | tf_op jit(solution)/shard_map/reduce_scatter | solution.py:39
  307.8 63.0 %all-gather.27.cloned.1.call-done = bf16[3,768,768]{2,1,0:T(8,128)(2,1)} async-done(((bf16[3,96,768]{2,1,0:T(8,128)(2,1)}), bf16[3,768,768]{2,1,0:T(8,128)(2,1)}) %all-gather.27.cloned.1.call-update) | async-done | bytes 3538960 | tf_op jit(solution)/shard_map/all_gather | solution.py:184
  402.3 56.9 %all-gather.29.cloned.1.call-done = bf16[3,768,768]{1,2,0:T(8,128)(2,1)} async-done(((bf16[3,768,96]{1,2,0:T(8,128)(2,1)}), bf16[3,768,768]{1,2,0:T(8,128)(2,1)}) %all-gather.29.cloned.1.call-update) | async-done | bytes 3538960 | tf_op jit(solution)/shard_map/all_gather | solution.py:185
  464.0 36.5 %reduce-scatter.29.cloned.1.call-done = f32[256,768]{1,0:T(8,128)} async-done(((f32[1024,768]{1,0:T(8,128)}), f32[256,768]{1,0:T(8,128)}) %reduce-scatter.29.cloned.1.call-update) | async-done | bytes 786448 | tf_op jit(solution)/shard_map/reduce_scatter | solution.py:39
  528.2 30.4 %while.67 = (s32[]{:T(128)}, bf16[3,1024,64]{1,2,0:T(8,128)(2,1)S(1)}, bf16[3,3,1024,64]{3,2,1,0:T(8,128)(2,1)}, s32[1024]{0:T(1024)S(1)}, pred[1024]{0:T(1024)(...) while((s32[]{:T(128)}, bf16[3,1024,64]{1,2,0:T(8,128)(2,1)S(1)}, ...), condition=%wide.region_21.23_spmd.clone, body=%wide.region_18.22_spmd.clone.sunk | while | flops 287307776 | bytes 30454936 | solution.py:92
  561.0 38.0 %reduce-scatter.31.cloned.1.call-done = f32[256,768]{1,0:T(8,128)} async-done(((f32[1024,768]{1,0:T(8,128)}), f32[256,768]{1,0:T(8,128)}) %reduce-scatter.31.cloned.1.call-update) | async-done | bytes 786448 | tf_op jit(solution)/shard_map/reduce_scatter | solution.py:39
  638.0 38.1 %reduce-scatter.33.cloned.1.call-done = f32[256,768]{1,0:T(8,128)} async-done(((f32[1024,768]{1,0:T(8,128)}), f32[256,768]{1,0:T(8,128)}) %reduce-scatter.33.cloned.1.call-update) | async-done | bytes 786448 | tf_op jit(solution)/shard_map/reduce_scatter | solution.py:39
  736.5 38.0 %reduce-scatter.35.cloned.1.call-done = f32[256,768]{1,0:T(8,128)} async-done(((f32[1024,768]{1,0:T(8,128)}), f32[256,768]{1,0:T(8,128)}) %reduce-scatter.35.cloned.1.call-update) | async-done | bytes 786448 | tf_op jit(solution)/shard_map/reduce_scatter | solution.py:39
  815.0 31.0 %all_gather.63 = f32[64,1000]{1,0:T(8,128)S(1)} all-gather(f32[8,1000]{1,0:T(8,128)} %param.42), channel_id=1, replica_groups=mesh['dp'=8,'mp'=4] {'dp'}, dimensions={0}, use_global_device_ids=true | all-gather | bytes 288000 | tf_op jit(solution)/shard_map/all_gather | solution.py:217
  863.6 34.8 %all-gather.39.cloned.1.call-done = bf16[768,1000]{1,0:T(8,128)(2,1)} async-done(((bf16[96,1000]{1,0:T(8,128)(2,1)}), bf16[768,1000]{1,0:T(8,128)(2,1)}) %all-gather.39.cloned.1.call-update) | async-done | bytes 1536016 | tf_op jit(solution)/shard_map/all_gather | solution.py:187
  992.7 49.2 %while.69 = (s32[]{:T(128)}, bf16[3,3,1024,64]{2,3,0,1:T(8,128)(2,1)}, bf16[3,3,1024,64]{3,2,1,0:T(8,128)(2,1)}, bf16[3,1024,64]{2,1,0:T(8,128)(2,1)S(1)}, s32[1...) while((s32[]{:T(128)}, ...), condition=%wide.region_51.53_spmd.clone, body=%wide.region_47.52_spmd.clone.sunk | while | flops 699855872 | bytes 59698856 | solution.py:131
  1165.9 47.2 %while.70 = (s32[]{:T(128)}, bf16[3,3,1024,64]{2,3,0,1:T(8,128)(2,1)S(1)}, bf16[3,3,1024,64]{3,2,1,0:T(8,128)(2,1)}, bf16[3,1024,64]{2,1,0:T(8,128)(2,1)S(1)}, s...) while((s32[]{:T(128)}, ...), condition=%wide.region_62.64_spmd.clone, body=%wide.region_58.63_spmd.clone.sunk | while | flops 699855872 | bytes 59698348 | solution.py:131
  1340.6 49.2 %while.71 = (s32[]{:T(128)}, bf16[3,3,1024,64]{2,3,0,1:T(8,128)(2,1)}, bf16[3,3,1024,64]{3,2,1,0:T(8,128)(2,1)}, bf16[3,1024,64]{2,1,0:T(8,128)(2,1)S(1)}, s32[1...) while((s32[]{:T(128)}, ...), condition=%wide.region_73.75_spmd.clone, body=%wide.region_69.74_spmd.clone.sunk | while | flops 699855872 | bytes 59698856 | solution.py:131
  1521.7 69.5 %all-reduce.3.cloned.1.call-done = f32[768,1000]{1,0:T(8,128)} async-done(((f32[768,1000]{1,0:T(8,128)}), f32[768,1000]{1,0:T(8,128)}) %all-reduce.3.cloned.1.call-update) | async-done | bytes 3072016 | tf_op jit(solution)/shard_map/psum | solution.py:266
  1593.3 40.3 %psum.38 = f32[7,2,768]{2,1,0:T(2,128)S(1)} all-reduce(f32[7,2,768]{2,1,0:T(2,128)S(1)} %constant_dynamic-update-slice_fusion), channel_id=1, replica_groups=mesh['dp'=8,'mp'=4] {'dp','mp'}, use_global_device_ids=true, to_apply=%region_103.105 | all-reduce | flops 10752 | bytes 86016 | tf_op jit(solution)/shard_map/psum | solution.py:266
  1662.5 130.2 %reduce-scatter.59.cloned.1.call-done = f32[96,2304]{1,0:T(8,128)} async-done(((f32[768,2304]{1,0:T(8,128)}), f32[96,2304]{1,0:T(8,128)}) %reduce-scatter.59.cloned.1.call-update) | async-done | bytes 884752
  1795.7 128.7 %reduce-scatter.49.cloned.1.call-done = f32[3,96,768]{2,1,0:T(8,128)} async-done(((f32[3,768,768]{2,1,0:T(8,128)}), f32[3,96,768]{2,1,0:T(8,128)}) %reduce-scatter.49.cloned.1.call-update) | async-done | bytes 884752 | tf_op jit(solution)/shard_map/reduce_scatter | solution.py:257
  1928.6 67.6 %reduce-scatter.53.cloned.1.call-done = f32[768,96]{0,1:T(8,128)} async-done(((f32[768,768]{0,1:T(8,128)}), f32[768,96]{0,1:T(8,128)}) %reduce-scatter.53.cloned.1.call-update) | async-done | bytes 294928 | tf_op jit(solution)/shard_map/reduce_scatter | solution.py:259
  1997.8 107.6 %reduce-scatter.55.cloned.1.call-done = f32[96,1728]{1,0:T(8,128)} async-done(((f32[768,1728]{1,0:T(8,128)}), f32[96,1728]{1,0:T(8,128)}) %reduce-scatter.55.cloned.1.call-update) | async-done | bytes 663568
  2117.9 40.1 %all-reduce = (f32[]{:T(128)}, f32[]{:T(128)}) all-reduce(f32[]{:T(128)S(6)} %mul.998, f32[]{:T(128)S(6)} %add.464), channel_id=1, replica_groups=mesh['dp'=8,'mp'=4] {'dp','mp'}, use_global_device_ids=true, to_apply=%region_41.43 | all-reduce | flops 2 | bytes 16 | tf_op jit(solution)/shard_map/psum | solution.py:266
  (758 shorter events, 1106.9 us)
Async XLA Ops:
  9.0 123.7 %reduce-scatter.25.cloned.1.call-start = ((), (), s32[]{:S(2)}) async-start(), calls=%async_computation.19 | async-start | bytes 3932160 | tf_op jit(solution)/shard_map/reduce_scatter | solution.py:39
  58.9 145.3 %all-gather.23.cloned.1.call-start = ((), (), s32[]{:S(2)}) async-start(), calls=%async_computation.21 | async-start | bytes 5308416 | tf_op jit(solution)/shard_map/all_gather | solution.py:182
  61.4 164.9 %all-gather.21.cloned.1.call-start = ((), (), s32[]{:S(2)}) async-start(), calls=%async_computation.20 | async-start | bytes 1966080 | tf_op jit(solution)/shard_map/all_gather | solution.py:31
  137.7 165.3 %reduce-scatter.27.cloned.1.call-start = ((), (), s32[]{:S(2)}) async-start(), calls=%async_computation.22 | async-start | bytes 3932160 | tf_op jit(solution)/shard_map/reduce_scatter | solution.py:39
  264.9 106.0 %all-gather.27.cloned.1.call-start = ((), (), s32[]{:S(2)}) async-start(), calls=%async_computation.24 | async-start | bytes 3981312 | tf_op jit(solution)/shard_map/all_gather | solution.py:184
  265.8 125.4 %all-gather.25.cloned.1.call-start = ((), (), s32[]{:S(2)}) async-start(), calls=%async_computation.23 | async-start | bytes 1966080 | tf_op jit(solution)/shard_map/all_gather | solution.py:31
  305.6 153.6 %all-gather.29.cloned.1.call-start = ((), (), s32[]{:S(2)}) async-start(), calls=%async_computation.25 | async-start | bytes 3981312 | tf_op jit(solution)/shard_map/all_gather | solution.py:185
  307.6 193.0 %reduce-scatter.29.cloned.1.call-start = ((), (), s32[]{:S(2)}) async-start(), calls=%async_computation.26 | async-start | bytes 3932160 | tf_op jit(solution)/shard_map/reduce_scatter | solution.py:39
  503.2 95.9 %reduce-scatter.31.cloned.1.call-start = ((), (), s32[]{:S(2)}) async-start(), calls=%async_computation.28 | async-start | bytes 3932160 | tf_op jit(solution)/shard_map/reduce_scatter | solution.py:39
  601.7 74.4 %reduce-scatter.33.cloned.1.call-start = ((), (), s32[]{:S(2)}) async-start(), calls=%async_computation.30 | async-start | bytes 3932160 | tf_op jit(solution)/shard_map/reduce_scatter | solution.py:39
  678.6 95.9 %reduce-scatter.35.cloned.1.call-start = ((), (), s32[]{:S(2)}) async-start(), calls=%async_computation.32 | async-start | bytes 3932160 | tf_op jit(solution)/shard_map/reduce_scatter | solution.py:39
  777.1 74.3 %reduce-scatter.37.cloned.1.call-start = ((), (), s32[]{:S(2)}) async-start(), calls=%async_computation.34 | async-start | bytes 3932160 | tf_op jit(solution)/shard_map/reduce_scatter | solution.py:39
  813.3 85.2 %all-gather.39.cloned.1.call-start = ((), (), s32[]{:S(2)}) async-start(), calls=%async_computation.35 | async-start | bytes 1769472 | tf_op jit(solution)/shard_map/all_gather | solution.py:187
  815.0 109.2 %all-gather.41.cloned.1.call-start = ((), (), s32[]{:S(2)}) async-start(), calls=%async_computation.36 | async-start | bytes 1966080 | tf_op jit(solution)/shard_map/all_gather | solution.py:45
  967.5 106.9 %reduce-scatter.41.cloned.1.call-start = ((), (), s32[]{:S(2)}) async-start(), calls=%async_computation.39 | async-start | bytes 1966080 | tf_op jit(solution)/shard_map/reduce_scatter | solution.py:49
  1143.5 102.3 %reduce-scatter.45.cloned.1.call-start = ((), (), s32[]{:S(2)}) async-start(), calls=%async_computation.43 | async-start | bytes 1966080 | tf_op jit(solution)/shard_map/reduce_scatter | solution.py:49
  1315.5 106.9 %reduce-scatter.51.cloned.1.call-start = ((), (), s32[]{:S(2)}) async-start(), calls=%async_computation.48 | async-start | bytes 1966080 | tf_op jit(solution)/shard_map/reduce_scatter | solution.py:49
  1394.1 88.1 %all-gather.53.cloned.1.call-start = ((), (), s32[]{:S(2)}) async-start(), calls=%async_computation.49 | async-start | bytes 1966080 | tf_op jit(solution)/shard_map/all_gather | solution.py:45
  1427.5 163.8 %all-reduce.3.cloned.1.call-start = ((), (), s32[]{:S(2)}) async-start(), calls=%async_computation.51 | async-start | bytes 6291456 | tf_op jit(solution)/shard_map/psum | solution.py:266
  1430.0 230.4 %reduce-scatter.57.cloned.1.call-start = ((), (), s32[]{:S(2)}) async-start(), calls=%async_computation.53 | async-start | bytes 2211840
  1442.3 350.4 %reduce-scatter.59.cloned.1.call-start = ((), (), s32[]{:S(2)}) async-start(), calls=%async_computation.54 | async-start | bytes 7962624
  1471.4 452.9 %reduce-scatter.49.cloned.1.call-start = ((), (), s32[]{:S(2)}) async-start(), calls=%async_computation.47 | async-start | bytes 7962624 | tf_op jit(solution)/shard_map/reduce_scatter | solution.py:257
  1482.1 514.1 %reduce-scatter.53.cloned.1.call-start = ((), (), s32[]{:S(2)}) async-start(), calls=%async_computation.50 | async-start | bytes 2654208 | tf_op jit(solution)/shard_map/reduce_scatter | solution.py:259
  1486.5 618.9 %reduce-scatter.55.cloned.1.call-start = ((), (), s32[]{:S(2)}) async-start(), calls=%async_computation.52 | async-start | bytes 6193152
  (184 other events, 5485.9 us)
Sparse Core Ops, SparseCore 0:
  10.8 43.7 all-gather.18
  59.1 36.7 reduce-scatter.24
  98.8 105.3 all-gather.22
  265.0 37.9 reduce-scatter.26
  305.6 65.2 all-gather.26
  393.9 65.1 all-gather.28
  464.1 36.4 reduce-scatter.28
  561.1 37.9 reduce-scatter.30
  638.0 37.9 reduce-scatter.32
  736.5 37.9 reduce-scatter.34
  813.4 37.9 reduce-scatter.36
  854.2 44.1 all-gather.38
  934.1 28.1 reduce-scatter.38
  1046.2 28.1 reduce-scatter.40
  1110.1 28.1 reduce-scatter.42
  1217.6 28.1 reduce-scatter.44
  1282.2 28.1 reduce-scatter.46
  1394.1 28.1 reduce-scatter.50
  1453.6 137.5 all-reduce.2
  1594.6 65.8 reduce-scatter.56
  1664.6 127.9 reduce-scatter.58
  1796.3 128.0 reduce-scatter.48
  1928.1 68.0 reduce-scatter.52
  2000.1 105.2 reduce-scatter.54
  (13 shorter events, 252.4 us)
where the time goes:
time: 2200 us; the launch traced here: 2190 us
  waiting for transfers between devices  1330 us (60%)
  matrix products  302 us (14%)
  blocking collectives  198 us (9%)
  local copies, waits for them, and re-layouts  196 us (9%)
  other arithmetic  140 us (6%)
  between operations  24.2 us (1%)
    unnamed x40, waiting for transfers between devices  263 us
    reduce_scatter x7, waiting for transfers between devices, scatter_rows(): lax.psum_scatter(term(jnp.int32(0), rows * lax.axis_size('mp')), 'mp', sc...  192 us
    reduce_scatter x6, waiting for transfers between devices, scatter_grad(): lax.psum_scatter(term(jnp.int32(0), rows * lax.axis_size('mp')).astype(jn...  169 us
    reduce_scatter x1, waiting for transfers between devices, body(): lax.psum_scatter(stacked[2], 'dp', scatter_dimension=1, tiled=True)  129 us
    all_gather x7, waiting for transfers between devices, gather_grad(): return lax.all_gather(value.astype(jnp.bfloat16), 'mp', axis=0, tiled=True)  117 us
    all_gather x6, waiting for transfers between devices, gather_rows(): return lax.all_gather(value, 'mp', axis=0, tiled=True)  103 us
    unnamed x330, local copies, waits for them, and re-layouts  98.7 us
    psum x2, blocking collectives, body(): lax.psum((first_model * g_head, norm_full, first_model * loss_local), ('d...  80.4 us
  transfers between devices with their start and end apart: 37, of which 35 were waited for; matrix products, arithmetic and copies ran while one was open for 9% of the time, Pallas kernels for 0%

commit v1 on v0

v1 whole, which is shorter than its diff:
```python
import jax
import jax.numpy as jnp
from jax import lax
from jax.sharding import PartitionSpec as P

HEAD_DIM = 64
LAYERS = 3
STEP = 10
MOST = 576

EPSILON = 1e-06
MASKED = -30000.0
CLIP = 0.005
BETA_ONE = 0.9
BETA_TWO = 0.999
ADAM_EPS = 1e-08
RATES = (0.02, 0.06, 0.02, 0.02, 0.02, 0.02, 0.5)
DECAYS = (0.05, 0.05, 0.05, 0.05, 0.05, 0.05, 0.0)
SQRT_HALF = 0.7071067811865476
INV_ROOT = 0.3989422804014327
HIGH = lax.Precision.HIGHEST
BF = jnp.bfloat16
F32 = jnp.float32

AXES = ("dp", "mp")
INNER = ("mp", 1)
OUTER = ("mp", 2)


def swap(value, bit):
    axis, mask = bit
    size = lax.axis_size(axis)
    return lax.ppermute(value, axis, [(i, i ^ mask) for i in range(size)])


def dp_bits():
    size = lax.axis_size("dp")
    bits = []
    mask = 1
    while mask < size:
        bits.append(("dp", mask))
        mask *= 2
    return bits


def dims_of(bits):
    return {bit: i for i, bit in enumerate([OUTER] + bits[::-1])}


def gather(value, order, dims):
    value = value.reshape((1,) * len(dims) + value.shape)
    for bit in order:
        value = jnp.concatenate([value, swap(value, bit)], dims[bit])
    return value


def scatter(value, order, dims):
    for bit in order:
        dim = dims[bit]
        keep = lax.index_in_dim(value, 0, dim)
        send = lax.index_in_dim(value, 1, dim)
        value = keep.astype(F32) + swap(send.astype(BF), bit).astype(F32)
        if bit is not order[-1]:
            value = value.astype(BF)
    return value.reshape(value.shape[len(dims) :])


def both(part):
    return part + swap(part.astype(BF), INNER).astype(F32)


def dot(left, right, contract):
    return lax.dot_general(left, right, ((contract[0:1], contract[1:2]), ((), ())), preferred_element_type=F32)


def nn(left, right):
    return dot(left, right, (1, 0))


def nt(left, right):
    return dot(left, right, (1, 1))


def tn(left, right):
    return dot(left, right, (0, 0))


def norm_stats(value):
    centred = value - jnp.mean(value, -1, keepdims=True)
    variance = jnp.mean(centred * centred, -1, keepdims=True)
    rstd = lax.rsqrt(variance + EPSILON)
    return centred * rstd, rstd


def layer_norm(value, norm):
    return norm_stats(value)[0] * norm[0] + norm[1]


def norm_back(value, norm, d_out):
    hat, rstd = norm_stats(value)
    d_hat = d_out * norm[0]
    d_value = rstd * (
        d_hat - jnp.mean(d_hat, -1, keepdims=True) - hat * jnp.mean(d_hat * hat, -1, keepdims=True)
    )
    return d_value, jnp.stack([jnp.sum(d_out * hat, 0), jnp.sum(d_out, 0)])


def split_heads(value):
    return value.reshape(value.shape[0], -1, HEAD_DIM).transpose(1, 0, 2)


def join_heads(value):
    return value.transpose(1, 0, 2).reshape(value.shape[1], -1)


def softmax_scores(query, key, keep):
    scores = jnp.einsum("htc,hsc->hts", query, key, preferred_element_type=F32) * HEAD_DIM ** (-0.5)
    return jax.nn.softmax(jnp.where(keep[None], scores, MASKED), -1)


def attend(query, key, value, keep):
    probs = softmax_scores(query, key, keep)
    return jnp.einsum("hts,hsc->htc", probs.astype(BF), value, preferred_element_type=F32)


def attend_back(query, key, value, d_out, keep):
    probs = softmax_scores(query, key, keep)
    d_probs = jnp.einsum("htc,hsc->hts", d_out, value, preferred_element_type=F32)
    delta = jnp.sum(probs * d_probs, -1, keepdims=True)
    d_scores = jnp.where(keep[None], probs * (d_probs - delta), 0.0).astype(BF)
    scale = HEAD_DIM ** (-0.5)
    d_query = jnp.einsum("hts,hsc->htc", d_scores, key, preferred_element_type=F32) * scale
    d_key = jnp.einsum("hts,htc->hsc", d_scores, query, preferred_element_type=F32) * scale
    d_value = jnp.einsum("hts,htc->hsc", probs.astype(BF), d_out, preferred_element_type=F32)
    return d_query.astype(BF), d_key.astype(BF), d_value.astype(BF)


def layer_forward(x, attn, ff, norms, keep):
    width = attn.shape[2] // 4
    normed = layer_norm(x, norms[0]).astype(BF)
    mixed = [
        jnp.concatenate([nn(normed, attn[o][:, j * width : (j + 1) * width]) for o in range(2)], 1).astype(BF)
        for j in range(3)
    ]
    heads = [split_heads(m) for m in mixed]
    attended = join_heads(attend(*heads, keep)).astype(BF)
    part = sum(nt(attended[:, o * width : (o + 1) * width], attn[o][:, 3 * width :]) for o in range(2))
    middle = x + both(part)
    hidden = ff.shape[2] // 2
    normed_two = layer_norm(middle, norms[1]).astype(BF)
    up = [nn(normed_two, ff[o][:, :hidden]) for o in range(2)]
    active = [jax.nn.gelu(u, approximate=False).astype(BF) for u in up]
    part = sum(nt(active[o], ff[o][:, hidden:]) for o in range(2))
    return middle + both(part), (x, middle, normed, heads, attended, normed_two, up, active)


def layer_backward(d_x, saved, attn, ff, norms, keep):
    x, middle, normed, heads, attended, normed_two, up, active = saved
    width = attn.shape[2] // 4
    hidden = ff.shape[2] // 2
    d_z = d_x.astype(BF)
    d_up = []
    g_ff = []
    for o in range(2):
        d_active = nn(d_z, ff[o][:, hidden:])
        slope = 0.5 * (1.0 + lax.erf(up[o] * SQRT_HALF)) + up[o] * jnp.exp(-0.5 * up[o] * up[o]) * INV_ROOT
        d_up.append((d_active * slope).astype(BF))
        g_ff.append(jnp.concatenate([tn(normed_two, d_up[o]).astype(BF), tn(d_z, active[o]).astype(BF)], 1))
    part = sum(nt(d_up[o], ff[o][:, :hidden]) for o in range(2))
    d_mid, g_norm_two = norm_back(middle, norms[1], both(part))
    d_mid = d_x + d_mid
    d_y = d_mid.astype(BF)
    d_att = jnp.concatenate([nn(d_y, attn[o][:, 3 * width :]) for o in range(2)], 1).astype(BF)
    d_heads = attend_back(*heads, split_heads(d_att), keep)
    d_mixed = [join_heads(h) for h in d_heads]
    g_attn = []
    part = 0.0
    for o in range(2):
        cols = slice(o * width, (o + 1) * width)
        g_attn.append(
            jnp.concatenate(
                [tn(normed, d_mixed[j][:, cols]).astype(BF) for j in range(3)] + [tn(d_y, attended[:, cols]).astype(BF)], 1
            )
        )
        for j in range(3):
            part = part + nt(d_mixed[j][:, cols], attn[o][:, j * width : (j + 1) * width])
    d_low, g_norm_one = norm_back(x, norms[0], both(part))
    return d_mid + d_low, jnp.stack(g_attn), jnp.stack(g_ff), jnp.stack([g_norm_one, g_norm_two])


def adam(weight, grad, first, second, rate, decay):
    first = BETA_ONE * first + (1.0 - BETA_ONE) * grad
    second = BETA_TWO * second + (1.0 - BETA_TWO) * grad * grad
    update = first / (1.0 - BETA_ONE**STEP) / (jnp.sqrt(second / (1.0 - BETA_TWO**STEP)) + ADAM_EPS)
    return (first, second, weight - rate * (update + decay * weight))


def body(pixels, lengths, valid_mask, teacher_logits, teacher_map, *state):
    masters, firsts, seconds = state[:7], state[7:14], state[14:]
    attend_in, attend_out, hidden_up, hidden_down, patch_embed, class_head, norm_params = masters
    bits = dp_bits()
    dims = dims_of(bits)
    low, high = bits[0], bits[1:]
    outer_last = high + [low, OUTER]
    low_last = high + [OUTER, low]
    rows = patch_embed.shape[1]
    inner = lax.axis_index("mp") % 2
    outer = lax.axis_index("mp") // 2
    images = lengths.shape[1]
    tokens = pixels.shape[0]
    total_images = images * lax.axis_size("dp")

    def cols(value):
        return value.astype(BF)

    patch_unit = cols(patch_embed.T)
    attn_units = [
        jnp.concatenate([cols(attend_in[l, j]) for j in range(3)] + [cols(attend_out[l].T)], 1) for l in range(LAYERS)
    ]
    ff_units = [jnp.concatenate([cols(hidden_up[l]), cols(hidden_down[l].T)], 1) for l in range(LAYERS)]
    half = class_head.shape[1] // 2
    head_unit = lax.dynamic_slice_in_dim(cols(class_head), inner * half, half, 1)

    def whole(unit, order):
        got = gather(unit, order, dims)
        return got.reshape(got.shape[0], -1, got.shape[-1])

    row = lengths[0]
    ends = jnp.cumsum(row)
    longest = jnp.argmax(row)
    start = ends[longest] - row[longest]
    place = jnp.arange(MOST, dtype=jnp.int32)

    def mine(value, which):
        twice = jnp.concatenate([value, value], 0)
        return lax.dynamic_slice_in_dim(twice, start + MOST * which, MOST, 0)

    pix = [mine(pixels, outer)]
    pix.append(swap(mine(pixels, 1 - outer), OUTER))
    held = jnp.where(outer == 0, MOST, tokens - MOST)
    position = (start + MOST * outer + place) % tokens
    segment = jnp.sum((position[:, None] >= ends[None, :]).astype(jnp.int32), 1)
    valid = jnp.where(place < held, mine(valid_mask, outer), 0) > 0
    keep = (segment[:, None] == segment[None, :]) & valid[None, :]
    image_ids = jnp.arange(images, dtype=jnp.int32)
    member = ((segment[None, :] == image_ids[:, None]) & valid[None, :]).astype(F32)
    owned = ((image_ids == longest) == (outer == 0)).astype(F32)[:, None]
    count = jnp.sum(member, 1)

    norms = gather(norm_params.astype(BF).reshape(-1, rows), high + [low], dims)
    norms = jnp.moveaxis(norms.reshape(-1, 7, 2, rows), 0, 2).reshape(7, 2, -1).astype(F32)

    patch = whole(patch_unit, outer_last)
    attn, ff = [], []
    for l in range(LAYERS):
        attn.append(whole(attn_units[l], low_last))
        ff.append(whole(ff_units[l], outer_last if l == 1 else low_last))
    head = whole(head_unit, high + [low])[0]

    teach_log = jax.nn.log_softmax(teacher_logits, -1)
    teach_log = gather(lax.dynamic_slice_in_dim(teach_log, inner * half, half, 1), high + [low], dims)
    teach_log = teach_log.reshape(-1, images, half)
    me = lax.axis_index("dp")
    source = jnp.sum(jnp.where(teacher_map == me, jnp.arange(teacher_map.shape[0], dtype=jnp.int32), 0))
    teach_log = lax.dynamic_index_in_dim(teach_log, jnp.bitwise_xor(source, me), 0, False)

    x = both(sum(nt(pix[o], patch[o]) for o in range(2)))
    saved = []
    for l in range(LAYERS):
        x, kept = layer_forward(x, attn[l], ff[l], norms[2 * l : 2 * l + 2], keep)
        saved.append(kept)

    divisor = jnp.maximum(count, 1.0)[:, None]
    pooled = jnp.dot(member, x, precision=HIGH) / divisor
    pooled_normed = layer_norm(pooled, norms[-1]).astype(BF)
    logits = nn(pooled_normed, head)
    theirs = swap(logits, INNER)
    peak = jnp.maximum(jnp.max(logits, -1, keepdims=True), jnp.max(theirs, -1, keepdims=True))
    total = jnp.sum(jnp.exp(logits - peak), -1, keepdims=True) + jnp.sum(jnp.exp(theirs - peak), -1, keepdims=True)
    student_log = logits - peak - jnp.log(total)
    loss_local = jnp.sum(owned * jnp.exp(teach_log) * (teach_log - student_log))
    d_logits = (owned * (jnp.exp(student_log) - jnp.exp(teach_log)) / total_images).astype(BF)
    g_head = tn(pooled_normed, d_logits).astype(BF)
    d_pooled, g_final = norm_back(pooled, norms[-1], both(nt(d_logits, head)))
    d_x = lax.dot_general(member, d_pooled / divisor, (((0,), (0,)), ((), ())), precision=HIGH)

    shape = (2,) * (1 + len(bits))

    def split(grad, order):
        return scatter(grad.reshape(shape + (rows, grad.shape[-1])), order[::-1], dims)

    g_attn, g_ff, g_norms = [None] * LAYERS, [None] * LAYERS, [None] * LAYERS
    g_head = scatter(g_head.reshape((1,) + shape[1:] + (rows, half)), (high + [low])[::-1], dims)
    for l in reversed(range(LAYERS)):
        d_x, g_a, g_f, g_norms[l] = layer_backward(d_x, saved[l], attn[l], ff[l], norms[2 * l : 2 * l + 2], keep)
        g_attn[l] = split(g_a, low_last)
        g_ff[l] = split(g_f, outer_last if l == 1 else low_last)
    d_x0 = d_x.astype(BF)
    g_patch = split(jnp.stack([tn(d_x0, p).astype(BF) for p in pix]), outer_last)

    g_head = g_head + swap(g_head, OUTER)
    other_half = swap(g_head, INNER)
    g_head = jnp.where(inner == 0, jnp.concatenate([g_head, other_half], 1), jnp.concatenate([other_half, g_head], 1))
    g_norm = jnp.concatenate(g_norms + [g_final[None]], 0).reshape(14, -1, rows)
    g_norm = jnp.moveaxis(g_norm, 1, 0).reshape((1,) + shape[1:] + (14, rows))
    for bit in (high + [low])[::-1]:
        g_norm = lax.index_in_dim(g_norm, 0, dims[bit]) + swap(lax.index_in_dim(g_norm, 1, dims[bit]), bit)
    g_norm = g_norm.reshape(14, rows)
    g_norm = g_norm + swap(g_norm, OUTER)
    other_norm = swap(g_norm, INNER)
    g_norm = (0.5 * (g_norm + other_norm)).reshape(7, 2, rows)

    width = attend_out.shape[1]
    hidden = hidden_up.shape[2]
    grads = (
        jnp.stack([jnp.stack([g[:, j * width : (j + 1) * width] for j in range(3)]) for g in g_attn]),
        jnp.stack([g[:, 3 * width :].T for g in g_attn]),
        jnp.stack([g[:, :hidden] for g in g_ff]),
        jnp.stack([g[:, hidden:].T for g in g_ff]),
        g_patch.T,
        g_head,
        g_norm,
    )
    first_model = (lax.axis_index("mp") == 0).astype(F32)
    squares = sum(jnp.sum(g * g) for g in g_attn + g_ff + [g_patch]) + first_model * (
        jnp.sum(g_head * g_head) + jnp.sum(g_norm * g_norm)
    )
    sums = jnp.stack([squares, loss_local * (outer >= 0)])
    for bit in [INNER, OUTER] + bits:
        sums = sums + swap(sums, bit)
    loss = sums[1]
    grad_norm = jnp.sqrt(sums[0])
    clip = jnp.minimum(1.0, CLIP / grad_norm)
    results = []
    for kind in range(7):
        results.append(
            adam(masters[kind], grads[kind] * clip, firsts[kind], seconds[kind], RATES[kind], DECAYS[kind])
        )
    return (loss, grad_norm) + tuple(r[i] for i in range(3) for r in results)


def solution(mesh):
    weights = (
        P(None, None, "dp", "mp"),
        P(None, "mp", "dp"),
        P(None, "dp", "mp"),
        P(None, "mp", "dp"),
        P("mp", "dp"),
        P("dp", None),
        P(None, None, "dp"),
    )
    placed = (P("dp", "mp"), P("dp", None), P("dp"), P("dp", None), P()) + weights * 3
    return jax.shard_map(
        body, mesh=mesh, in_specs=placed, out_specs=(P(), P()) + weights * 3, check_vma=False
    )
```

time: 2200 us -> 1030 us (0.47)
  waiting for transfers between devices: 1330 us -> 292 us
  blocking collectives: 198 us -> 0 us
  local copies, waits for them, and re-layouts: 196 us -> 97 us
  starting transfers between devices: 3.5 us -> 88.2 us
  matrix products: 302 us -> 346 us
  other arithmetic: 140 us -> 177 us
    reduce_scatter x15 -> x0, waiting for transfers between devices: 557 us -> none  [the longest x7 192 us: scatter_rows(): lax.psum_scatter(term(jnp.int32(0), rows * lax.axis_size('mp')), 'mp', sc...]
    all_gather x18 -> x0, waiting for transfers between devices: 437 us -> none  [the longest x7 117 us: gather_grad(): return lax.all_gather(value.astype(jnp.bfloat16), 'mp', axis=0, tiled=True)]
    ppermute x0 -> x96, waiting for transfers between devices: none -> 292 us  [swap(): return lax.ppermute(value, axis, [(i, i ^ mask) for i in range(size)])]
    unnamed x40 -> x0, waiting for transfers between devices: 263 us -> none
    all_gather x3 -> x0, blocking collectives: 107 us -> none  [the longest x1 45 us: body(): lax.all_gather(attend_out.astype(jnp.bfloat16), 'dp', axis=2, tiled=True)]
    psum x3 -> x0, blocking collectives: 90.7 us -> none  [the longest x2 80.4 us: body(): lax.psum((first_model * g_head, norm_full, first_model * loss_local), ('d...]
    ppermute x0 -> x96, starting transfers between devices: none -> 88.2 us  [swap(): return lax.ppermute(value, axis, [(i, i ^ mask) for i in range(size)])]
    unnamed x330 -> x549, local copies, waits for them, and re-layouts: 98.7 us -> 23.4 us
  transfers between devices with their start and end apart: 37 -> 96, of which waited for: 35 -> 37; matrix products, arithmetic and copies ran while one was open for 9% -> 57% of each run, Pallas kernels for 0% -> 0%
where the time goes in v1:
time: 1030 us; the launch traced here: 1020 us
  matrix products  346 us (34%)
  waiting for transfers between devices  292 us (28%)
  other arithmetic  177 us (17%)
  local copies, waits for them, and re-layouts  97 us (9%)
  starting transfers between devices  88.2 us (9%)
  between operations  17.3 us (2%)
    ppermute x96, waiting for transfers between devices, swap(): return lax.ppermute(value, axis, [(i, i ^ mask) for i in range(size)])  292 us
    dot_general x115, matrix products, dot(): lax.dot_general(left, right, ((contract[0:1], contract[1:2]), ((), ())),...  187 us
    ppermute x96, starting transfers between devices, swap(): return lax.ppermute(value, axis, [(i, i ^ mask) for i in range(size)])  88.2 us
    dot_general x3, matrix products, attend_back(): jnp.einsum('hts,htc->hsc', d_scores, query, preferred_element_type=F32)  46 us
    dot_general x3, matrix products, attend_back(): jnp.einsum('hts,hsc->htc', d_scores, key, preferred_element_type=F32)  43.9 us
    concatenate x34, other arithmetic, gather(): value = jnp.concatenate([value, swap(value, bit)], dims[bit])  38.8 us
    convert_element_type x23, other arithmetic, scatter(): value = value.astype(BF)  26.5 us
    sub x3, matrix products, softmax_scores(): return jax.nn.softmax(jnp.where(keep[None], scores, MASKED), -1)  24.4 us
  transfers between devices with their start and end apart: 96, of which 37 were waited for; matrix products, arithmetic and copies ran while one was open for 57% of the time, Pallas kernels for 0%

profile of v1, /device:TPU:0, one launch (start us, length us, event | category | flops | bytes accessed | tf_op | source)
XLA Modules:
  0.0 1017.8 jit_solution(3331771704152836859)
XLA Ops:
  33.1 10.5 %collective-permute-done.7 = bf16[1,1,2,1,14,96]{5,3,2,1,4,0:T(2,128)(2,1)S(1)} collective-permute-done((bf16[1,1,2,1,14,96]{5,3,2,1,4,0:T(2,128)(2,1)S(1)}, bf16[1,1,2,1,14,96]{5,3,2,1,4,0:T(2,128)(2,1)S(1)}, u32[]{:S(2)}, u32[]{:S(2)}) %collective-permute-start.7) | collective-permute-done | bytes 5408 | tf_op jit(solution)/shard_map/ppermute | solution.py:33
  63.1 13.7 %collective-permute-done.10 = bf16[1,1,2,1,96,768]{5,4,3,2,1,0:T(8,128)(2,1)S(1)} collective-permute-done((bf16[1,1,2,1,96,768]{5,4,3,2,1,0:T(8,128)(2,1)S(1)}, bf16[1,1,2,1,96,768]{5,4,3,2,1,0:T(8,128)(2,1)S(1)}, u32[]{:S(2)}, u32[]{:S(2)}) %collective-permute-start.10) | collective-permute-done | bytes 294944 | tf_op jit(solution)/shard_map/ppermute | solution.py:33
  79.0 10.3 %collective-permute-done.15 = bf16[1,1,2,1,96,1536]{5,4,3,2,1,0:T(8,128)(2,1)S(1)} collective-permute-done((bf16[1,1,2,1,96,1536]{5,4,3,2,1,0:T(8,128)(2,1)}, bf16[1,1,2,1,96,1536]{5,4,3,2,1,0:T(8,128)(2,1)S(1)}, u32[]{:S(2)}, u32[]{:S(2)}) %collective-permute-start.15) | collective-permute-done | bytes 589856 | tf_op jit(solution)/shard_map/ppermute | solution.py:33
  90.9 18.1 %collective-permute-done.11 = bf16[1,2,2,1,96,768]{5,4,3,2,1,0:T(8,128)(2,1)} collective-permute-done((bf16[1,2,2,1,96,768]{5,4,3,2,1,0:T(8,128)(2,1)}, bf16[1,2,2,1,96,768]{5,4,3,2,1,0:T(8,128)(2,1)}, u32[]{:S(2)}, u32[]{:S(2)}) %collective-permute-start.11) | collective-permute-done | bytes 589856 | tf_op jit(solution)/shard_map/ppermute | solution.py:33
  120.9 11.7 %collective-permute-done.16 = bf16[1,2,2,1,96,1536]{5,4,3,2,1,0:T(8,128)(2,1)S(1)} collective-permute-done((bf16[1,2,2,1,96,1536]{5,4,3,2,1,0:T(8,128)(2,1)S(1)}, bf16[1,2,2,1,96,1536]{5,4,3,2,1,0:T(8,128)(2,1)S(1)}, u32[]{:S(2)}, u32[]{:S(2)}) %collective-permute-start.16) | collective-permute-done | bytes 1179680 | tf_op jit(solution)/shard_map/ppermute | solution.py:33
  148.1 8.6 fusion.503
  209.8 7.4 collective-permute-done.26
  220.0 20.6 %collective-permute-done.22 = bf16[2,2,2,1,96,768]{5,4,3,2,1,0:T(8,128)(2,1)S(1)} collective-permute-done((bf16[2,2,2,1,96,768]{5,4,3,2,1,0:T(8,128)(2,1)S(1)}, bf16[2,2,2,1,96,768]{5,4,3,2,1,0:T(8,128)(2,1)S(1)}, u32[]{:S(2)}, u32[]{:S(2)}) %collective-permute-start.22) | collective-permute-done | bytes 1179680 | tf_op jit(solution)/shard_map/ppermute | solution.py:33
  251.9 7.9 fusion.506
  276.0 28.8 %collective-permute-done.31 = bf16[1,2,2,1,96,768]{5,4,3,2,1,0:T(8,128)(2,1)} collective-permute-done((bf16[1,2,2,1,96,768]{5,4,3,2,1,0:T(8,128)(2,1)S(1)}, bf16[1,2,2,1,96,768]{5,4,3,2,1,0:T(8,128)(2,1)}, u32[]{:S(2)}, u32[]{:S(2)}) %collective-permute-start.31) | collective-permute-done | bytes 589856 | tf_op jit(solution)/shard_map/ppermute | solution.py:33
  344.3 7.9 fusion.509
  360.2 27.9 %collective-permute-done.37 = bf16[2,2,2,1,96,1536]{5,4,3,2,1,0:T(8,128)(2,1)} collective-permute-done((bf16[2,2,2,1,96,1536]{5,4,3,2,1,0:T(8,128)(2,1)}, bf16[2,2,2,1,96,1536]{5,4,3,2,1,0:T(8,128)(2,1)}, u32[]{:S(2)}, u32[]{:S(2)}) %collective-permute-start.37) | collective-permute-done | bytes 2359328 | tf_op jit(solution)/shard_map/ppermute | solution.py:33
  460.0 8.6 collective-permute-done.82
  511.9 14.3 %fusion.181 = bf16[6,576,64]{1,2,0:T(8,128)(2,1)S(1)} fusion(f32[6,576,576]{1,2,0:T(8,128)} %fusion.336, pred[576,576]{0,1:T(8,128)(4,1)} %compare_and_fusion, bf16[576,3,64]{0,2,1:T(8,128)(2,1)} %bitcast.698, bf16[576,3,64]{0,2,1:T(8,128)(2,1)} %bitcast.704, f32[6,576,576]{1,2,0:T(8,128)} %get-tuple-element.258, f32[6,576]{1,0:T(8,128)S(1)} %copy-done.264), kind=kOutput, calls=%fused_computation.346 | convolution fusion | flops 270069696 | bytes 17155584 | tf_op jit(solution)/shard_map/hts,hsc->htc/dot_general | solution.py:132
  526.1 15.6 %fusion.178 = bf16[6,576,64]{1,2,0:T(8,128)(2,1)} fusion(f32[6,576,576]{1,2,0:T(8,128)} %fusion.336, pred[576,576]{0,1:T(8,128)(4,1)} %compare_and_fusion, bf16[576,3,64]{0,2,1:T(8,128)(2,1)} %bitcast.700, bf16[576,3,64]{0,2,1:T(8,128)(2,1)} %bitcast.702, f32[6,576,576]{1,2,0:T(8,128)} %get-tuple-element.258, f32[6,576]{1,0:T(8,128)S(1)} %copy-done.264), kind=kOutput, calls=%fused_computation.345 | convolution fusion | flops 269406144 | bytes 17155584 | tf_op jit(solution)/shard_map/hts,htc->hsc/dot_general | solution.py:133
  634.0 14.9 %fusion.187 = bf16[6,576,64]{1,2,0:T(8,128)(2,1)} fusion(f32[6,576,576]{1,2,0:T(8,128)} %fusion.335, pred[576,576]{0,1:T(8,128)(4,1)} %compare_and_fusion, bf16[576,3,64]{0,2,1:T(8,128)(2,1)} %bitcast.690, bf16[576,3,64]{0,2,1:T(8,128)(2,1)} %bitcast.696, f32[6,576,576]{1,2,0:T(8,128)} %get-tuple-element.248, f32[6,576]{1,0:T(8,128)S(1)} %copy-done.262), kind=kOutput, calls=%fused_computation.348 | convolution fusion | flops 270069696 | bytes 17155584 | tf_op jit(solution)/shard_map/hts,hsc->htc/dot_general | solution.py:132
  648.9 14.9 %fusion.184 = bf16[6,576,64]{1,2,0:T(8,128)(2,1)S(1)} fusion(f32[6,576,576]{1,2,0:T(8,128)} %fusion.335, pred[576,576]{0,1:T(8,128)(4,1)S(1)} %copy-done.171, bf16[576,3,64]{0,2,1:T(8,128)(2,1)} %bitcast.692, bf16[576,3,64]{0,2,1:T(8,128)(2,1)} %bitcast.694, f32[6,576,576]{1,2,0:T(8,128)} %get-tuple-element.248, f32[6,576]{1,0:T(8,128)S(1)} %copy-done.262), kind=kOutput, calls=%fused_computation.347 | convolution fusion | flops 269406144 | bytes 17155584 | tf_op jit(solution)/shard_map/hts,htc->hsc/dot_general | solution.py:133
  766.1 14.8 %fusion.193 = bf16[6,576,64]{1,2,0:T(8,128)(2,1)} fusion(f32[6,576,576]{1,2,0:T(8,128)} %fusion.334, pred[576,576]{0,1:T(8,128)(4,1)} %compare_and_fusion, bf16[576,3,64]{0,2,1:T(8,128)(2,1)} %bitcast.682, bf16[576,3,64]{0,2,1:T(8,128)(2,1)} %bitcast.688, f32[6,576,576]{1,2,0:T(8,128)} %get-tuple-element.238, f32[6,576]{1,0:T(8,128)} %get-tuple-element.237), kind=kOutput, calls=%fused_computation.350 | convolution fusion | flops 270069696 | bytes 17155584 | tf_op jit(solution)/shard_map/hts,hsc->htc/dot_general | solution.py:132
  780.9 15.5 %fusion.190 = bf16[6,576,64]{1,2,0:T(8,128)(2,1)} fusion(f32[6,576,576]{1,2,0:T(8,128)} %fusion.334, pred[576,576]{0,1:T(8,128)(4,1)} %compare_and_fusion, bf16[576,3,64]{0,2,1:T(8,128)(2,1)} %bitcast.684, bf16[576,3,64]{0,2,1:T(8,128)(2,1)} %bitcast.686, f32[6,576,576]{1,2,0:T(8,128)} %get-tuple-element.238, f32[6,576]{1,0:T(8,128)} %get-tuple-element.237), kind=kOutput, calls=%fused_computation.349 | convolution fusion | flops 269406144 | bytes 17155584 | tf_op jit(solution)/shard_map/hts,htc->hsc/dot_general | solution.py:133
  872.5 14.6 %collective-permute-done.70 = bf16[1,1,2,1,96,1536]{5,4,3,2,1,0:T(8,128)(2,1)} collective-permute-done((bf16[1,1,2,1,96,1536]{5,4,3,2,1,0:T(8,128)(2,1)}, bf16[1,1,2,1,96,1536]{5,4,3,2,1,0:T(8,128)(2,1)}, u32[]{:S(2)}, u32[]{:S(2)}) %collective-permute-start.70) | collective-permute-done | bytes 589856 | tf_op jit(solution)/shard_map/ppermute | solution.py:33
  891.7 16.6 %collective-permute-done.53 = bf16[1,2,2,1,96,768]{5,4,3,2,1,0:T(8,128)(2,1)S(1)} collective-permute-done((bf16[1,2,2,1,96,768]{5,4,3,2,1,0:T(8,128)(2,1)S(1)}, bf16[1,2,2,1,96,768]{5,4,3,2,1,0:T(8,128)(2,1)S(1)}, u32[]{:S(2)}, u32[]{:S(2)}) %collective-permute-start.53) | collective-permute-done | bytes 589856 | tf_op jit(solution)/shard_map/ppermute | solution.py:33
  914.0 9.5 collective-permute-done.54
  935.1 19.8 %collective-permute-done.79 = bf16[1,1,2,1,96,768]{5,4,3,2,1,0:T(8,128)(2,1)S(1)} collective-permute-done((bf16[1,1,2,1,96,768]{5,4,3,2,1,0:T(8,128)(2,1)S(1)}, bf16[1,1,2,1,96,768]{5,4,3,2,1,0:T(8,128)(2,1)S(1)}, u32[]{:S(2)}, u32[]{:S(2)}) %collective-permute-start.79) | collective-permute-done | bytes 294944 | tf_op jit(solution)/shard_map/ppermute | solution.py:33
  955.0 10.5 %collective-permute-done.66 = bf16[1,1,2,1,96,1536]{5,4,3,2,1,0:T(8,128)(2,1)S(1)} collective-permute-done((bf16[1,1,2,1,96,1536]{5,4,3,2,1,0:T(8,128)(2,1)S(1)}, bf16[1,1,2,1,96,1536]{5,4,3,2,1,0:T(8,128)(2,1)S(1)}, u32[]{:S(2)}, u32[]{:S(2)}) %collective-permute-start.66) | collective-permute-done | bytes 589856 | tf_op jit(solution)/shard_map/ppermute | solution.py:33
  (1145 shorter events, 657.6 us)
Async XLA Ops:
  9.9 79.6 %collective-permute-start.19 = (bf16[1,1,1,1,96,768]{5,4,3,2,1,0:T(8,128)(2,1)S(1)}, bf16[1,1,1,1,96,768]{5,4,3,2,1,0:T(8,128)(2,1)S(1)}, u32[]{:S(2)}, u32[]{:S(2)}) collective-permute-start(bf16[1,1,1,1,96,768]{5,4,3,2,1,0:T(8,128)(2,1)S(1)} %maximum_bitcast_fusion.31), channel_id=1, source_target_pairs={{0,8},{4,12},{8,0},{12,4},{16,24},{20,28},{24,16},{28,20},{1,9},{5... | collective-permute-start | bytes 442376 | tf_op jit(solution)/shard_map/ppermute | solution.py:33
  48.2 64.5 %collective-permute-start.3 = (bf16[576,768]{1,0:T(8,128)(2,1)}, bf16[576,768]{1,0:T(8,128)(2,1)}, u32[]{:S(2)}, u32[]{:S(2)}) collective-permute-start(bf16[576,768]{1,0:T(8,128)(2,1)} %constant_dynamic-slice_fusion), channel_id=1, source_target_pairs={{0,2},{1,3},{2,0},{3,1},{4,6},{5,7},{6,4},{7,5},{8,10},{9,11},{10,... | collective-permute-start | bytes 2654216 | tf_op jit(solution)/shard_map/ppermute | solution.py:33
  61.6 53.1 %collective-permute-start.4 = (bf16[1,2,2,2,96,768]{5,4,3,2,1,0:T(8,128)(2,1)}, bf16[1,2,2,2,96,768]{5,4,3,2,1,0:T(8,128)(2,1)}, u32[]{:S(2)}, u32[]{:S(2)}) collective-permute-start(bf16[1,2,2,2,96,768]{5,4,3,2,1,0:T(8,128)(2,1)} %pad_maximum_fusion.18), channel_id=1, source_target_pairs={{0,2},{1,3},{2,0},{3,1},{4,6},{5,7},{6,4},{7,5},{8,10},{9,11},{10,... | collective-permute-start | bytes 3538952 | tf_op jit(solution)/shard_map/ppermute | solution.py:33
  109.0 55.9 %collective-permute-start.29 = (bf16[1,1,1,1,96,768]{5,4,3,2,1,0:T(8,128)(2,1)}, bf16[1,1,1,1,96,768]{5,4,3,2,1,0:T(8,128)(2,1)}, u32[]{:S(2)}, u32[]{:S(2)}) collective-permute-start(bf16[1,1,1,1,96,768]{5,4,3,2,1,0:T(8,128)(2,1)} %maximum_bitcast_fusion.32), channel_id=1, source_target_pairs={{0,8},{4,12},{8,0},{12,4},{16,24},{20,28},{24,16},{28,20},{1,9},{5... | collective-permute-start | bytes 442376 | tf_op jit(solution)/shard_map/ppermute | solution.py:33
  112.7 55.5 %collective-permute-start.34 = (bf16[1,1,1,1,96,1536]{5,4,3,2,1,0:T(8,128)(2,1)S(1)}, bf16[1,1,1,1,96,1536]{5,4,3,2,1,0:T(8,128)(2,1)}, u32[]{:S(2)}, u32[]{:S(2)}) collective-permute-start(bf16[1,1,1,1,96,1536]{5,4,3,2,1,0:T(8,128)(2,1)S(1)} %maximum_bitcast_fusion.26), channel_id=1, source_target_pairs={{0,8},{4,12},{8,0},{12,4},{16,24},{20,28},{24,16},{28,20},{1,9},{5... | collective-permute-start | bytes 884744 | tf_op jit(solution)/shard_map/ppermute | solution.py:33
  114.7 49.0 %collective-permute-start.20 = (bf16[1,1,2,1,96,768]{5,4,3,2,1,0:T(8,128)(2,1)}, bf16[1,1,2,1,96,768]{5,4,3,2,1,0:T(8,128)(2,1)}, u32[]{:S(2)}, u32[]{:S(2)}) collective-permute-start(bf16[1,1,2,1,96,768]{5,4,3,2,1,0:T(8,128)(2,1)} %pad_maximum_fusion.42), channel_id=1, source_target_pairs={{0,16},{4,20},{8,24},{12,28},{16,0},{20,4},{24,8},{28,12},{1,17},{... | collective-permute-start | bytes 884744 | tf_op jit(solution)/shard_map/ppermute | solution.py:33
  137.5 54.6 %collective-permute-start.17 = (bf16[2,2,2,1,96,1536]{5,4,3,2,1,0:T(8,128)(2,1)}, bf16[2,2,2,1,96,1536]{5,4,3,2,1,0:T(8,128)(2,1)}, u32[]{:S(2)}, u32[]{:S(2)}) collective-permute-start(bf16[2,2,2,1,96,1536]{5,4,3,2,1,0:T(8,128)(2,1)} %pad_maximum_fusion.5), channel_id=1, source_target_pairs={{0,4},{4,0},{8,12},{12,8},{16,20},{20,16},{24,28},{28,24},{1,5},{5... | collective-permute-start | bytes 7077896 | tf_op jit(solution)/shard_map/ppermute | solution.py:33
  168.2 102.3 %collective-permute-start.39 = (bf16[1,1,1,1,96,500]{5,4,3,2,1,0:T(8,128)(2,1)}, bf16[1,1,1,1,96,500]{5,4,3,2,1,0:T(8,128)(2,1)}, u32[]{:S(2)}, u32[]{:S(2)}) collective-permute-start(bf16[1,1,1,1,96,500]{5,4,3,2,1,0:T(8,128)(2,1)} %fusion.392), channel_id=1, source_target_pairs={{0,8},{4,12},{8,0},{12,4},{16,24},{20,28},{24,16},{28,20},{1,9},{5... | collective-permute-start | bytes 288008 | tf_op jit(solution)/shard_map/ppermute | solution.py:33
  171.0 97.0 %collective-permute-start.30 = (bf16[1,1,2,1,96,768]{5,4,3,2,1,0:T(8,128)(2,1)}, bf16[1,1,2,1,96,768]{5,4,3,2,1,0:T(8,128)(2,1)}, u32[]{:S(2)}, u32[]{:S(2)}) collective-permute-start(bf16[1,1,2,1,96,768]{5,4,3,2,1,0:T(8,128)(2,1)} %pad_maximum_fusion.43), channel_id=1, source_target_pairs={{0,16},{4,20},{8,24},{12,28},{16,0},{20,4},{24,8},{28,12},{1,17},{... | collective-permute-start | bytes 884744 | tf_op jit(solution)/shard_map/ppermute | solution.py:33
  180.6 93.3 %collective-permute-start.35 = (bf16[1,1,2,1,96,1536]{5,4,3,2,1,0:T(8,128)(2,1)}, bf16[1,1,2,1,96,1536]{5,4,3,2,1,0:T(8,128)(2,1)}, u32[]{:S(2)}, u32[]{:S(2)}) collective-permute-start(bf16[1,1,2,1,96,1536]{5,4,3,2,1,0:T(8,128)(2,1)} %pad_maximum_fusion.38), channel_id=1, source_target_pairs={{0,16},{4,20},{8,24},{12,28},{16,0},{20,4},{24,8},{28,12},{1,17},{... | collective-permute-start | bytes 1769480 | tf_op jit(solution)/shard_map/ppermute | solution.py:33
  240.5 71.4 %collective-permute-start.27 = (bf16[1,2,2,2,96,1536]{5,4,3,2,1,0:T(8,128)(2,1)}, bf16[1,2,2,2,96,1536]{5,4,3,2,1,0:T(8,128)(2,1)}, u32[]{:S(2)}, u32[]{:S(2)}) collective-permute-start(bf16[1,2,2,2,96,1536]{5,4,3,2,1,0:T(8,128)(2,1)} %pad_maximum_fusion.7), channel_id=1, source_target_pairs={{0,2},{1,3},{2,0},{3,1},{4,6},{5,7},{6,4},{7,5},{8,10},{9,11},{10,... | collective-permute-start | bytes 7077896 | tf_op jit(solution)/shard_map/ppermute | solution.py:33
  270.4 139.7 %collective-permute-start.43 = (f32[1,1,1,1,8,500]{5,4,3,2,1,0:T(8,128)S(1)}, f32[1,1,1,1,8,500]{5,4,3,2,1,0:T(8,128)S(1)}, u32[]{:S(2)}, u32[]{:S(2)}) collective-permute-start(f32[1,1,1,1,8,500]{5,4,3,2,1,0:T(8,128)S(1)} %fusion.403), channel_id=1, source_target_pairs={{0,8},{4,12},{8,0},{12,4},{16,24},{20,28},{24,16},{28,20},{1,9},{5... | collective-permute-start | bytes 48008 | tf_op jit(solution)/shard_map/ppermute | solution.py:33
  273.9 133.9 %collective-permute-start.40 = (bf16[1,1,2,1,96,500]{5,4,3,2,1,0:T(8,128)(2,1)}, bf16[1,1,2,1,96,500]{5,4,3,2,1,0:T(8,128)(2,1)}, u32[]{:S(2)}, u32[]{:S(2)}) collective-permute-start(bf16[1,1,2,1,96,500]{5,4,3,2,1,0:T(8,128)(2,1)} %pad_maximum_fusion.44), channel_id=1, source_target_pairs={{0,16},{4,20},{8,24},{12,28},{16,0},{20,4},{24,8},{28,12},{1,17},{... | collective-permute-start | bytes 576008 | tf_op jit(solution)/shard_map/ppermute | solution.py:33
  334.1 53.9 %collective-permute-start.37 = (bf16[2,2,2,1,96,1536]{5,4,3,2,1,0:T(8,128)(2,1)}, bf16[2,2,2,1,96,1536]{5,4,3,2,1,0:T(8,128)(2,1)}, u32[]{:S(2)}, u32[]{:S(2)}) collective-permute-start(bf16[2,2,2,1,96,1536]{5,4,3,2,1,0:T(8,128)(2,1)} %pad_maximum_fusion.9), channel_id=1, source_target_pairs={{0,4},{4,0},{8,12},{12,8},{16,20},{20,16},{24,28},{28,24},{1,5},{5... | collective-permute-start | bytes 7077896 | tf_op jit(solution)/shard_map/ppermute | solution.py:33
  486.3 119.6 %collective-permute-start.72 = (bf16[2,2,2,1,96,1536]{5,4,3,2,1,0:T(8,128)(2,1)}, bf16[2,2,2,1,96,1536]{5,4,3,2,1,0:T(8,128)(2,1)}, u32[]{:S(2)}, u32[]{:S(2)}) collective-permute-start(bf16[2,2,2,1,96,1536]{5,4,3,2,1,0:T(8,128)(2,1)} %pad_maximum_fusion.2), channel_id=1, source_target_pairs={{0,4},{4,0},{8,12},{12,8},{16,20},{20,16},{24,28},{28,24},{1,5},{5... | collective-permute-start | bytes 7077896 | tf_op jit(solution)/shard_map/ppermute | solution.py:33
  490.7 71.7 %collective-permute-start.85 = (f32[96,500]{1,0:T(8,128)}, f32[96,500]{1,0:T(8,128)}, u32[]{:S(2)}, u32[]{:S(2)}) collective-permute-start(f32[96,500]{1,0:T(8,128)} %fusion.469), channel_id=1, source_target_pairs={{0,1},{1,0},{2,3},{3,2},{4,5},{5,4},{6,7},{7,6},{8,9},{9,8},{10,11... | collective-permute-start | bytes 576008 | tf_op jit(solution)/shard_map/ppermute | solution.py:33
  601.2 142.9 %collective-permute-start.68 = (bf16[1,2,2,2,96,1536]{5,4,3,2,1,0:T(8,128)(2,1)}, bf16[1,2,2,2,96,1536]{5,4,3,2,1,0:T(8,128)(2,1)}, u32[]{:S(2)}, u32[]{:S(2)}) collective-permute-start(bf16[1,2,2,2,96,1536]{5,4,3,2,1,0:T(8,128)(2,1)} %bitcast.599), channel_id=1, source_target_pairs={{0,2},{1,3},{2,0},{3,1},{4,6},{5,7},{6,4},{7,5},{8,10},{9,11},{10,... | collective-permute-start | bytes 7077896 | tf_op jit(solution)/shard_map/ppermute | solution.py:33
  604.7 69.5 %collective-permute-start.61 = (bf16[1,2,2,1,96,768]{5,4,3,2,1,0:T(8,128)(2,1)}, bf16[1,2,2,1,96,768]{5,4,3,2,1,0:T(8,128)(2,1)}, u32[]{:S(2)}, u32[]{:S(2)}) collective-permute-start(bf16[1,2,2,1,96,768]{5,4,3,2,1,0:T(8,128)(2,1)} %slice.1096), channel_id=1, source_target_pairs={{0,2},{1,3},{2,0},{3,1},{4,6},{5,7},{6,4},{7,5},{8,10},{9,11},{10,... | collective-permute-start | bytes 1769480 | tf_op jit(solution)/shard_map/ppermute | solution.py:33
  609.5 91.8 %collective-permute-start.73 = (bf16[1,2,2,1,96,1536]{5,4,3,2,1,0:T(8,128)(2,1)}, bf16[1,2,2,1,96,1536]{5,4,3,2,1,0:T(8,128)(2,1)}, u32[]{:S(2)}, u32[]{:S(2)}) collective-permute-start(bf16[1,2,2,1,96,1536]{5,4,3,2,1,0:T(8,128)(2,1)} %slice.1118), channel_id=1, source_target_pairs={{0,2},{1,3},{2,0},{3,1},{4,6},{5,7},{6,4},{7,5},{8,10},{9,11},{10,... | collective-permute-start | bytes 3538952 | tf_op jit(solution)/shard_map/ppermute | solution.py:33
  735.9 152.5 %collective-permute-start.64 = (bf16[2,2,2,1,96,1536]{5,4,3,2,1,0:T(8,128)(2,1)}, bf16[2,2,2,1,96,1536]{5,4,3,2,1,0:T(8,128)(2,1)}, u32[]{:S(2)}, u32[]{:S(2)}) collective-permute-start(bf16[2,2,2,1,96,1536]{5,4,3,2,1,0:T(8,128)(2,1)} %pad_maximum_fusion.3), channel_id=1, source_target_pairs={{0,4},{4,0},{8,12},{12,8},{16,20},{20,16},{24,28},{28,24},{1,5},{5... | collective-permute-start | bytes 7077896 | tf_op jit(solution)/shard_map/ppermute | solution.py:33
  739.6 68.8 %collective-permute-start.57 = (bf16[1,2,2,1,96,768]{5,4,3,2,1,0:T(8,128)(2,1)}, bf16[1,2,2,1,96,768]{5,4,3,2,1,0:T(8,128)(2,1)}, u32[]{:S(2)}, u32[]{:S(2)}) collective-permute-start(bf16[1,2,2,1,96,768]{5,4,3,2,1,0:T(8,128)(2,1)} %slice.1088), channel_id=1, source_target_pairs={{0,2},{1,3},{2,0},{3,1},{4,6},{5,7},{6,4},{7,5},{8,10},{9,11},{10,... | collective-permute-start | bytes 1769480 | tf_op jit(solution)/shard_map/ppermute | solution.py:33
  742.4 79.6 %collective-permute-start.75 = (bf16[1,1,1,1,96,1536]{5,4,3,2,1,0:T(8,128)(2,1)}, bf16[1,1,1,1,96,1536]{5,4,3,2,1,0:T(8,128)(2,1)}, u32[]{:S(2)}, u32[]{:S(2)}) collective-permute-start(bf16[1,1,1,1,96,1536]{5,4,3,2,1,0:T(8,128)(2,1)} %slice.1122), channel_id=1, source_target_pairs={{0,8},{4,12},{8,0},{12,4},{16,24},{20,28},{24,16},{28,20},{1,9},{5... | collective-permute-start | bytes 884744 | tf_op jit(solution)/shard_map/ppermute | solution.py:33
  748.0 110.6 %collective-permute-start.69 = (bf16[1,2,2,1,96,1536]{5,4,3,2,1,0:T(8,128)(2,1)}, bf16[1,2,2,1,96,1536]{5,4,3,2,1,0:T(8,128)(2,1)}, u32[]{:S(2)}, u32[]{:S(2)}) collective-permute-start(bf16[1,2,2,1,96,1536]{5,4,3,2,1,0:T(8,128)(2,1)} %slice.1110), channel_id=1, source_target_pairs={{0,4},{4,0},{8,12},{12,8},{16,20},{20,16},{24,28},{28,24},{1,5},{5... | collective-permute-start | bytes 3538952 | tf_op jit(solution)/shard_map/ppermute | solution.py:33
  817.0 52.4 %collective-permute-start.52 = (bf16[2,2,2,1,96,768]{5,4,3,2,1,0:T(8,128)(2,1)}, bf16[2,2,2,1,96,768]{5,4,3,2,1,0:T(8,128)(2,1)}, u32[]{:S(2)}, u32[]{:S(2)}) collective-permute-start(bf16[2,2,2,1,96,768]{5,4,3,2,1,0:T(8,128)(2,1)} %pad_maximum_fusion.17), channel_id=1, source_target_pairs={{0,4},{4,0},{8,12},{12,8},{16,20},{20,16},{24,28},{28,24},{1,5},{5... | collective-permute-start | bytes 3538952 | tf_op jit(solution)/shard_map/ppermute | solution.py:33
  (342 other events, 3834.5 us)

commit v2 on v1

v2 whole, which is shorter than its diff:
```python
import functools

import jax
import jax.numpy as jnp
from jax import lax
from jax.experimental import pallas as pl
from jax.experimental.pallas import tpu as pltpu
from jax.sharding import PartitionSpec as P

HEAD_DIM = 64
LAYERS = 3
STEP = 10
MOST = 576
FF_BLOCK = 256

EPSILON = 1e-06
MASKED = -30000.0
CLIP = 0.005
BETA_ONE = 0.9
BETA_TWO = 0.999
ADAM_EPS = 1e-08
RATES = (0.02, 0.06, 0.02, 0.02, 0.02, 0.02, 0.5)
DECAYS = (0.05, 0.05, 0.05, 0.05, 0.05, 0.05, 0.0)
SQRT_HALF = 0.7071067811865476
INV_ROOT = 0.3989422804014327
HIGH = lax.Precision.HIGHEST
BF = jnp.bfloat16
F32 = jnp.float32

AXES = ("dp", "mp")
INNER = ("mp", 1)
OUTER = ("mp", 2)


def swap(value, bit):
    axis, mask = bit
    size = lax.axis_size(axis)
    return lax.ppermute(value, axis, [(i, i ^ mask) for i in range(size)])


def dp_bits():
    size = lax.axis_size("dp")
    bits = []
    mask = 1
    while mask < size:
        bits.append(("dp", mask))
        mask *= 2
    return bits


def dims_of(bits):
    return {bit: i for i, bit in enumerate([OUTER, bits[0]] + bits[:0:-1])}


def gather(value, order, dims):
    value = value.reshape((1,) * len(dims) + value.shape)
    for bit in order:
        value = jnp.concatenate([value, swap(value, bit)], dims[bit])
    return value


def scatter(keep, send, order, dims):
    for bit, after in zip(order, order[1:] + [None]):
        value = keep.astype(F32) + swap(send.astype(BF), bit).astype(F32)
        if after is None:
            return value.reshape(value.shape[len(dims) :])
        value = value.astype(BF)
        keep = lax.index_in_dim(value, 0, dims[after])
        send = lax.index_in_dim(value, 1, dims[after])


def both(part):
    return part + swap(part.astype(BF), INNER).astype(F32)


def dot(left, right, contract):
    return lax.dot_general(left, right, ((contract[0:1], contract[1:2]), ((), ())), preferred_element_type=F32)


def nn(left, right):
    return dot(left, right, (1, 0))


def nt(left, right):
    return dot(left, right, (1, 1))


def tn(left, right):
    return dot(left, right, (0, 0))


def norm_stats(value):
    centred = value - jnp.mean(value, -1, keepdims=True)
    variance = jnp.mean(centred * centred, -1, keepdims=True)
    rstd = lax.rsqrt(variance + EPSILON)
    return centred * rstd, rstd


def layer_norm(value, norm):
    return norm_stats(value)[0] * norm[0:1] + norm[1:2]


def norm_back(value, norm, d_out):
    hat, rstd = norm_stats(value)
    d_hat = d_out * norm[0:1]
    d_value = rstd * (
        d_hat - jnp.mean(d_hat, -1, keepdims=True) - hat * jnp.mean(d_hat * hat, -1, keepdims=True)
    )
    return d_value, jnp.concatenate([jnp.sum(d_out * hat, 0, keepdims=True), jnp.sum(d_out, 0, keepdims=True)], 0)


def load_weight(w, a_ref, b_ref, half, by_outer):
    step = pl.program_id(0)
    rows = w.shape[0] // 2
    if by_outer:

        @pl.when(step < half)
        def _():
            w[:rows] = a_ref[0]
            w[rows:] = a_ref[1]

        @pl.when(step >= half)
        def _():
            w[:rows] = b_ref[0]
            w[rows:] = b_ref[1]

    else:
        w[:rows] = a_ref[0]
        w[rows:] = b_ref[0]


def store_grad(parts, a_ref, b_ref, half, by_outer):
    step = pl.program_id(0)

    def put(target, which, top):
        at = 0
        for part in parts:
            rows = part.shape[0] // 2
            value = part[:rows] if top else part[rows:]
            target[which, :, at : at + part.shape[1]] = value.astype(BF)
            at += part.shape[1]

    if by_outer:

        @pl.when(step < half)
        def _():
            put(a_ref, 0, True)
            put(a_ref, 1, False)

        @pl.when(step >= half)
        def _():
            put(b_ref, 0, True)
            put(b_ref, 1, False)

    else:
        put(a_ref, 0, True)
        put(b_ref, 0, False)


def half_specs(weight, columns, by_outer):
    half = weight.shape[2] // columns
    rows = weight.shape[1]
    if by_outer:
        return half, [
            pl.BlockSpec((2, rows, columns), lambda i: (0, 0, jnp.minimum(i, half - 1))),
            pl.BlockSpec((2, rows, columns), lambda i: (0, 0, jnp.maximum(i - half, 0))),
        ]
    return half, [pl.BlockSpec((1, rows, columns), lambda i: (i // half, 0, i % half))] * 2


def full(value):
    return pl.BlockSpec(value.shape, lambda i: (0,) * len(value.shape))


def spec_of(shape):
    return pl.BlockSpec(shape, lambda i: (0,) * len(shape))


def params():
    return pltpu.CompilerParams(dimension_semantics=("arbitrary",), vmem_limit_bytes=56 * 1024 * 1024)


def masked_probs(query, key, keep):
    scores = jnp.where(keep, nt(query, key) * HEAD_DIM ** (-0.5), MASKED)
    weight = jnp.exp(scores - jnp.max(scores, -1, keepdims=True))
    return weight / jnp.sum(weight, -1, keepdims=True)


def attn_fwd_kernel(count, half, by_outer, *refs):
    adds = refs[:count]
    norm, segq, segk, a_ref, b_ref, x_ref, mix_ref, part_ref, normed, w, acc = refs[count:]
    step = pl.program_id(0)

    @pl.when(step == 0)
    def _():
        x = adds[0][...]
        for other in adds[1:]:
            x = x + other[...].astype(F32)
        x_ref[...] = x
        normed[...] = layer_norm(x, norm[...]).astype(BF)
        acc[...] = jnp.zeros_like(acc)

    load_weight(w, a_ref, b_ref, half, by_outer)
    mixed = nn(normed[...], w[...]).astype(BF)
    c = HEAD_DIM
    keep = segq[...] == segk[...]
    probs = masked_probs(mixed[:, :c], mixed[:, c : 2 * c], keep)
    out = nn(probs.astype(BF), mixed[:, 2 * c : 3 * c]).astype(BF)
    mix_ref[0] = jnp.concatenate([mixed[:, : 3 * c], out], 1)
    acc[...] += nt(out, w[:, 3 * c :])

    @pl.when(step == pl.num_programs(0) - 1)
    def _():
        part_ref[...] = acc[...].astype(BF)


def attn_forward(adds, norm, segq, segk, pair, by_outer):
    tokens, width = adds[0].shape
    columns = 4 * HEAD_DIM
    half, halves = half_specs(pair[0], columns, by_outer)
    return pl.pallas_call(
        functools.partial(attn_fwd_kernel, len(adds), half, by_outer),
        grid=(2 * half,),
        in_specs=[full(v) for v in adds] + [full(norm), full(segq), full(segk)] + halves,
        out_specs=[
            spec_of((tokens, width)),
            pl.BlockSpec((1, tokens, columns), lambda i: (i, 0, 0)),
            spec_of((tokens, width)),
        ],
        out_shape=[
            jax.ShapeDtypeStruct((tokens, width), F32),
            jax.ShapeDtypeStruct((2 * half, tokens, columns), BF),
            jax.ShapeDtypeStruct((tokens, width), BF),
        ],
        scratch_shapes=[
            pltpu.VMEM((tokens, width), BF),
            pltpu.VMEM((width, columns), BF),
            pltpu.VMEM((tokens, width), F32),
        ],
        compiler_params=params(),
        cost_estimate=pl.CostEstimate(flops=16 * 10**9, bytes_accessed=10**7, transcendentals=10**6),
        name="attn_forward",
    )(*adds, norm, segq, segk, *pair)


def ff_fwd_kernel(count, half, by_outer, *refs):
    adds = refs[:count]
    norm, a_ref, b_ref, x_ref, part_ref, normed, w, acc = refs[count:]
    step = pl.program_id(0)

    @pl.when(step == 0)
    def _():
        x = adds[0][...]
        for other in adds[1:]:
            x = x + other[...].astype(F32)
        x_ref[...] = x
        normed[...] = layer_norm(x, norm[...]).astype(BF)
        acc[...] = jnp.zeros_like(acc)

    load_weight(w, a_ref, b_ref, half, by_outer)
    columns = w.shape[1] // 2
    up = nn(normed[...], w[:, :columns])
    active = (0.5 * up * (1.0 + lax.erf(up * SQRT_HALF))).astype(BF)
    acc[...] += nt(active, w[:, columns:])

    @pl.when(step == pl.num_programs(0) - 1)
    def _():
        part_ref[...] = acc[...].astype(BF)


def ff_forward(adds, norm, pair, by_outer):
    tokens, width = adds[0].shape
    columns = FF_BLOCK * 2
    half, halves = half_specs(pair[0], columns, by_outer)
    return pl.pallas_call(
        functools.partial(ff_fwd_kernel, len(adds), half, by_outer),
        grid=(2 * half,),
        in_specs=[full(v) for v in adds] + [full(norm)] + halves,
        out_specs=[spec_of((tokens, width)), spec_of((tokens, width))],
        out_shape=[
            jax.ShapeDtypeStruct((tokens, width), F32),
            jax.ShapeDtypeStruct((tokens, width), BF),
        ],
        scratch_shapes=[
            pltpu.VMEM((tokens, width), BF),
            pltpu.VMEM((width, columns), BF),
            pltpu.VMEM((tokens, width), F32),
        ],
        compiler_params=params(),
        cost_estimate=pl.CostEstimate(flops=10 * 10**9, bytes_accessed=10**7, transcendentals=10**6),
        name="ff_forward",
    )(*adds, norm, *pair)


def back_prologue(back, d_ref, g_ref):
    d_base = back[0][...]
    if len(back) == 1:
        d_ref[...] = d_base
        return d_base
    value, norm, own, other = back[1:]
    d_value, g_ref[...] = norm_back(value[...], norm[...], own[...].astype(F32) + other[...].astype(F32))
    d_all = d_base + d_value
    d_ref[...] = d_all
    return d_all


def ff_back_kernel(count, half, by_outer, *refs):
    back = refs[:count]
    value, norm, a_ref, b_ref, d_ref, ga_ref, gb_ref, part_ref, g_ref = refs[count : count + 9]
    normed, normed_t, dz, dz_t, w, acc = refs[count + 9 :]
    step = pl.program_id(0)

    @pl.when(step == 0)
    def _():
        d_all = back_prologue(back, d_ref, g_ref)
        dz[...] = d_all.astype(BF)
        dz_t[...] = d_all.T.astype(BF)
        here = layer_norm(value[...], norm[...])
        normed[...] = here.astype(BF)
        normed_t[...] = here.T.astype(BF)
        acc[...] = jnp.zeros_like(acc)

    load_weight(w, a_ref, b_ref, half, by_outer)
    columns = w.shape[1] // 2
    up = nn(normed[...], w[:, :columns])
    phi = 0.5 * (1.0 + lax.erf(up * SQRT_HALF))
    active = (up * phi).astype(BF)
    slope = phi + up * jnp.exp(-0.5 * up * up) * INV_ROOT
    d_up = (nn(dz[...], w[:, columns:]) * slope).astype(BF)
    acc[...] += nt(d_up, w[:, :columns])
    store_grad([nn(normed_t[...], d_up), nn(dz_t[...], active)], ga_ref, gb_ref, half, by_outer)

    @pl.when(step == pl.num_programs(0) - 1)
    def _():
        part_ref[...] = acc[...].astype(BF)


def back_out(tokens, width, pair, halves):
    specs = [spec_of((tokens, width))] + halves + [spec_of((tokens, width)), spec_of((2, width))]
    shapes = [
        jax.ShapeDtypeStruct((tokens, width), F32),
        jax.ShapeDtypeStruct(pair[0].shape, BF),
        jax.ShapeDtypeStruct(pair[0].shape, BF),
        jax.ShapeDtypeStruct((tokens, width), BF),
        jax.ShapeDtypeStruct((2, width), F32),
    ]
    return specs, shapes


def ff_backward(back, value, norm, pair, by_outer):
    tokens, width = value.shape
    columns = FF_BLOCK * 2
    half, halves = half_specs(pair[0], columns, by_outer)
    specs, shapes = back_out(tokens, width, pair, halves)
    return pl.pallas_call(
        functools.partial(ff_back_kernel, len(back), half, by_outer),
        grid=(2 * half,),
        in_specs=[full(v) for v in back] + [full(value), full(norm)] + halves,
        out_specs=specs,
        out_shape=shapes,
        scratch_shapes=[
            pltpu.VMEM((tokens, width), BF),
            pltpu.VMEM((width, tokens), BF),
            pltpu.VMEM((tokens, width), BF),
            pltpu.VMEM((width, tokens), BF),
            pltpu.VMEM((width, columns), BF),
            pltpu.VMEM((tokens, width), F32),
        ],
        compiler_params=params(),
        cost_estimate=pl.CostEstimate(flops=18 * 10**9, bytes_accessed=10**7, transcendentals=10**6),
        name="ff_backward",
    )(*back, value, norm, *pair)


def attn_back_kernel(count, half, by_outer, *refs):
    back = refs[:count]
    value, norm, segq, segk, mix_ref, a_ref, b_ref, d_ref, ga_ref, gb_ref, part_ref, g_ref = refs[count : count + 12]
    normed_t, dy, dy_t, w, acc = refs[count + 12 :]
    step = pl.program_id(0)

    @pl.when(step == 0)
    def _():
        d_all = back_prologue(back, d_ref, g_ref)
        dy[...] = d_all.astype(BF)
        dy_t[...] = d_all.T.astype(BF)
        normed_t[...] = layer_norm(value[...], norm[...]).T.astype(BF)
        acc[...] = jnp.zeros_like(acc)

    load_weight(w, a_ref, b_ref, half, by_outer)
    c = HEAD_DIM
    scale = HEAD_DIM ** (-0.5)
    query, key, val = (mix_ref[0, :, j * c : (j + 1) * c] for j in range(3))
    d_out = nn(dy[...], w[:, 3 * c :]).astype(BF)
    keep = segq[...] == segk[...]
    probs = masked_probs(query, key, keep)
    d_probs = nt(d_out, val)
    delta = jnp.sum(probs * d_probs, -1, keepdims=True)
    d_scores = jnp.where(keep, probs * (d_probs - delta), 0.0).astype(BF)
    d_query = (nn(d_scores, key) * scale).astype(BF)
    d_key = (tn(d_scores, query) * scale).astype(BF)
    d_val = tn(probs.astype(BF), d_out).astype(BF)
    d_left = jnp.concatenate([d_query, d_key], 1)
    zero = jnp.zeros_like(d_val)
    d_right = jnp.concatenate([d_val, zero], 1)
    out = jnp.concatenate([zero, mix_ref[0, :, 3 * c :]], 1)
    acc[...] += nt(d_left, w[:, : 2 * c]) + nt(d_right, w[:, 2 * c :])
    left = nn(normed_t[...], d_left)
    right = nn(normed_t[...], d_right) + nn(dy_t[...], out)
    store_grad([left, right], ga_ref, gb_ref, half, by_outer)

    @pl.when(step == pl.num_programs(0) - 1)
    def _():
        part_ref[...] = acc[...].astype(BF)


def attn_backward(back, value, norm, segq, segk, mix, pair, by_outer):
    tokens, width = value.shape
    columns = 4 * HEAD_DIM
    half, halves = half_specs(pair[0], columns, by_outer)
    specs, shapes = back_out(tokens, width, pair, halves)
    return pl.pallas_call(
        functools.partial(attn_back_kernel, len(back), half, by_outer),
        grid=(2 * half,),
        in_specs=[full(v) for v in back]
        + [full(value), full(norm), full(segq), full(segk)]
        + [pl.BlockSpec((1, tokens, columns), lambda i: (i, 0, 0))]
        + halves,
        out_specs=specs,
        out_shape=shapes,
        scratch_shapes=[
            pltpu.VMEM((width, tokens), BF),
            pltpu.VMEM((tokens, width), BF),
            pltpu.VMEM((width, tokens), BF),
            pltpu.VMEM((width, columns), BF),
            pltpu.VMEM((tokens, width), F32),
        ],
        compiler_params=params(),
        cost_estimate=pl.CostEstimate(flops=30 * 10**9, bytes_accessed=10**7, transcendentals=10**6),
        name="attn_backward",
    )(*back, value, norm, segq, segk, mix, *pair)


def adam(weight, grad, first, second, rate, decay):
    first = BETA_ONE * first + (1.0 - BETA_ONE) * grad
    second = BETA_TWO * second + (1.0 - BETA_TWO) * grad * grad
    update = first / (1.0 - BETA_ONE**STEP) / (jnp.sqrt(second / (1.0 - BETA_TWO**STEP)) + ADAM_EPS)
    return (first, second, weight - rate * (update + decay * weight))


def body(pixels, lengths, valid_mask, teacher_logits, teacher_map, *state):
    masters, firsts, seconds = state[:7], state[7:14], state[14:]
    attend_in, attend_out, hidden_up, hidden_down, patch_embed, class_head, norm_params = masters
    bits = dp_bits()
    dims = dims_of(bits)
    low, high = bits[0], bits[1:]
    outer_last = high + [low, OUTER]
    low_last = high + [OUTER, low]
    rows = patch_embed.shape[1]
    inner = lax.axis_index("mp") % 2
    outer = lax.axis_index("mp") // 2
    images = lengths.shape[1]
    tokens = pixels.shape[0]
    total_images = images * lax.axis_size("dp")

    heads = attend_in.shape[3] // HEAD_DIM
    hidden = hidden_up.shape[2]
    width = attend_out.shape[2] * lax.axis_size("dp")

    def attn_unit(l):
        into = attend_in[l].astype(BF).reshape(3, rows, heads, HEAD_DIM)
        out = attend_out[l].T.astype(BF).reshape(1, rows, heads, HEAD_DIM)
        return jnp.concatenate([into, out], 0).transpose(1, 2, 0, 3).reshape(rows, -1)

    def ff_unit(l):
        up = hidden_up[l].astype(BF).reshape(rows, -1, 1, FF_BLOCK)
        down = hidden_down[l].T.astype(BF).reshape(rows, -1, 1, FF_BLOCK)
        return jnp.concatenate([up, down], 2).reshape(rows, -1)

    half = class_head.shape[1] // 2
    head_unit = lax.dynamic_slice_in_dim(class_head.astype(BF), inner * half, half, 1)

    def pair_of(unit, order):
        own = gather(unit, order[:-1], dims)
        other = swap(own, order[-1])
        return tuple(v.reshape(2, width // 2, v.shape[-1]) for v in (own, other))

    row = lengths[0]
    ends = jnp.cumsum(row)
    longest = jnp.argmax(row)
    start = ends[longest] - row[longest]
    place = jnp.arange(MOST, dtype=jnp.int32)

    def mine(value, which):
        twice = jnp.concatenate([value, value], 0)
        return lax.dynamic_slice_in_dim(twice, start + MOST * which, MOST, 0)

    pix = [mine(pixels, outer), mine(pixels, 1 - outer)]
    held = jnp.where(outer == 0, MOST, tokens - MOST)
    position = (start + MOST * outer + place) % tokens
    segment = jnp.sum((position[:, None] >= ends[None, :]).astype(jnp.int32), 1)
    valid = jnp.where(place < held, mine(valid_mask, outer), 0) > 0
    segq = segment[:, None]
    segk = jnp.where(valid, segment, -1)[None, :]
    image_ids = jnp.arange(images, dtype=jnp.int32)
    member = ((segment[None, :] == image_ids[:, None]) & valid[None, :]).astype(F32)
    owned = ((image_ids == longest) == (outer == 0)).astype(F32)[:, None]
    count = jnp.sum(member, 1)

    norms = gather(norm_params.astype(BF).reshape(-1, rows), high + [low], dims)
    norms = jnp.moveaxis(norms.reshape(-1, 7, 2, rows), 0, 2).reshape(7, 2, -1).astype(F32)

    patch = gather(patch_embed.T.astype(BF), high + [low], dims).reshape(width, -1)
    attn_outer = [True, False, True]
    ff_outer = [False, True, False]
    orders = {True: outer_last, False: low_last}
    attn, ff = [], []
    for l in range(LAYERS):
        attn.append(pair_of(attn_unit(l), orders[attn_outer[l]]))
        ff.append(pair_of(ff_unit(l), orders[ff_outer[l]]))
    head = gather(head_unit, high + [low], dims).reshape(width, half)

    teach_log = jax.nn.log_softmax(teacher_logits, -1)
    teach_log = gather(lax.dynamic_slice_in_dim(teach_log, inner * half, half, 1), high + [low], dims)
    teach_log = jnp.swapaxes(teach_log.reshape((2, -1, images, half)), 0, 1).reshape(-1, images, half)
    me = lax.axis_index("dp")
    source = jnp.sum(jnp.where(teacher_map == me, jnp.arange(teacher_map.shape[0], dtype=jnp.int32), 0))
    teach_log = lax.dynamic_index_in_dim(teach_log, jnp.bitwise_xor(source, me), 0, False)

    mid = width // 2

    def of_inner(value, which):
        return jnp.where(which == 0, value[..., :mid], value[..., mid:])

    part = nt(jnp.concatenate(pix, 0), patch).astype(BF)
    part = of_inner(part, inner).astype(F32) + swap(of_inner(part, 1 - inner), INNER).astype(F32)
    part = part[:MOST] + swap(part[MOST:].astype(BF), OUTER).astype(F32)
    other = swap(part, INNER)
    x = jnp.where(inner == 0, jnp.concatenate([part, other], 1), jnp.concatenate([other, part], 1))

    adds = [x]
    xs, middles, mixes = [], [], []
    for l in range(LAYERS):
        x, mix, own = attn_forward(adds, norms[2 * l], segq, segk, attn[l], attn_outer[l])
        middle, own = ff_forward([x, own, swap(own, INNER)], norms[2 * l + 1], ff[l], ff_outer[l])
        adds = [middle, own, swap(own, INNER)]
        xs.append(x)
        middles.append(middle)
        mixes.append(mix)
    x = sum(v.astype(F32) for v in adds)

    divisor = jnp.maximum(count, 1.0)[:, None]
    pooled = jnp.dot(member, x, precision=HIGH) / divisor
    pooled_normed = layer_norm(pooled, norms[-1]).astype(BF)
    logits = nn(pooled_normed, head)
    theirs = swap(logits, INNER)
    peak = jnp.maximum(jnp.max(logits, -1, keepdims=True), jnp.max(theirs, -1, keepdims=True))
    total = jnp.sum(jnp.exp(logits - peak), -1, keepdims=True) + jnp.sum(jnp.exp(theirs - peak), -1, keepdims=True)
    student_log = logits - peak - jnp.log(total)
    loss_local = jnp.sum(owned * jnp.exp(teach_log) * (teach_log - student_log))
    d_logits = (owned * (jnp.exp(student_log) - jnp.exp(teach_log)) / total_images).astype(BF)
    g_head = tn(pooled_normed, d_logits).astype(BF)
    d_pooled, g_final = norm_back(pooled, norms[-1], both(nt(d_logits, head)))
    d_x = lax.dot_general(member, d_pooled / divisor, (((0,), (0,)), ((), ())), precision=HIGH)

    shape = (1,) + (2,) * len(bits)

    def halved(grad):
        grad = grad.reshape(shape + (rows, grad.shape[-1]))
        return lax.index_in_dim(grad, 0, dims[low]), lax.index_in_dim(grad, 1, dims[low])

    def split(keep, send, by_outer):
        order = orders[by_outer][::-1]
        lead = list((2,) * (1 + len(bits)))
        lead[dims[order[0]]] = 1
        keep, send = (v.reshape(tuple(lead) + (rows, v.shape[-1])) for v in (keep, send))
        return scatter(keep, send, order, dims)

    dp_order = (high + [low])[::-1]
    g_attn, g_ff, g_norms = [None] * LAYERS, [None] * LAYERS, [None] * LAYERS
    g_head = scatter(*halved(g_head), dp_order, dims)
    back = [d_x]
    for l in reversed(range(LAYERS)):
        d_x, keep, send, own, g_above = ff_backward(back, middles[l], norms[2 * l + 1], ff[l], ff_outer[l])
        if l < LAYERS - 1:
            g_norms[l + 1].insert(0, g_above)
        g_ff[l] = split(keep, send, ff_outer[l])
        back = [d_x, middles[l], norms[2 * l + 1], own, swap(own, INNER)]
        d_mid, keep, send, own, g_two = attn_backward(
            back, xs[l], norms[2 * l], segq, segk, mixes[l], attn[l], attn_outer[l]
        )
        g_norms[l] = [g_two]
        g_attn[l] = split(keep, send, attn_outer[l])
        back = [d_mid, xs[l], norms[2 * l], own, swap(own, INNER)]
    d_low, g_one = norm_back(xs[0], norms[0], back[3].astype(F32) + back[4].astype(F32))
    g_norms[0].insert(0, g_one)
    d_x0 = (back[0] + d_low).astype(BF)
    theirs = swap(of_inner(d_x0, inner), OUTER)
    other = swap(theirs, INNER)
    theirs = jnp.where(inner == 0, jnp.concatenate([theirs, other], 1), jnp.concatenate([other, theirs], 1))
    g_patch = tn(jnp.concatenate([d_x0, theirs], 0), jnp.concatenate(pix, 0)).astype(BF)
    g_patch = scatter(*halved(g_patch), dp_order, dims)

    g_head = g_head + swap(g_head, OUTER)
    other_half = swap(g_head, INNER)
    g_head = jnp.where(inner == 0, jnp.concatenate([g_head, other_half], 1), jnp.concatenate([other_half, g_head], 1))
    g_norm = jnp.stack([g for pair in g_norms for g in pair] + [g_final]).reshape(14, -1, rows)
    g_norm = jnp.moveaxis(g_norm, 1, 0).reshape(shape + (14, rows))
    for bit in dp_order:
        g_norm = lax.index_in_dim(g_norm, 0, dims[bit]) + swap(lax.index_in_dim(g_norm, 1, dims[bit]), bit)
    g_norm = g_norm.reshape(14, rows)
    g_norm = g_norm + swap(g_norm, OUTER)
    other_norm = swap(g_norm, INNER)
    g_norm = (0.5 * (g_norm + other_norm)).reshape(7, 2, rows)

    g_attn_heads = [g.reshape(rows, heads, 4, HEAD_DIM) for g in g_attn]
    g_ff_blocks = [g.reshape(rows, -1, 2, FF_BLOCK) for g in g_ff]
    grads = (
        jnp.stack([jnp.stack([g[:, :, j].reshape(rows, -1) for j in range(3)]) for g in g_attn_heads]),
        jnp.stack([g[:, :, 3].reshape(rows, -1).T for g in g_attn_heads]),
        jnp.stack([g[:, :, 0].reshape(rows, -1) for g in g_ff_blocks]),
        jnp.stack([g[:, :, 1].reshape(rows, -1).T for g in g_ff_blocks]),
        g_patch.T,
        g_head,
        g_norm,
    )
    first_model = (lax.axis_index("mp") == 0).astype(F32)
    squares = sum(jnp.sum(g * g) for g in g_attn + g_ff + [g_patch]) + first_model * (
        jnp.sum(g_head * g_head) + jnp.sum(g_norm * g_norm)
    )
    sums = jnp.stack([squares, loss_local * (outer >= 0)])
    for bit in [INNER, OUTER] + bits:
        sums = sums + swap(sums, bit)
    loss = sums[1]
    grad_norm = jnp.sqrt(sums[0])
    clip = jnp.minimum(1.0, CLIP / grad_norm)
    results = []
    for kind in range(7):
        results.append(
            adam(masters[kind], grads[kind] * clip, firsts[kind], seconds[kind], RATES[kind], DECAYS[kind])
        )
    return (loss, grad_norm) + tuple(r[i] for i in range(3) for r in results)


def solution(mesh):
    weights = (
        P(None, None, "dp", "mp"),
        P(None, "mp", "dp"),
        P(None, "dp", "mp"),
        P(None, "mp", "dp"),
        P("mp", "dp"),
        P("dp", None),
        P(None, None, "dp"),
    )
    placed = (P("dp", "mp"), P("dp", None), P("dp"), P("dp", None), P()) + weights * 3
    return jax.shard_map(
        body, mesh=mesh, in_specs=placed, out_specs=(P(), P()) + weights * 3, check_vma=False
    )
```

time: 1030 us -> 842 us (0.82)
  matrix products: 346 us -> 8.83 us
  Pallas kernels: 0 us -> 226 us
  other arithmetic: 177 us -> 94.7 us
    pallas_call x0 -> x12, Pallas kernels: none -> 226 us  [the longest x3 86.5 us: attn_backward(): pl.pallas_call(functools.partial(attn_back_kernel, len(back), half, by_ou...]
    dot_general x115 -> x5, matrix products: 187 us -> 4.47 us  [dot(): lax.dot_general(left, right, ((contract[0:1], contract[1:2]), ((), ())),...]
    dot_general x15 -> x0, matrix products: 129 us -> none  [the longest x3 46 us: attend_back(): jnp.einsum('hts,htc->hsc', d_scores, query, preferred_element_type=F32)]
    concatenate x11 -> x3, local copies, waits for them, and re-layouts: 30 us -> 1.27 us  [ff_unit(): return jnp.concatenate([up, down], 2).reshape(rows, -1)]
    sub x3 -> x0, matrix products: 24.4 us -> none  [softmax_scores(): return jax.nn.softmax(jnp.where(keep[None], scores, MASKED), -1)]
    convert_element_type x13 -> x1, other arithmetic: 19.1 us -> 2.32 us  [body(): d_x0 = (back[0] + d_low).astype(BF)]
    concatenate x12 -> x3, other arithmetic: 16.3 us -> 0.83 us  [ff_unit(): return jnp.concatenate([up, down], 2).reshape(rows, -1)]
    slice x30 -> x37, local copies, waits for them, and re-layouts: 11.9 us -> 26 us  [the longest x22 9.82 us: scatter(): send = lax.index_in_dim(value, 1, dims[after])]
  transfers between devices with their start and end apart: 96 -> 97, of which waited for: 37 -> 41; matrix products, arithmetic and copies ran while one was open for 57% -> 20% of each run, Pallas kernels for 0% -> 25%
where the time goes in v2:
time: 842 us; the launch traced here: 836 us
  waiting for transfers between devices  297 us (35%)
  Pallas kernels  226 us (27%)
  local copies, waits for them, and re-layouts  99.2 us (12%)
  starting transfers between devices  95.8 us (11%)
  other arithmetic  94.7 us (11%)
  between operations  14.9 us (2%)
  matrix products  8.83 us (1%)
    ppermute x97, waiting for transfers between devices, swap(): return lax.ppermute(value, axis, [(i, i ^ mask) for i in range(size)])  297 us
    ppermute x97, starting transfers between devices, swap(): return lax.ppermute(value, axis, [(i, i ^ mask) for i in range(size)])  95.8 us
    pallas_call x3, Pallas kernels, attn_backward(): pl.pallas_call(functools.partial(attn_back_kernel, len(back), half, by_ou...  86.5 us
    pallas_call x3, Pallas kernels, attn_forward(): pl.pallas_call(functools.partial(attn_fwd_kernel, len(adds), half, by_out...  53 us
    pallas_call x3, Pallas kernels, ff_backward(): pl.pallas_call(functools.partial(ff_back_kernel, len(back), half, by_oute...  52.6 us
    pallas_call x3, Pallas kernels, ff_forward(): pl.pallas_call(functools.partial(ff_fwd_kernel, len(adds), half, by_outer...  34.2 us
    concatenate x25, other arithmetic, gather(): value = jnp.concatenate([value, swap(value, bit)], dims[bit])  27.9 us
    unnamed x230, local copies, waits for them, and re-layouts  27.3 us
  transfers between devices with their start and end apart: 97, of which 41 were waited for; matrix products, arithmetic and copies ran while one was open for 20% of the time, Pallas kernels for 25%

profile of v2, /device:TPU:0, one launch (start us, length us, event | category | flops | bytes accessed | tf_op | source)
XLA Modules:
  0.0 836.5 jit_solution(2052831229820757895)
XLA Ops:
  65.6 19.5 %collective-permute-done.10 = bf16[1,1,1,2,96,768]{4,5,3,2,1,0:T(8,128)(2,1)S(1)} collective-permute-done((bf16[1,1,1,2,96,768]{4,5,3,2,1,0:T(8,128)(2,1)S(1)}, bf16[1,1,1,2,96,768]{4,5,3,2,1,0:T(8,128)(2,1)S(1)}, u32[]{:S(2)}, u32[]{:S(2)}) %collective-permute-start.10) | collective-permute-done | bytes 294944 | tf_op jit(solution)/shard_map/ppermute | solution.py:38
  92.5 11.4 %collective-permute-done.15 = bf16[1,1,1,2,96,1536]{5,4,3,2,1,0:T(8,128)(2,1)} collective-permute-done((bf16[1,1,1,2,96,1536]{5,4,3,2,1,0:T(8,128)(2,1)}, bf16[1,1,1,2,96,1536]{5,4,3,2,1,0:T(8,128)(2,1)}, u32[]{:S(2)}, u32[]{:S(2)}) %collective-permute-start.15) | collective-permute-done | bytes 589856 | tf_op jit(solution)/shard_map/ppermute | solution.py:38
  141.6 18.0 %collective-permute-done.12 = bf16[1,2,2,2,96,768]{5,4,3,2,1,0:T(8,128)(2,1)} collective-permute-done((bf16[1,2,2,2,96,768]{5,4,3,2,1,0:T(8,128)(2,1)}, bf16[1,2,2,2,96,768]{5,4,3,2,1,0:T(8,128)(2,1)}, u32[]{:S(2)}, u32[]{:S(2)}) %collective-permute-start.12) | collective-permute-done | bytes 1179680 | tf_op jit(solution)/shard_map/ppermute | solution.py:38
  159.5 17.5 %attn_forward.3 = (f32[576,768]{1,0:T(8,128)}, bf16[6,576,256]{2,1,0:T(8,128)(2,1)}, bf16[576,768]{1,0:T(8,128)(2,1)}) custom-call(f32[576,768]{1,0:T(8,128)} %maximum_select_fusion.refs_0_, f32[2,768]{1,0:T(2,128)} %squeeze.21.refs_1_.refs_6_, s32[576,1]{1,0:T(8,128)} %broadcast_in_dim.33.refs_2_.refs_4_.refs_7_, ...), custom_call_target="tpu_custom_call" | custom-call | flops 16000000000 | bytes 10000000 | tf_op jit(solution)/shard_map/attn_forward/pallas_call | solution.py:221
  202.9 11.2 %ff_forward.3 = (f32[576,768]{1,0:T(8,128)}, bf16[576,768]{1,0:T(8,128)(2,1)}) custom-call(f32[576,768]{1,0:T(8,128)} %get-tuple-element.69.refs_0_.refs_5_, bf16[576,768]{1,0:T(8,128)(2,1)} %get-tuple-element.70.refs_1_, bf16[576,768]{1,0:T(8,128)(2,1)} %collective-permute-done.13.refs_2_, f32[2,768]{1,0:T(2,128)} %squeeze.22.refs_3_.refs_6_.refs_2_, ...), custom_call_target="tpu_custom_call" | custom-call | flops 10000000000 | bytes 10000000 | tf_op jit(solution)/shard_map/ff_forward/pallas_call | solution.py:275
  229.9 19.4 %collective-permute-done.22 = bf16[2,1,2,2,96,768]{5,4,3,2,1,0:T(8,128)(2,1)} collective-permute-done((bf16[2,1,2,2,96,768]{5,4,3,2,1,0:T(8,128)(2,1)}, bf16[2,1,2,2,96,768]{5,4,3,2,1,0:T(8,128)(2,1)}, u32[]{:S(2)}, u32[]{:S(2)}) %collective-permute-start.22) | collective-permute-done | bytes 1179680 | tf_op jit(solution)/shard_map/ppermute | solution.py:38
  249.3 17.6 %attn_forward.4 = (f32[576,768]{1,0:T(8,128)}, bf16[6,576,256]{2,1,0:T(8,128)(2,1)}, bf16[576,768]{1,0:T(8,128)(2,1)}) custom-call(f32[576,768]{1,0:T(8,128)} %get-tuple-element.71.refs_0_.refs_5_.refs_1_, bf16[576,768]{1,0:T(8,128)(2,1)} %get-tuple-element.72.refs_1_, bf16[576,768]{1,0:T(8,128)(2,1)} %collective-permute-done.18.refs_2_, ...), custom_call_target="tpu_custom_call" | custom-call | flops 16000000000 | bytes 10000000 | tf_op jit(solution)/shard_map/attn_forward/pallas_call | solution.py:221
  290.4 11.9 %ff_forward.4 = (f32[576,768]{1,0:T(8,128)}, bf16[576,768]{1,0:T(8,128)(2,1)}) custom-call(f32[576,768]{1,0:T(8,128)} %get-tuple-element.73.refs_0_.refs_5_.refs_1_, bf16[576,768]{1,0:T(8,128)(2,1)} %get-tuple-element.74.refs_1_, bf16[576,768]{1,0:T(8,128)(2,1)} %collective-permute-done.23.refs_2_, f32[2,768]{1,0:T(2,128)} %squeeze.24.refs_3_.refs_6_.refs_2_, ...), custom_call_target="tpu_custom_call" | custom-call | flops 10000000000 | bytes 10000000 | tf_op jit(solution)/shard_map/ff_forward/pallas_call | solution.py:275
  312.8 17.0 %collective-permute-done.32 = bf16[1,2,2,2,96,768]{5,4,3,2,1,0:T(8,128)(2,1)S(1)} collective-permute-done((bf16[1,2,2,2,96,768]{5,4,3,2,1,0:T(8,128)(2,1)}, bf16[1,2,2,2,96,768]{5,4,3,2,1,0:T(8,128)(2,1)S(1)}, u32[]{:S(2)}, u32[]{:S(2)}) %collective-permute-start.32) | collective-permute-done | bytes 1179680 | tf_op jit(solution)/shard_map/ppermute | solution.py:38
  330.7 17.8 %attn_forward.5 = (f32[576,768]{1,0:T(8,128)}, bf16[6,576,256]{2,1,0:T(8,128)(2,1)}, bf16[576,768]{1,0:T(8,128)(2,1)}) custom-call(f32[576,768]{1,0:T(8,128)} %get-tuple-element.75.refs_0_.refs_5_.refs_1_, bf16[576,768]{1,0:T(8,128)(2,1)} %get-tuple-element.76.refs_1_, bf16[576,768]{1,0:T(8,128)(2,1)} %collective-permute-done.28.refs_2_, ...), custom_call_target="tpu_custom_call" | custom-call | flops 16000000000 | bytes 10000000 | tf_op jit(solution)/shard_map/attn_forward/pallas_call | solution.py:221
  361.0 11.2 %ff_forward.5 = (f32[576,768]{1,0:T(8,128)}, bf16[576,768]{1,0:T(8,128)(2,1)}) custom-call(f32[576,768]{1,0:T(8,128)} %get-tuple-element.77.refs_0_.refs_5_.refs_1_, bf16[576,768]{1,0:T(8,128)(2,1)} %get-tuple-element.78.refs_1_, bf16[576,768]{1,0:T(8,128)(2,1)} %copy-done.101, f32[2,768]{1,0:T(2,128)} %squeeze.26.refs_3_.refs_2_, ...), custom_call_target="tpu_custom_call" | custom-call | flops 10000000000 | bytes 10000000 | tf_op jit(solution)/shard_map/ff_forward/pallas_call | solution.py:275
  394.5 15.5 %ff_backward.3 = (f32[576,768]{1,0:T(8,128)}, bf16[2,384,1536]{2,1,0:T(8,128)(2,1)}, bf16[2,384,1536]{2,1,0:T(8,128)(2,1)}, bf16[576,768]{1,0:T(8,128)(2,1)}, f32[2,768]{1,0:T(2,128)}) custom-call(f32[576,768]{1,0:T(8,128)} %fusion.33.refs_0_, f32[576,768]{1,0:T(8,128)} %get-tuple-element.79.refs_1_, f32[2,768]{1,0:T(2,128)} %squeeze.26.refs_3_.refs_2_, ...), custom_call_target="tpu_custom_call" | custom-call | flops 17999998976 | bytes 10000000 | tf_op jit(solution)/shard_map/ff_backward/pallas_call | solution.py:355
  423.5 28.9 %attn_backward.3 = (f32[576,768]{1,0:T(8,128)}, bf16[2,384,768]{2,1,0:T(8,128)(2,1)}, bf16[2,384,768]{2,1,0:T(8,128)(2,1)}, bf16[576,768]{1,0:T(8,128)(2,1)}, f32[2,768]{1,0:T(2,128)}) custom-call(f32[576,768]{1,0:T(8,128)} %get-tuple-element.81.refs_0_, f32[576,768]{1,0:T(8,128)} %get-tuple-element.79.refs_1_, f32[2,768]{1,0:T(2,128)} %squeeze.26.refs_3_.refs_2_, ...), custom_call_target="tpu_custom_call" | custom-call | flops 30000001024 | bytes 10000000 | tf_op jit(solution)/shard_map/attn_backward/pallas_call | solution.py:421
  465.9 19.5 %ff_backward.4 = (f32[576,768]{1,0:T(8,128)}, bf16[2,384,1536]{2,1,0:T(8,128)(2,1)}, bf16[2,384,1536]{2,1,0:T(8,128)(2,1)}, bf16[576,768]{1,0:T(8,128)(2,1)}, f32[2,768]{1,0:T(2,128)}) custom-call(f32[576,768]{1,0:T(8,128)} %get-tuple-element.84.refs_0_, f32[576,768]{1,0:T(8,128)} %get-tuple-element.77.refs_0_.refs_5_.refs_1_, ...), custom_call_target="tpu_custom_call" | custom-call | flops 17999998976 | bytes 10000000 | tf_op jit(solution)/shard_map/ff_backward/pallas_call | solution.py:355
  485.5 10.4 %collective-permute-done.60 = bf16[1,2,2,2,96,768]{5,4,3,2,1,0:T(8,128)(2,1)S(1)} collective-permute-done((bf16[1,2,2,2,96,768]{5,4,3,2,1,0:T(8,128)(2,1)}, bf16[1,2,2,2,96,768]{5,4,3,2,1,0:T(8,128)(2,1)S(1)}, u32[]{:S(2)}, u32[]{:S(2)}) %collective-permute-start.60) | collective-permute-done | bytes 1179680 | tf_op jit(solution)/shard_map/ppermute | solution.py:38
  502.8 10.7 %collective-permute-done.61 = bf16[1,1,2,2,96,768]{5,4,3,2,1,0:T(8,128)(2,1)S(1)} collective-permute-done((bf16[1,1,2,2,96,768]{5,4,3,2,1,0:T(8,128)(2,1)}, bf16[1,1,2,2,96,768]{5,4,3,2,1,0:T(8,128)(2,1)S(1)}, u32[]{:S(2)}, u32[]{:S(2)}) %collective-permute-start.61) | collective-permute-done | bytes 589856 | tf_op jit(solution)/shard_map/ppermute | solution.py:38
  514.2 28.4 %attn_backward.4 = (f32[576,768]{1,0:T(8,128)}, bf16[2,384,768]{2,1,0:T(8,128)(2,1)}, bf16[2,384,768]{2,1,0:T(8,128)(2,1)}, bf16[576,768]{1,0:T(8,128)(2,1)}, f32[2,768]{1,0:T(2,128)}) custom-call(f32[576,768]{1,0:T(8,128)} %get-tuple-element.86.refs_0_, f32[576,768]{1,0:T(8,128)} %get-tuple-element.75.refs_0_.refs_5_.refs_1_, ...), custom_call_target="tpu_custom_call" | custom-call | flops 30000001024 | bytes 10000000 | tf_op jit(solution)/shard_map/attn_backward/pallas_call | solution.py:421
  543.9 18.1 %collective-permute-done.72 = bf16[2,1,2,2,96,1536]{5,4,3,2,1,0:T(8,128)(2,1)S(1)} collective-permute-done((bf16[2,1,2,2,96,1536]{5,4,3,2,1,0:T(8,128)(2,1)}, bf16[2,1,2,2,96,1536]{5,4,3,2,1,0:T(8,128)(2,1)S(1)}, u32[]{:S(2)}, u32[]{:S(2)}) %collective-permute-start.72) | collective-permute-done | bytes 2359328 | tf_op jit(solution)/shard_map/ppermute | solution.py:38
  568.2 17.6 %ff_backward.5 = (f32[576,768]{1,0:T(8,128)}, bf16[2,384,1536]{2,1,0:T(8,128)(2,1)}, bf16[2,384,1536]{2,1,0:T(8,128)(2,1)}, bf16[576,768]{1,0:T(8,128)(2,1)}, f32[2,768]{1,0:T(2,128)}) custom-call(f32[576,768]{1,0:T(8,128)} %get-tuple-element.89.refs_0_, f32[576,768]{1,0:T(8,128)} %get-tuple-element.73.refs_0_.refs_5_.refs_1_, ...), custom_call_target="tpu_custom_call" | custom-call | flops 17999998976 | bytes 10000000 | tf_op jit(solution)/shard_map/ff_backward/pallas_call | solution.py:355
  601.0 16.8 %collective-permute-done.74 = bf16[1,1,1,2,96,1536]{5,4,3,2,1,0:T(8,128)(2,1)S(1)} collective-permute-done((bf16[1,1,1,2,96,1536]{5,4,3,2,1,0:T(8,128)(2,1)S(1)}, bf16[1,1,1,2,96,1536]{5,4,3,2,1,0:T(8,128)(2,1)S(1)}, u32[]{:S(2)}, u32[]{:S(2)}) %collective-permute-start.74) | collective-permute-done | bytes 589856 | tf_op jit(solution)/shard_map/ppermute | solution.py:38
  620.2 29.2 %attn_backward.5 = (f32[576,768]{1,0:T(8,128)}, bf16[2,384,768]{2,1,0:T(8,128)(2,1)}, bf16[2,384,768]{2,1,0:T(8,128)(2,1)}, bf16[576,768]{1,0:T(8,128)(2,1)}, f32[2,768]{1,0:T(2,128)}) custom-call(f32[576,768]{1,0:T(8,128)} %get-tuple-element.91.refs_0_, f32[576,768]{1,0:T(8,128)} %get-tuple-element.71.refs_0_.refs_5_.refs_1_, ...), custom_call_target="tpu_custom_call" | custom-call | flops 30000001024 | bytes 10000000 | tf_op jit(solution)/shard_map/attn_backward/pallas_call | solution.py:421
  702.7 12.6 %collective-permute-done.70 = bf16[1,1,1,2,96,1536]{5,4,3,2,1,0:T(8,128)(2,1)S(1)} collective-permute-done((bf16[1,1,1,2,96,1536]{5,4,3,2,1,0:T(8,128)(2,1)S(1)}, bf16[1,1,1,2,96,1536]{5,4,3,2,1,0:T(8,128)(2,1)S(1)}, u32[]{:S(2)}, u32[]{:S(2)}) %collective-permute-start.70) | collective-permute-done | bytes 589856 | tf_op jit(solution)/shard_map/ppermute | solution.py:38
  750.8 16.6 %collective-permute-done.80 = bf16[1,1,1,2,96,768]{5,4,3,2,1,0:T(8,128)(2,1)} collective-permute-done((bf16[1,1,1,2,96,768]{5,4,3,2,1,0:T(8,128)(2,1)}, bf16[1,1,1,2,96,768]{5,4,3,2,1,0:T(8,128)(2,1)}, u32[]{:S(2)}, u32[]{:S(2)}) %collective-permute-start.80) | collective-permute-done | bytes 294944 | tf_op jit(solution)/shard_map/ppermute | solution.py:38
  769.2 10.7 %collective-permute-done.66 = bf16[1,1,1,2,96,1536]{5,4,3,2,1,0:T(8,128)(2,1)S(1)} collective-permute-done((bf16[1,1,1,2,96,1536]{5,4,3,2,1,0:T(8,128)(2,1)}, bf16[1,1,1,2,96,1536]{5,4,3,2,1,0:T(8,128)(2,1)S(1)}, u32[]{:S(2)}, u32[]{:S(2)}) %collective-permute-start.66) | collective-permute-done | bytes 589856 | tf_op jit(solution)/shard_map/ppermute | solution.py:38
  (653 shorter events, 414.1 us)
Async XLA Ops:
  5.5 51.6 %collective-permute-start.6 = (bf16[1,1,1,1,14,96]{5,4,3,2,1,0:T(8,128)(2,1)S(1)}, bf16[1,1,1,1,14,96]{5,4,3,2,1,0:T(8,128)(2,1)S(1)}, u32[]{:S(2)}, u32[]{:S(2)}) collective-permute-start(bf16[1,1,1,1,14,96]{5,4,3,2,1,0:T(8,128)(2,1)S(1)} %reshape_reshape.39), channel_id=1, source_target_pairs={{0,8},{4,12},{8,0},{12,4},{16,24},{20,28},{24,16},{28,20},{1,9},{5... | collective-permute-start | bytes 8072 | tf_op jit(solution)/shard_map/ppermute | solution.py:38
  8.5 48.7 %collective-permute-start.9 = (bf16[1,1,1,1,96,768]{4,5,3,2,1,0:T(8,128)(2,1)S(1)}, bf16[1,1,1,1,96,768]{4,5,3,2,1,0:T(8,128)(2,1)S(1)}, u32[]{:S(2)}, u32[]{:S(2)}) collective-permute-start(bf16[1,1,1,1,96,768]{4,5,3,2,1,0:T(8,128)(2,1)S(1)} %bitcast.240), channel_id=1, source_target_pairs={{0,8},{4,12},{8,0},{12,4},{16,24},{20,28},{24,16},{28,20},{1,9},{5... | collective-permute-start | bytes 442376 | tf_op jit(solution)/shard_map/ppermute | solution.py:38
  13.2 50.7 %collective-permute-start.14 = (bf16[1,1,1,1,96,1536]{5,4,3,2,1,0:T(8,128)(2,1)S(1)}, bf16[1,1,1,1,96,1536]{5,4,3,2,1,0:T(8,128)(2,1)}, u32[]{:S(2)}, u32[]{:S(2)}) collective-permute-start(bf16[1,1,1,1,96,1536]{5,4,3,2,1,0:T(8,128)(2,1)S(1)} %reshape_reshape.41), channel_id=1, source_target_pairs={{0,8},{4,12},{8,0},{12,4},{16,24},{20,28},{24,16},{28,20},{1,9},{5... | collective-permute-start | bytes 884744 | tf_op jit(solution)/shard_map/ppermute | solution.py:38
  17.5 107.5 %collective-permute-start.24 = (bf16[1,1,1,1,96,1536]{5,4,3,2,1,0:T(8,128)(2,1)}, bf16[1,1,1,1,96,1536]{5,4,3,2,1,0:T(8,128)(2,1)}, u32[]{:S(2)}, u32[]{:S(2)}) collective-permute-start(bf16[1,1,1,1,96,1536]{5,4,3,2,1,0:T(8,128)(2,1)} %reshape_reshape.43), channel_id=1, source_target_pairs={{0,8},{4,12},{8,0},{12,4},{16,24},{20,28},{24,16},{28,20},{1,9},{5... | collective-permute-start | bytes 884744 | tf_op jit(solution)/shard_map/ppermute | solution.py:38
  62.4 47.5 %collective-permute-start.8 = (bf16[1,1,2,2,14,96]{5,4,3,2,1,0:T(8,128)(2,1)}, bf16[1,1,2,2,14,96]{5,4,3,2,1,0:T(8,128)(2,1)}, u32[]{:S(2)}, u32[]{:S(2)}) collective-permute-start(bf16[1,1,2,2,14,96]{5,4,3,2,1,0:T(8,128)(2,1)} %pad_maximum_fusion.30), channel_id=1, source_target_pairs={{0,4},{4,0},{8,12},{12,8},{16,20},{20,16},{24,28},{28,24},{1,5},{5... | collective-permute-start | bytes 32264 | tf_op jit(solution)/shard_map/ppermute | solution.py:38
  65.6 38.2 %collective-permute-start.15 = (bf16[1,1,1,2,96,1536]{5,4,3,2,1,0:T(8,128)(2,1)}, bf16[1,1,1,2,96,1536]{5,4,3,2,1,0:T(8,128)(2,1)}, u32[]{:S(2)}, u32[]{:S(2)}) collective-permute-start(bf16[1,1,1,2,96,1536]{5,4,3,2,1,0:T(8,128)(2,1)} %constant_dynamic-update-slice_fusion.4), channel_id=1, source_target_pairs={{0,16},{4,20},{8,24},{12,28},{16,0},{20,4},{24,8},{28,12},{1,17},{... | collective-permute-start | bytes 1769480 | tf_op jit(solution)/shard_map/ppermute | solution.py:38
  117.4 42.1 %collective-permute-start.12 = (bf16[1,2,2,2,96,768]{5,4,3,2,1,0:T(8,128)(2,1)}, bf16[1,2,2,2,96,768]{5,4,3,2,1,0:T(8,128)(2,1)}, u32[]{:S(2)}, u32[]{:S(2)}) collective-permute-start(bf16[1,2,2,2,96,768]{5,4,3,2,1,0:T(8,128)(2,1)} %copy.274), channel_id=1, source_target_pairs={{0,2},{1,3},{2,0},{3,1},{4,6},{5,7},{6,4},{7,5},{8,10},{9,11},{10,... | collective-permute-start | bytes 3538952 | tf_op jit(solution)/shard_map/ppermute | solution.py:38
  121.5 55.7 %collective-permute-start.20 = (bf16[1,1,1,2,96,768]{4,5,3,2,1,0:T(8,128)(2,1)S(1)}, bf16[1,1,1,2,96,768]{4,5,3,2,1,0:T(8,128)(2,1)S(1)}, u32[]{:S(2)}, u32[]{:S(2)}) collective-permute-start(bf16[1,1,1,2,96,768]{4,5,3,2,1,0:T(8,128)(2,1)S(1)} %pad_maximum_fusion.20), channel_id=1, source_target_pairs={{0,16},{4,20},{8,24},{12,28},{16,0},{20,4},{24,8},{28,12},{1,17},{... | collective-permute-start | bytes 884744 | tf_op jit(solution)/shard_map/ppermute | solution.py:38
  126.0 58.4 %collective-permute-start.25 = (bf16[1,1,1,2,96,1536]{5,4,3,2,1,0:T(8,128)(2,1)S(1)}, bf16[1,1,1,2,96,1536]{5,4,3,2,1,0:T(8,128)(2,1)S(1)}, u32[]{:S(2)}, u32[]{:S(2)}) collective-permute-start(bf16[1,1,1,2,96,1536]{5,4,3,2,1,0:T(8,128)(2,1)S(1)} %constant_dynamic-update-slice_fusion.6), channel_id=1, source_target_pairs={{0,16},{4,20},{8,24},{12,28},{16,0},{20,4},{24,8},{28,12},{1,17},{... | collective-permute-start | bytes 1769480 | tf_op jit(solution)/shard_map/ppermute | solution.py:38
  138.6 64.2 %collective-permute-start.17 = (bf16[2,1,2,2,96,1536]{5,4,3,2,1,0:T(8,128)(2,1)}, bf16[2,1,2,2,96,1536]{5,4,3,2,1,0:T(8,128)(2,1)}, u32[]{:S(2)}, u32[]{:S(2)}) collective-permute-start(bf16[2,1,2,2,96,1536]{5,4,3,2,1,0:T(8,128)(2,1)} %pad_maximum_fusion), channel_id=1, source_target_pairs={{0,4},{4,0},{8,12},{12,8},{16,20},{20,16},{24,28},{28,24},{1,5},{5... | collective-permute-start | bytes 7077896 | tf_op jit(solution)/shard_map/ppermute | solution.py:38
  202.3 47.0 %collective-permute-start.22 = (bf16[2,1,2,2,96,768]{5,4,3,2,1,0:T(8,128)(2,1)}, bf16[2,1,2,2,96,768]{5,4,3,2,1,0:T(8,128)(2,1)}, u32[]{:S(2)}, u32[]{:S(2)}) collective-permute-start(bf16[2,1,2,2,96,768]{5,4,3,2,1,0:T(8,128)(2,1)} %copy.282), channel_id=1, source_target_pairs={{0,4},{4,0},{8,12},{12,8},{16,20},{20,16},{24,28},{28,24},{1,5},{5... | collective-permute-start | bytes 3538952 | tf_op jit(solution)/shard_map/ppermute | solution.py:38
  214.0 35.3 %collective-permute-start.18 = (bf16[576,768]{1,0:T(8,128)(2,1)}, bf16[576,768]{1,0:T(8,128)(2,1)}, u32[]{:S(2)}, u32[]{:S(2)}) collective-permute-start(bf16[576,768]{1,0:T(8,128)(2,1)} %get-tuple-element.72.refs_1_), channel_id=1, source_target_pairs={{0,1},{1,0},{2,3},{3,2},{4,5},{5,4},{6,7},{7,6},{8,9},{9,8},{10,11... | collective-permute-start | bytes 2654216 | tf_op jit(solution)/shard_map/ppermute | solution.py:38
  217.5 49.6 %collective-permute-start.30 = (bf16[1,1,1,2,96,768]{4,5,3,2,1,0:T(8,128)(2,1)}, bf16[1,1,1,2,96,768]{4,5,3,2,1,0:T(8,128)(2,1)}, u32[]{:S(2)}, u32[]{:S(2)}) collective-permute-start(bf16[1,1,1,2,96,768]{4,5,3,2,1,0:T(8,128)(2,1)} %pad_maximum_fusion.22), channel_id=1, source_target_pairs={{0,16},{4,20},{8,24},{12,28},{16,0},{20,4},{24,8},{28,12},{1,17},{... | collective-permute-start | bytes 884744 | tf_op jit(solution)/shard_map/ppermute | solution.py:38
  218.5 52.3 %collective-permute-start.35 = (bf16[1,1,1,2,96,1536]{5,4,3,2,1,0:T(8,128)(2,1)S(1)}, bf16[1,1,1,2,96,1536]{5,4,3,2,1,0:T(8,128)(2,1)}, u32[]{:S(2)}, u32[]{:S(2)}) collective-permute-start(bf16[1,1,1,2,96,1536]{5,4,3,2,1,0:T(8,128)(2,1)S(1)} %constant_dynamic-update-slice_fusion.8), channel_id=1, source_target_pairs={{0,16},{4,20},{8,24},{12,28},{16,0},{20,4},{24,8},{28,12},{1,17},{... | collective-permute-start | bytes 1769480 | tf_op jit(solution)/shard_map/ppermute | solution.py:38
  228.4 62.0 %collective-permute-start.27 = (bf16[1,2,2,2,96,1536]{5,4,3,2,1,0:T(8,128)(2,1)}, bf16[1,2,2,2,96,1536]{5,4,3,2,1,0:T(8,128)(2,1)}, u32[]{:S(2)}, u32[]{:S(2)}) collective-permute-start(bf16[1,2,2,2,96,1536]{5,4,3,2,1,0:T(8,128)(2,1)} %pad_maximum_fusion.1), channel_id=1, source_target_pairs={{0,2},{1,3},{2,0},{3,1},{4,6},{5,7},{6,4},{7,5},{8,10},{9,11},{10,... | collective-permute-start | bytes 7077896 | tf_op jit(solution)/shard_map/ppermute | solution.py:38
  288.9 40.9 %collective-permute-start.32 = (bf16[1,2,2,2,96,768]{5,4,3,2,1,0:T(8,128)(2,1)}, bf16[1,2,2,2,96,768]{5,4,3,2,1,0:T(8,128)(2,1)S(1)}, u32[]{:S(2)}, u32[]{:S(2)}) collective-permute-start(bf16[1,2,2,2,96,768]{5,4,3,2,1,0:T(8,128)(2,1)} %copy.288), channel_id=1, source_target_pairs={{0,2},{1,3},{2,0},{3,1},{4,6},{5,7},{6,4},{7,5},{8,10},{9,11},{10,... | collective-permute-start | bytes 3538952 | tf_op jit(solution)/shard_map/ppermute | solution.py:38
  310.7 49.4 %collective-permute-start.37 = (bf16[2,1,2,2,96,1536]{5,4,3,2,1,0:T(8,128)(2,1)}, bf16[2,1,2,2,96,1536]{5,4,3,2,1,0:T(8,128)(2,1)}, u32[]{:S(2)}, u32[]{:S(2)}) collective-permute-start(bf16[2,1,2,2,96,1536]{5,4,3,2,1,0:T(8,128)(2,1)} %pad_maximum_fusion.2), channel_id=1, source_target_pairs={{0,4},{4,0},{8,12},{12,8},{16,20},{20,16},{24,28},{28,24},{1,5},{5... | collective-permute-start | bytes 7077896 | tf_op jit(solution)/shard_map/ppermute | solution.py:38
  499.7 62.3 %collective-permute-start.72 = (bf16[2,1,2,2,96,1536]{5,4,3,2,1,0:T(8,128)(2,1)}, bf16[2,1,2,2,96,1536]{5,4,3,2,1,0:T(8,128)(2,1)S(1)}, u32[]{:S(2)}, u32[]{:S(2)}) collective-permute-start(bf16[2,1,2,2,96,1536]{5,4,3,2,1,0:T(8,128)(2,1)} %bitcast.297), channel_id=1, source_target_pairs={{0,4},{4,0},{8,12},{12,8},{16,20},{20,16},{24,28},{28,24},{1,5},{5... | collective-permute-start | bytes 7077896 | tf_op jit(solution)/shard_map/ppermute | solution.py:38
  502.2 92.7 %collective-permute-start.68 = (bf16[1,2,2,2,96,1536]{5,4,3,2,1,0:T(8,128)(2,1)}, bf16[1,2,2,2,96,1536]{5,4,3,2,1,0:T(8,128)(2,1)}, u32[]{:S(2)}, u32[]{:S(2)}) collective-permute-start(bf16[1,2,2,2,96,1536]{5,4,3,2,1,0:T(8,128)(2,1)} %bitcast.298), channel_id=1, source_target_pairs={{0,2},{1,3},{2,0},{3,1},{4,6},{5,7},{6,4},{7,5},{8,10},{9,11},{10,... | collective-permute-start | bytes 7077896 | tf_op jit(solution)/shard_map/ppermute | solution.py:38
  585.9 112.5 %collective-permute-start.64 = (bf16[2,1,2,2,96,1536]{5,4,3,2,1,0:T(8,128)(2,1)}, bf16[2,1,2,2,96,1536]{5,4,3,2,1,0:T(8,128)(2,1)}, u32[]{:S(2)}, u32[]{:S(2)}) collective-permute-start(bf16[2,1,2,2,96,1536]{5,4,3,2,1,0:T(8,128)(2,1)} %bitcast.296), channel_id=1, source_target_pairs={{0,4},{4,0},{8,12},{12,8},{16,20},{20,16},{24,28},{28,24},{1,5},{5... | collective-permute-start | bytes 7077896 | tf_op jit(solution)/shard_map/ppermute | solution.py:38
  598.5 89.0 %collective-permute-start.69 = (bf16[1,1,2,2,96,1536]{5,4,3,2,1,0:T(8,128)(2,1)}, bf16[1,1,2,2,96,1536]{5,4,3,2,1,0:T(8,128)(2,1)}, u32[]{:S(2)}, u32[]{:S(2)}) collective-permute-start(bf16[1,1,2,2,96,1536]{5,4,3,2,1,0:T(8,128)(2,1)} %slice.495), channel_id=1, source_target_pairs={{0,4},{4,0},{8,12},{12,8},{16,20},{20,16},{24,28},{28,24},{1,5},{5... | collective-permute-start | bytes 3538952 | tf_op jit(solution)/shard_map/ppermute | solution.py:38
  649.5 45.4 %collective-permute-start.52 = (bf16[1,2,2,2,96,768]{5,4,3,2,1,0:T(8,128)(2,1)}, bf16[1,2,2,2,96,768]{5,4,3,2,1,0:T(8,128)(2,1)}, u32[]{:S(2)}, u32[]{:S(2)}) collective-permute-start(bf16[1,2,2,2,96,768]{5,4,3,2,1,0:T(8,128)(2,1)} %bitcast.301), channel_id=1, source_target_pairs={{0,2},{1,3},{2,0},{3,1},{4,6},{5,7},{6,4},{7,5},{8,10},{9,11},{10,... | collective-permute-start | bytes 3538952 | tf_op jit(solution)/shard_map/ppermute | solution.py:38
  701.8 39.3 %collective-permute-start.65 = (bf16[1,1,2,2,96,1536]{5,4,3,2,1,0:T(8,128)(2,1)}, bf16[1,1,2,2,96,1536]{5,4,3,2,1,0:T(8,128)(2,1)}, u32[]{:S(2)}, u32[]{:S(2)}) collective-permute-start(bf16[1,1,2,2,96,1536]{5,4,3,2,1,0:T(8,128)(2,1)} %slice.489), channel_id=1, source_target_pairs={{0,2},{1,3},{2,0},{3,1},{4,6},{5,7},{6,4},{7,5},{8,10},{9,11},{10,... | collective-permute-start | bytes 3538952 | tf_op jit(solution)/shard_map/ppermute | solution.py:38
  743.5 36.4 %collective-permute-start.66 = (bf16[1,1,1,2,96,1536]{5,4,3,2,1,0:T(8,128)(2,1)}, bf16[1,1,1,2,96,1536]{5,4,3,2,1,0:T(8,128)(2,1)S(1)}, u32[]{:S(2)}, u32[]{:S(2)}) collective-permute-start(bf16[1,1,1,2,96,1536]{5,4,3,2,1,0:T(8,128)(2,1)} %slice.491), channel_id=1, source_target_pairs={{0,16},{4,20},{8,24},{12,28},{16,0},{20,4},{24,8},{28,12},{1,17},{... | collective-permute-start | bytes 1769480 | tf_op jit(solution)/shard_map/ppermute | solution.py:38
  (178 other events, 2247.0 us)

commit v3 on v2

v3 whole, which is shorter than its diff:
```python
import functools

import jax
import jax.numpy as jnp
from jax import lax
from jax.experimental import pallas as pl
from jax.experimental.pallas import tpu as pltpu
from jax.sharding import PartitionSpec as P

HEAD_DIM = 64
LAYERS = 3
STEP = 10
MOST = 576
FF_BLOCK = 256

EPSILON = 1e-06
MASKED = -30000.0
CLIP = 0.005
BETA_ONE = 0.9
BETA_TWO = 0.999
ADAM_EPS = 1e-08
RATES = (0.02, 0.06, 0.02, 0.02, 0.02, 0.02, 0.5)
DECAYS = (0.05, 0.05, 0.05, 0.05, 0.05, 0.05, 0.0)
SQRT_HALF = 0.7071067811865476
INV_ROOT = 0.3989422804014327
HIGH = lax.Precision.HIGHEST
BF = jnp.bfloat16
F32 = jnp.float32

AXES = ("dp", "mp")
INNER = ("mp", 1)
OUTER = ("mp", 2)
LOW = ("dp", 1)
FIRST = (LOW, OUTER)
SECOND = (OUTER, LOW)


def swap(value, bit):
    n_dp, n_mp = (lax.axis_size(axis) for axis in AXES)
    pairs = []
    for dp in range(n_dp):
        for mp in range(n_mp):
            axis, mask = bit if isinstance(bit[0], str) else bit[mp % 2]
            to = (dp ^ mask) * n_mp + mp if axis == "dp" else dp * n_mp + (mp ^ mask)
            pairs.append((dp * n_mp + mp, to))
    return lax.ppermute(value, AXES, pairs)


class Steps:
    def __init__(self):
        self.before = []
        self.made = []

    def next(self):
        self.before, self.made = self.made, []

    def tie(self, value):
        if not self.before:
            return value
        return lax.optimization_barrier((value, *self.before))[0]

    def add(self, value):
        self.made.append(value)
        return value

    def swap(self, value, bit):
        return self.add(swap(self.tie(value), bit))


def dp_bits():
    size = lax.axis_size("dp")
    bits = []
    mask = 1
    while mask < size:
        bits.append(("dp", mask))
        mask *= 2
    return bits


def both(part):
    return part + swap(part.astype(BF), INNER).astype(F32)


def dot(left, right, contract):
    return lax.dot_general(left, right, ((contract[0:1], contract[1:2]), ((), ())), preferred_element_type=F32)


def nn(left, right):
    return dot(left, right, (1, 0))


def nt(left, right):
    return dot(left, right, (1, 1))


def tn(left, right):
    return dot(left, right, (0, 0))


def norm_stats(value):
    centred = value - jnp.mean(value, -1, keepdims=True)
    variance = jnp.mean(centred * centred, -1, keepdims=True)
    rstd = lax.rsqrt(variance + EPSILON)
    return centred * rstd, rstd


def layer_norm(value, norm):
    return norm_stats(value)[0] * norm[0:1] + norm[1:2]


def norm_back(value, norm, d_out):
    hat, rstd = norm_stats(value)
    d_hat = d_out * norm[0:1]
    d_value = rstd * (
        d_hat - jnp.mean(d_hat, -1, keepdims=True) - hat * jnp.mean(d_hat * hat, -1, keepdims=True)
    )
    return d_value, jnp.concatenate([jnp.sum(d_out * hat, 0, keepdims=True), jnp.sum(d_out, 0, keepdims=True)], 0)


def load_weight(w, flag, own, near, across, both_ways):
    outer = pl.program_id(0) % 2
    rows = w.shape[0] // 2

    @pl.when(outer == 0)
    def _():
        w[:rows] = own[...]

    @pl.when(outer == 1)
    def _():
        w[rows:] = both_ways[...]

    @pl.when((outer == 0) & (flag[0] == 0))
    def _():
        w[rows:] = across[...]

    @pl.when((outer == 0) & (flag[0] == 1))
    def _():
        w[rows:] = near[...]

    @pl.when((outer == 1) & (flag[0] == 0))
    def _():
        w[:rows] = near[...]

    @pl.when((outer == 1) & (flag[0] == 1))
    def _():
        w[:rows] = across[...]


def store_grad(parts, flag, own, near, across, both_ways):
    outer = pl.program_id(0) % 2

    def put(target, top):
        at = 0
        for part in parts:
            rows = part.shape[0] // 2
            value = part[:rows] if top else part[rows:]
            target[:, at : at + part.shape[1]] = value.astype(BF)
            at += part.shape[1]

    @pl.when(outer == 0)
    def _():
        put(own, True)

    @pl.when(outer == 1)
    def _():
        put(both_ways, False)

    @pl.when((outer == 0) & (flag[0] == 0))
    def _():
        put(across, False)

    @pl.when((outer == 0) & (flag[0] == 1))
    def _():
        put(near, False)

    @pl.when((outer == 1) & (flag[0] == 0))
    def _():
        put(near, True)

    @pl.when((outer == 1) & (flag[0] == 1))
    def _():
        put(across, True)


def quarter_specs(weight, columns):
    steps = 2 * (weight.shape[1] // columns)
    return steps, [pl.BlockSpec((weight.shape[0], columns), lambda i: (0, i // 2))] * 4


def full(value):
    return pl.BlockSpec(value.shape, lambda i: (0,) * len(value.shape))


def spec_of(shape):
    return pl.BlockSpec(shape, lambda i: (0,) * len(shape))


FLAG = pl.BlockSpec(memory_space=pltpu.SMEM)
NO_COST = pl.CostEstimate(flops=10**6, bytes_accessed=10**4, transcendentals=0)


def params():
    return pltpu.CompilerParams(dimension_semantics=("arbitrary",), vmem_limit_bytes=56 * 1024 * 1024)


def masked_probs(scaled_query, key, keep):
    scores = jnp.where(keep, nt(scaled_query, key), MASKED)
    weight = jnp.exp(scores - jnp.max(scores, -1, keepdims=True))
    return weight * (1.0 / jnp.sum(weight, -1, keepdims=True))


def attn_fwd_kernel(count, *refs):
    flag = refs[0]
    adds = refs[1 : count + 1]
    norm, segq, segk, *weight, x_ref, mix_ref, part_ref, normed, w, acc = refs[count + 1 :]
    step = pl.program_id(0)

    @pl.when(step == 0)
    def _():
        x = adds[0][...]
        for other in adds[1:]:
            x = x + other[...].astype(F32)
        x_ref[...] = x
        normed[...] = layer_norm(x, norm[...]).astype(BF)
        acc[...] = jnp.zeros_like(acc)

    load_weight(w, flag, *weight)
    mixed = nn(normed[...], w[...]).astype(BF)
    c = HEAD_DIM
    keep = segq[...] == segk[...]
    probs = masked_probs(mixed[:, :c] * HEAD_DIM ** (-0.5), mixed[:, c : 2 * c], keep)
    out = nn(probs.astype(BF), mixed[:, 2 * c : 3 * c]).astype(BF)
    mix_ref[0] = jnp.concatenate([mixed[:, : 3 * c], out], 1)
    acc[...] += nt(out, w[:, 3 * c :])

    @pl.when(step == pl.num_programs(0) - 1)
    def _():
        part_ref[...] = acc[...].astype(BF)


def attn_forward(adds, norm, segq, segk, pieces, flag):
    tokens, width = adds[0].shape
    columns = 4 * HEAD_DIM
    steps, quarters = quarter_specs(pieces[0], columns)
    return pl.pallas_call(
        functools.partial(attn_fwd_kernel, len(adds)),
        grid=(steps,),
        in_specs=[FLAG] + [full(v) for v in adds] + [full(norm), full(segq), full(segk)] + quarters,
        out_specs=[
            spec_of((tokens, width)),
            pl.BlockSpec((1, tokens, columns), lambda i: (i, 0, 0)),
            spec_of((tokens, width)),
        ],
        out_shape=[
            jax.ShapeDtypeStruct((tokens, width), F32),
            jax.ShapeDtypeStruct((steps, tokens, columns), BF),
            jax.ShapeDtypeStruct((tokens, width), BF),
        ],
        scratch_shapes=[
            pltpu.VMEM((tokens, width), BF),
            pltpu.VMEM((width, columns), BF),
            pltpu.VMEM((tokens, width), F32),
        ],
        compiler_params=params(),
        cost_estimate=NO_COST,
        name="attn_forward",
    )(flag, *adds, norm, segq, segk, *pieces)


def ff_fwd_kernel(count, *refs):
    flag = refs[0]
    adds = refs[1 : count + 1]
    norm, *weight, x_ref, part_ref, normed, w, acc = refs[count + 1 :]
    step = pl.program_id(0)

    @pl.when(step == 0)
    def _():
        x = adds[0][...]
        for other in adds[1:]:
            x = x + other[...].astype(F32)
        x_ref[...] = x
        normed[...] = layer_norm(x, norm[...]).astype(BF)
        acc[...] = jnp.zeros_like(acc)

    load_weight(w, flag, *weight)
    columns = w.shape[1] // 2
    up = nn(normed[...], w[:, :columns])
    active = (0.5 * up * (1.0 + lax.erf(up * SQRT_HALF))).astype(BF)
    acc[...] += nt(active, w[:, columns:])

    @pl.when(step == pl.num_programs(0) - 1)
    def _():
        part_ref[...] = acc[...].astype(BF)


def ff_forward(adds, norm, pieces, flag):
    tokens, width = adds[0].shape
    columns = FF_BLOCK * 2
    steps, quarters = quarter_specs(pieces[0], columns)
    return pl.pallas_call(
        functools.partial(ff_fwd_kernel, len(adds)),
        grid=(steps,),
        in_specs=[FLAG] + [full(v) for v in adds] + [full(norm)] + quarters,
        out_specs=[spec_of((tokens, width)), spec_of((tokens, width))],
        out_shape=[
            jax.ShapeDtypeStruct((tokens, width), F32),
            jax.ShapeDtypeStruct((tokens, width), BF),
        ],
        scratch_shapes=[
            pltpu.VMEM((tokens, width), BF),
            pltpu.VMEM((width, columns), BF),
            pltpu.VMEM((tokens, width), F32),
        ],
        compiler_params=params(),
        cost_estimate=NO_COST,
        name="ff_forward",
    )(flag, *adds, norm, *pieces)


def back_prologue(back, d_ref, g_ref):
    d_base = back[0][...]
    if len(back) == 1:
        d_ref[...] = d_base
        return d_base
    value, norm, own, other = back[1:]
    d_value, g_ref[...] = norm_back(value[...], norm[...], own[...].astype(F32) + other[...].astype(F32))
    d_all = d_base + d_value
    d_ref[...] = d_all
    return d_all


def ff_back_kernel(count, *refs):
    flag = refs[0]
    back = refs[1 : count + 1]
    value, norm = refs[count + 1 : count + 3]
    weight, d_ref, grad = refs[count + 3 : count + 7], refs[count + 7], refs[count + 8 : count + 12]
    part_ref, g_ref, normed, normed_t, dz, dz_t, w, acc = refs[count + 12 :]
    step = pl.program_id(0)

    @pl.when(step == 0)
    def _():
        d_all = back_prologue(back, d_ref, g_ref)
        dz[...] = d_all.astype(BF)
        dz_t[...] = d_all.T.astype(BF)
        here = layer_norm(value[...], norm[...])
        normed[...] = here.astype(BF)
        normed_t[...] = here.T.astype(BF)
        acc[...] = jnp.zeros_like(acc)

    load_weight(w, flag, *weight)
    columns = w.shape[1] // 2
    up = nn(normed[...], w[:, :columns])
    phi = 0.5 * (1.0 + lax.erf(up * SQRT_HALF))
    active = (up * phi).astype(BF)
    slope = phi + up * jnp.exp(-0.5 * up * up) * INV_ROOT
    d_up = (nn(dz[...], w[:, columns:]) * slope).astype(BF)
    acc[...] += nt(d_up, w[:, :columns])
    store_grad([nn(normed_t[...], d_up), nn(dz_t[...], active)], flag, *grad)

    @pl.when(step == pl.num_programs(0) - 1)
    def _():
        part_ref[...] = acc[...].astype(BF)


def back_out(tokens, width, pieces, quarters):
    specs = [spec_of((tokens, width))] + quarters + [spec_of((tokens, width)), spec_of((2, width))]
    shapes = [
        jax.ShapeDtypeStruct((tokens, width), F32),
        *[jax.ShapeDtypeStruct(piece.shape, BF) for piece in pieces],
        jax.ShapeDtypeStruct((tokens, width), BF),
        jax.ShapeDtypeStruct((2, width), F32),
    ]
    return specs, shapes


def ff_backward(back, value, norm, pieces, flag):
    tokens, width = value.shape
    columns = FF_BLOCK * 2
    steps, quarters = quarter_specs(pieces[0], columns)
    specs, shapes = back_out(tokens, width, pieces, quarters)
    return pl.pallas_call(
        functools.partial(ff_back_kernel, len(back)),
        grid=(steps,),
        in_specs=[FLAG] + [full(v) for v in back] + [full(value), full(norm)] + quarters,
        out_specs=specs,
        out_shape=shapes,
        scratch_shapes=[
            pltpu.VMEM((tokens, width), BF),
            pltpu.VMEM((width, tokens), BF),
            pltpu.VMEM((tokens, width), BF),
            pltpu.VMEM((width, tokens), BF),
            pltpu.VMEM((width, columns), BF),
            pltpu.VMEM((tokens, width), F32),
        ],
        compiler_params=params(),
        cost_estimate=NO_COST,
        name="ff_backward",
    )(flag, *back, value, norm, *pieces)


def attn_back_kernel(count, *refs):
    flag = refs[0]
    back = refs[1 : count + 1]
    value, norm, segq, segk, mix_ref = refs[count + 1 : count + 6]
    weight, d_ref, grad = refs[count + 6 : count + 10], refs[count + 10], refs[count + 11 : count + 15]
    part_ref, g_ref, normed_t, dy, dy_t, w, acc = refs[count + 15 :]
    step = pl.program_id(0)

    @pl.when(step == 0)
    def _():
        d_all = back_prologue(back, d_ref, g_ref)
        dy[...] = d_all.astype(BF)
        dy_t[...] = d_all.T.astype(BF)
        normed_t[...] = layer_norm(value[...], norm[...]).T.astype(BF)
        acc[...] = jnp.zeros_like(acc)

    load_weight(w, flag, *weight)
    c = HEAD_DIM
    scale = HEAD_DIM ** (-0.5)
    query, key, val = (mix_ref[0, :, j * c : (j + 1) * c] for j in range(3))
    query = query * scale
    d_out = nn(dy[...], w[:, 3 * c :]).astype(BF)
    keep = segq[...] == segk[...]
    probs = masked_probs(query, key, keep)
    d_probs = nt(d_out, val)
    delta = jnp.sum(probs * d_probs, -1, keepdims=True)
    d_scores = jnp.where(keep, probs * (d_probs - delta), 0.0).astype(BF)
    d_query = (nn(d_scores, key) * scale).astype(BF)
    d_key = tn(d_scores, query).astype(BF)
    d_val = tn(probs.astype(BF), d_out).astype(BF)
    d_left = jnp.concatenate([d_query, d_key], 1)
    zero = jnp.zeros_like(d_val)
    d_right = jnp.concatenate([d_val, zero], 1)
    out = jnp.concatenate([zero, mix_ref[0, :, 3 * c :]], 1)
    acc[...] += nt(d_left, w[:, : 2 * c]) + nt(d_right, w[:, 2 * c :])
    left = nn(normed_t[...], d_left)
    right = nn(normed_t[...], d_right) + nn(dy_t[...], out)
    store_grad([left, right], flag, *grad)

    @pl.when(step == pl.num_programs(0) - 1)
    def _():
        part_ref[...] = acc[...].astype(BF)


def attn_backward(back, value, norm, segq, segk, mix, pieces, flag):
    tokens, width = value.shape
    columns = 4 * HEAD_DIM
    steps, quarters = quarter_specs(pieces[0], columns)
    specs, shapes = back_out(tokens, width, pieces, quarters)
    return pl.pallas_call(
        functools.partial(attn_back_kernel, len(back)),
        grid=(steps,),
        in_specs=[FLAG] + [full(v) for v in back]
        + [full(value), full(norm), full(segq), full(segk)]
        + [pl.BlockSpec((1, tokens, columns), lambda i: (i, 0, 0))]
        + quarters,
        out_specs=specs,
        out_shape=shapes,
        scratch_shapes=[
            pltpu.VMEM((width, tokens), BF),
            pltpu.VMEM((tokens, width), BF),
            pltpu.VMEM((width, tokens), BF),
            pltpu.VMEM((width, columns), BF),
            pltpu.VMEM((tokens, width), F32),
        ],
        compiler_params=params(),
        cost_estimate=NO_COST,
        name="attn_backward",
    )(flag, *back, value, norm, segq, segk, mix, *pieces)


def last_kernel(base, value, norm, own, other, d_ref, g_ref):
    d_value, g_ref[...] = norm_back(value[...], norm[...], own[...].astype(F32) + other[...].astype(F32))
    d_ref[...] = (base[...] + d_value).astype(BF)


def input_gradient(back):
    tokens, width = back[0].shape
    return pl.pallas_call(
        last_kernel,
        grid=(1,),
        in_specs=[full(v) for v in back],
        out_specs=[spec_of((tokens, width)), spec_of((2, width))],
        out_shape=[
            jax.ShapeDtypeStruct((tokens, width), BF),
            jax.ShapeDtypeStruct((2, width), F32),
        ],
        compiler_params=params(),
        cost_estimate=NO_COST,
        name="input_gradient",
    )(*back)


def finish_kernel(token, *refs):
    a_keep, a_got, f_keep, f_got, into, out, up, down, square = refs
    c = HEAD_DIM
    g = a_keep[...].astype(F32) + a_got[...].astype(F32)
    total = jnp.sum(g * g, 0, keepdims=True).sum(1, keepdims=True)
    heads = g.shape[1] // (4 * c)
    parts = [[g[:, (4 * h + j) * c : (4 * h + j + 1) * c] for h in range(heads)] for j in range(4)]
    for j in range(3):
        into[j] = jnp.concatenate(parts[j], 1)
    out[...] = jnp.concatenate(parts[3], 1).T
    g = f_keep[...].astype(F32) + f_got[...].astype(F32)
    total = total + jnp.sum(g * g, 0, keepdims=True).sum(1, keepdims=True)
    for i in range(g.shape[1] // (2 * FF_BLOCK)):
        here = slice(i * FF_BLOCK, (i + 1) * FF_BLOCK)
        up[:, here] = g[:, 2 * i * FF_BLOCK : (2 * i + 1) * FF_BLOCK]
        down[here] = g[:, (2 * i + 1) * FF_BLOCK : (2 * i + 2) * FF_BLOCK].T
    square[...] = total


def finish(a_pair, f_pair, token):
    rows, width = a_pair[0].shape
    hidden = f_pair[0].shape[1] // 2
    values = (*a_pair, *f_pair)
    outs = [(3, rows, width // 4), (width // 4, rows), (rows, hidden), (hidden, rows), (1, 1)]
    return pl.pallas_call(
        finish_kernel,
        grid=(1,),
        in_specs=[pl.BlockSpec(memory_space=pl.ANY)] + [full(v) for v in values],
        out_specs=[spec_of(o) for o in outs],
        out_shape=[jax.ShapeDtypeStruct(o, F32) for o in outs],
        compiler_params=params(),
        cost_estimate=NO_COST,
        name="finish",
    )(token, *values)


def adam(weight, grad, first, second, rate, decay):
    first = BETA_ONE * first + (1.0 - BETA_ONE) * grad
    second = BETA_TWO * second + (1.0 - BETA_TWO) * grad * grad
    update = first / (1.0 - BETA_ONE**STEP) / (jnp.sqrt(second / (1.0 - BETA_TWO**STEP)) + ADAM_EPS)
    return (first, second, weight - rate * (update + decay * weight))


def body(pixels, lengths, valid_mask, teacher_logits, teacher_map, *state):
    masters, firsts, seconds = state[:7], state[7:14], state[14:]
    attend_in, attend_out, hidden_up, hidden_down, patch_embed, class_head, norm_params = masters
    bits = dp_bits()
    low, high = bits[0], bits[1:]
    steps = Steps()
    rows = patch_embed.shape[1]
    inner = lax.axis_index("mp") % 2
    outer = lax.axis_index("mp") // 2
    images = lengths.shape[1]
    tokens = pixels.shape[0]
    total_images = images * lax.axis_size("dp")

    heads = attend_in.shape[3] // HEAD_DIM
    hidden = hidden_up.shape[2]
    width = attend_out.shape[2] * lax.axis_size("dp")

    def attn_unit(l):
        into = attend_in[l].astype(BF).reshape(3, rows, heads, HEAD_DIM)
        out = attend_out[l].T.astype(BF).reshape(1, rows, heads, HEAD_DIM)
        return jnp.concatenate([into, out], 0).transpose(1, 2, 0, 3).reshape(rows, -1)

    def ff_unit(l):
        up = hidden_up[l].astype(BF).reshape(rows, -1, 1, FF_BLOCK)
        down = hidden_down[l].T.astype(BF).reshape(rows, -1, 1, FF_BLOCK)
        return jnp.concatenate([up, down], 2).reshape(rows, -1)

    half = class_head.shape[1] // 2
    head_unit = lax.dynamic_slice_in_dim(class_head.astype(BF), inner * half, half, 1)

    flag = inner.reshape(1)

    def over(unit, bits):
        for bit in bits:
            unit = jnp.stack([unit, steps.swap(unit, bit)])
        return unit

    def over_high(unit):
        if len(high) != 2:
            return over(unit, high)
        (axis, a), (_, b) = high
        return jnp.stack([unit] + [steps.swap(unit, (axis, mask)) for mask in (a, b, a | b)])

    def near(own):
        return [own, steps.swap(own, SECOND), steps.swap(own, FIRST)]

    def across(held):
        return held + [steps.swap(held[1], FIRST)]

    def far(unit):
        unit = over_high(unit)
        return unit.reshape(-1, unit.shape[-1])

    row = lengths[0]
    ends = jnp.cumsum(row)
    longest = jnp.argmax(row)
    start = ends[longest] - row[longest]
    place = jnp.arange(MOST, dtype=jnp.int32)

    def mine(value, which):
        twice = jnp.concatenate([value, value], 0)
        return lax.dynamic_slice_in_dim(twice, start + MOST * which, MOST, 0)

    pix = [mine(pixels, outer), mine(pixels, 1 - outer)]
    held = jnp.where(outer == 0, MOST, tokens - MOST)
    position = (start + MOST * outer + place) % tokens
    segment = jnp.sum((position[:, None] >= ends[None, :]).astype(jnp.int32), 1)
    valid = jnp.where(place < held, mine(valid_mask, outer), 0) > 0
    segq = segment[:, None]
    segk = jnp.where(valid, segment, -1)[None, :]
    image_ids = jnp.arange(images, dtype=jnp.int32)
    member = ((segment[None, :] == image_ids[:, None]) & valid[None, :]).astype(F32)
    owned = ((image_ids == longest) == (outer == 0)).astype(F32)[:, None]
    count = jnp.sum(member, 1)

    mid = width // 2

    def of_inner(value, which):
        return jnp.where(which == 0, value[..., :mid], value[..., mid:])

    def halves(own, other):
        return jnp.where(inner == 0, jnp.concatenate([own, other], 1), jnp.concatenate([other, own], 1))

    dp_order = high + [low]
    teach = jax.nn.log_softmax(teacher_logits, -1)
    teach = lax.dynamic_slice_in_dim(teach, inner * half, half, 1)
    attn = [attn_unit(l) for l in range(LAYERS)]
    ff = [ff_unit(l) for l in range(LAYERS)]

    one, two = high[:1], high[1:]

    def flat(unit):
        return unit.reshape(-1, unit.shape[-1])

    for unit in attn + ff + [head_unit]:
        steps.add(unit)
    pixel_count = patch_embed.shape[0]
    patch = jnp.concatenate([patch_embed.astype(BF), norm_params.astype(BF).reshape(-1, rows)], 0).T
    patch = far(patch)
    attn[0] = over(attn[0], one)
    steps.next()
    attn[0] = flat(over(attn[0], two))
    ff[0] = over(ff[0], one)
    patch = over(patch, [low]).reshape(width, -1)
    steps.next()
    ff[0] = flat(over(ff[0], two))
    attn[1] = over(attn[1], one)
    attn[0] = near(attn[0])
    patch = steps.tie(patch)
    norms = patch[:, pixel_count:].T.astype(F32).reshape(7, 2, width)
    part = nt(jnp.concatenate(pix, 0), patch[:, :pixel_count]).astype(BF)
    part = of_inner(part, inner).astype(F32) + swap(of_inner(part, 1 - inner), INNER).astype(F32)
    part, theirs = part[:MOST], steps.add(part[MOST:].astype(BF))
    steps.next()
    part = part + steps.swap(theirs, OUTER).astype(F32)
    attn[0] = across(attn[0])
    ff[0] = near(ff[0])
    attn[1] = flat(over(attn[1], two))
    ff[1] = over(ff[1], one)
    x = steps.add(halves(part, swap(part, INNER)))
    steps.next()
    xs, middles, mixes = [], [], []

    def run_attn(l, adds):
        x, mix, own = attn_forward([steps.tie(adds[0])] + adds[1:], norms[2 * l], segq, segk, attn[l], flag)
        xs.append(x)
        mixes.append(mix)
        steps.add(own)
        return [x, own, swap(own, INNER)]

    def run_ff(l, adds):
        middle, own = ff_forward([steps.tie(adds[0])] + adds[1:], norms[2 * l + 1], ff[l], flag)
        middles.append(middle)
        steps.add(own)
        return [middle, own, swap(own, INNER)]

    ff[0] = across(ff[0])
    attn[1] = near(attn[1])
    ff[1] = flat(over(ff[1], two))
    attn[2] = over(attn[2], one)
    adds = run_attn(0, [x])
    steps.next()
    attn[1] = across(attn[1])
    ff[1] = near(ff[1])
    attn[2] = flat(over(attn[2], two))
    ff[2] = over(ff[2], one)
    adds = run_ff(0, adds)
    steps.next()
    ff[1] = across(ff[1])
    attn[2] = near(attn[2])
    ff[2] = flat(over(ff[2], two))
    adds = run_attn(1, adds)
    steps.next()
    attn[2] = across(attn[2])
    ff[2] = near(ff[2])
    head = over(head_unit, one)
    adds = run_ff(1, adds)
    steps.next()
    ff[2] = across(ff[2])
    teach = over(teach, one)
    head = over(head, two)
    adds = run_attn(2, adds)
    steps.next()
    teach = over(over(teach, two), [low])
    head = over(head, [low]).reshape(width, half)
    adds = run_ff(2, adds)
    x = sum(v.astype(F32) for v in adds)

    teach = jnp.swapaxes(teach.reshape((2, -1, images, half)), 0, 1).reshape(-1, images, half)
    me = lax.axis_index("dp")
    source = jnp.sum(jnp.where(teacher_map == me, jnp.arange(teacher_map.shape[0], dtype=jnp.int32), 0))
    teach_log = lax.dynamic_index_in_dim(teach, jnp.bitwise_xor(source, me), 0, False)

    divisor = jnp.maximum(count, 1.0)[:, None]
    pooled = jnp.dot(member, x, precision=HIGH) / divisor
    pooled_normed = layer_norm(pooled, norms[-1]).astype(BF)
    logits = nn(pooled_normed, head)
    theirs = swap(logits, INNER)
    peak = jnp.maximum(jnp.max(logits, -1, keepdims=True), jnp.max(theirs, -1, keepdims=True))
    total = jnp.sum(jnp.exp(logits - peak), -1, keepdims=True) + jnp.sum(jnp.exp(theirs - peak), -1, keepdims=True)
    student_log = logits - peak - jnp.log(total)
    loss_local = jnp.sum(owned * jnp.exp(teach_log) * (teach_log - student_log))
    d_logits = (owned * (jnp.exp(student_log) - jnp.exp(teach_log)) / total_images).astype(BF)
    g_head = tn(pooled_normed, d_logits).astype(BF)
    d_pooled, g_final = norm_back(pooled, norms[-1], both(nt(d_logits, head)))
    d_x = lax.dot_general(member, d_pooled / divisor, (((0,), (0,)), ((), ())), precision=HIGH)

    steps = Steps()
    g, g_norms = {}, {}

    def near(name):
        own, near, across, both_ways = g[name]
        near = near.astype(F32) + steps.swap(both_ways, FIRST).astype(F32)
        g[name] = own, near.astype(BF), steps.swap(across, FIRST)

    def blocks_of(value):
        value = value.astype(BF).reshape((-1, rows, value.shape[-1]))
        return [value[i] for i in range(value.shape[0])]

    def near_last(name):
        own, near, received = g[name]
        value = own.astype(F32) + received.astype(F32) + steps.swap(near, SECOND).astype(F32)
        g[name] = blocks_of(value)

    def near_low(name):
        keep, send = g[name]
        g[name] = blocks_of(keep.astype(F32) + steps.swap(send, low).astype(F32))

    def far_first(*names):
        for bit in high[:0:-1]:
            half = len(g[names[0]]) // 2
            got = steps.swap(jnp.stack([v for name in names for v in g[name][half:]]), bit)
            for k, name in enumerate(names):
                g[name] = [
                    (g[name][i].astype(F32) + got[k * half + i].astype(F32)).astype(BF) for i in range(half)
                ]

    def far_last(*names):
        got = steps.swap(jnp.stack([g[name][1] for name in names]), high[0])
        for k, name in enumerate(names):
            g[name] = (g[name][0], got[k])

    def back_ff(l, back):
        back = [steps.tie(back[0])] + back[1:]
        d_x, *grad, own, g_above = ff_backward(back, middles[l], norms[2 * l + 1], ff[l], flag)
        g["ff", l] = grad
        if l < LAYERS - 1:
            g_norms[2 * l + 2] = g_above
        steps.add(own)
        return [d_x, middles[l], norms[2 * l + 1], own, swap(own, INNER)]

    def back_attn(l, back):
        back = [steps.tie(back[0])] + back[1:]
        d_mid, *grad, own, g_above = attn_backward(
            back, xs[l], norms[2 * l], segq, segk, mixes[l], attn[l], flag
        )
        g["attn", l] = grad
        g_norms[2 * l + 1] = g_above
        steps.add(own)
        return [d_mid, xs[l], norms[2 * l], own, swap(own, INNER)]

    g["head"] = (g_head[:mid], g_head[mid:])
    near_low("head")
    back = back_ff(2, [d_x])
    steps.next()
    near(("ff", 2))
    far_first("head")
    back = back_attn(2, back)
    steps.next()
    near(("attn", 2))
    near_last(("ff", 2))
    far_last("head")
    back = back_ff(1, back)
    steps.next()
    near(("ff", 1))
    near_last(("attn", 2))
    far_first(("ff", 2))
    back = back_attn(1, back)
    steps.next()
    near(("attn", 1))
    near_last(("ff", 1))
    far_first(("attn", 2))
    far_last(("ff", 2))
    back = back_ff(0, back)
    steps.next()
    near(("ff", 0))
    near_last(("attn", 1))
    far_first(("ff", 1))
    far_last(("attn", 2))
    back = back_attn(0, back)
    steps.next()
    d_x0, g_norms[0] = input_gradient([steps.tie(back[0])] + back[1:])
    theirs = steps.swap(of_inner(d_x0, inner), OUTER)
    near(("attn", 0))
    near_last(("ff", 0))
    far_first(("attn", 1))
    far_last(("ff", 1))
    theirs = halves(theirs, swap(theirs, INNER))
    g_patch = tn(jnp.concatenate([d_x0, theirs], 0), jnp.concatenate(pix, 0)).astype(BF)
    steps.add(g_patch)
    g["patch"] = (g_patch[:mid], g_patch[mid:])
    token = g_norms[0]
    done = [None] * LAYERS
    done[2] = finish(g["attn", 2], g["ff", 2], token)
    steps.next()
    near_low("patch")
    near_last(("attn", 0))
    far_first(("ff", 0))
    far_last(("attn", 1))
    g_head = steps.tie(g["head"][0]).astype(F32) + g["head"][1].astype(F32)
    g_head = g_head + steps.swap(g_head, OUTER)
    g_norm = steps.tie(jnp.concatenate([g_norms[i] for i in range(6)] + [g_final], 0))
    g_norm = 0.5 * (g_norm + swap(g_norm, INNER))
    done[1] = finish(g["attn", 1], g["ff", 1], g_patch)
    steps.next()
    far_first(("attn", 0), "patch")
    far_last(("ff", 0))
    g_norm = g_norm + steps.swap(g_norm, OUTER)
    g_norm = jnp.moveaxis(g_norm.reshape(14, 2, -1, rows), 0, 2)
    g_norm = g_norm[0] + steps.swap(g_norm[1], low)
    g_head = halves(g_head, swap(g_head, INNER))
    steps.next()
    far_last(("attn", 0), "patch")
    g_norm = g_norm.reshape((2,) * len(high) + (14, rows))
    for bit in high[::-1]:
        g_norm = g_norm[0] + steps.swap(g_norm[1], bit)
    g_norm = g_norm.reshape(7, 2, rows)
    done[0] = finish(g["attn", 0], g["ff", 0], g_patch)
    g_patch = g["patch"][0].astype(F32) + g["patch"][1].astype(F32)

    grads = tuple(jnp.stack([layer[i] for layer in done]) for i in range(4)) + (g_patch.T, g_head, g_norm)
    first_model = (lax.axis_index("mp") == 0).astype(F32)
    squares = sum(layer[4][0, 0] for layer in done) + jnp.sum(g_patch * g_patch) + first_model * (
        jnp.sum(g_head * g_head) + jnp.sum(g_norm * g_norm)
    )
    sums = jnp.stack([squares, loss_local * (outer >= 0)])
    sums = sums + swap(sums, INNER)
    sums = sums + swap(sums, OUTER)
    if len(high) == 2:
        (axis, a), (_, b) = high
        sums = sums + swap(sums, low)
        sums = (sums + swap(sums, (axis, a))) + (swap(sums, (axis, b)) + swap(sums, (axis, a | b)))
    else:
        for bit in bits:
            sums = sums + swap(sums, bit)
    loss = sums[1]
    grad_norm = jnp.sqrt(sums[0])
    clip = jnp.minimum(1.0, CLIP / grad_norm)
    results = []
    for kind in range(7):
        results.append(
            adam(masters[kind], grads[kind] * clip, firsts[kind], seconds[kind], RATES[kind], DECAYS[kind])
        )
    return (loss, grad_norm) + tuple(r[i] for i in range(3) for r in results)


def solution(mesh):
    weights = (
        P(None, None, "dp", "mp"),
        P(None, "mp", "dp"),
        P(None, "dp", "mp"),
        P(None, "mp", "dp"),
        P("mp", "dp"),
        P("dp", None),
        P(None, None, "dp"),
    )
    placed = (P("dp", "mp"), P("dp", None), P("dp"), P("dp", None), P()) + weights * 3
    return jax.shard_map(
        body, mesh=mesh, in_specs=placed, out_specs=(P(), P()) + weights * 3, check_vma=False
    )
```

time: 842 us -> 734 us (0.87)
  waiting for transfers between devices: 297 us -> 204 us
  local copies, waits for them, and re-layouts: 99.2 us -> 57.8 us
  Pallas kernels: 226 us -> 248 us
    ppermute x97 -> x106, waiting for transfers between devices: 297 us -> 204 us  [swap(): return lax.ppermute(value, AXES, pairs)]
    concatenate x25 -> x0, other arithmetic: 27.9 us -> none  [gather(): value = jnp.concatenate([value, swap(value, bit)], dims[bit])]
    another operation x9 -> x33, other arithmetic: 4.12 us -> 27.1 us  [the longest x19 20.5 us: over(): unit = jnp.stack([unit, steps.swap(unit, bit)])]
    slice x36 -> x15, local copies, waits for them, and re-layouts: 23.9 us -> 1.01 us  [the longest x1 0.62 us: run_ff(): norms[2 * l + 1]]
    pallas_call x12 -> x16, Pallas kernels: 226 us -> 248 us  [the longest x3 88 us: attn_backward(): pl.pallas_call(functools.partial(attn_back_kernel, len(back)), grid=(step...]
    convert_element_type x25 -> x30, other arithmetic: 22 us -> 32.5 us  [the longest x13 14.4 us: far_first(): (g[name][i].astype(F32) + got[k * half + i].astype(F32)).astype(BF)]
    concatenate x11 -> x1, local copies, waits for them, and re-layouts: 12.2 us -> 2.68 us  [body(): jnp.concatenate([g_norms[i] for i in range(6)] + [g_final], 0)]
    ppermute x97 -> x106, starting transfers between devices: 95.8 us -> 93.8 us  [swap(): return lax.ppermute(value, AXES, pairs)]
  transfers between devices with their start and end apart: 97 -> 106, of which waited for: 41 -> 38; matrix products, arithmetic and copies ran while one was open for 20% -> 16% of each run, Pallas kernels for 25% -> 31%
where the time goes in v3:
time: 734 us; the launch traced here: 727 us
  Pallas kernels  248 us (34%)
  waiting for transfers between devices  204 us (28%)
  other arithmetic  99.6 us (14%)
  starting transfers between devices  93.8 us (13%)
  local copies, waits for them, and re-layouts  57.8 us (8%)
  between operations  13.1 us (2%)
  matrix products  10.9 us (1%)
    ppermute x106, waiting for transfers between devices, swap(): return lax.ppermute(value, AXES, pairs)  204 us
    ppermute x106, starting transfers between devices, swap(): return lax.ppermute(value, AXES, pairs)  93.8 us
    pallas_call x3, Pallas kernels, attn_backward(): pl.pallas_call(functools.partial(attn_back_kernel, len(back)), grid=(step...  88 us
    pallas_call x3, Pallas kernels, ff_backward(): pl.pallas_call(functools.partial(ff_back_kernel, len(back)), grid=(steps,...  56.2 us
    pallas_call x3, Pallas kernels, attn_forward(): pl.pallas_call(functools.partial(attn_fwd_kernel, len(adds)), grid=(steps...  54.2 us
    pallas_call x3, Pallas kernels, ff_forward(): pl.pallas_call(functools.partial(ff_fwd_kernel, len(adds)), grid=(steps,)...  36.9 us
    unnamed x247, local copies, waits for them, and re-layouts  26.6 us
    another operation x19, other arithmetic, over(): unit = jnp.stack([unit, steps.swap(unit, bit)])  20.5 us
  transfers between devices with their start and end apart: 106, of which 38 were waited for; matrix products, arithmetic and copies ran while one was open for 16% of the time, Pallas kernels for 31%

profile of v3, /device:TPU:0, one launch (start us, length us, event | category | flops | bytes accessed | tf_op | source)
XLA Modules:
  0.0 727.2 jit_solution(4213680777123948195)
XLA Ops:
  46.7 9.7 %collective-permute-done.5 = bf16[2,96,768]{1,2,0:T(8,128)(2,1)} collective-permute-done((bf16[2,96,768]{1,2,0:T(8,128)(2,1)}, bf16[2,96,768]{1,2,0:T(8,128)(2,1)}, u32[]{:S(2)}, u32[]{:S(2)}) %collective-permute-start.5) | collective-permute-done | bytes 294944 | tf_op jit(solution)/shard_map/ppermute | solution.py:46
  73.3 12.6 %collective-permute-done.9 = bf16[96,768]{0,1:T(8,128)(2,1)S(1)} collective-permute-done((bf16[96,768]{0,1:T(8,128)(2,1)S(1)}, bf16[96,768]{0,1:T(8,128)(2,1)S(1)}, u32[]{:S(2)}, u32[]{:S(2)}) %collective-permute-start.9) | collective-permute-done | bytes 147488 | tf_op jit(solution)/shard_map/ppermute | solution.py:46
  85.9 11.4 %collective-permute-done.8 = bf16[2,96,1536]{2,1,0:T(8,128)(2,1)S(1)} collective-permute-done((bf16[2,96,1536]{2,1,0:T(8,128)(2,1)S(1)}, bf16[2,96,1536]{2,1,0:T(8,128)(2,1)S(1)}, u32[]{:S(2)}, u32[]{:S(2)}) %collective-permute-start.8) | collective-permute-done | bytes 589856 | tf_op jit(solution)/shard_map/ppermute | solution.py:46
  97.8 11.6 %collective-permute-done.12 = bf16[576,384]{1,0:T(8,128)(2,1)S(1)} collective-permute-done((bf16[576,384]{1,0:T(8,128)(2,1)S(1)}, bf16[576,384]{1,0:T(8,128)(2,1)S(1)}, u32[]{:S(2)}, u32[]{:S(2)}) %collective-permute-start.12) | collective-permute-done | bytes 442400 | tf_op jit(solution)/shard_map/ppermute | solution.py:46
  122.2 11.1 %collective-permute-done.17 = bf16[2,96,768]{1,2,0:T(8,128)(2,1)} collective-permute-done((bf16[2,96,768]{1,2,0:T(8,128)(2,1)}, bf16[2,96,768]{1,2,0:T(8,128)(2,1)}, u32[]{:S(2)}, u32[]{:S(2)}) %collective-permute-start.17) | collective-permute-done | bytes 294944 | tf_op jit(solution)/shard_map/ppermute | solution.py:46
  133.3 11.3 %collective-permute-done.14.refs_8_.refs_14_ = bf16[384,768]{1,0:T(8,128)(2,1)} collective-permute-done((bf16[384,768]{1,0:T(8,128)(2,1)}, bf16[384,768]{1,0:T(8,128)(2,1)}, u32[]{:S(2)}, u32[]{:S(2)}) %collective-permute-start.14) | collective-permute-done | bytes 589856 | tf_op jit(solution)/shard_map/ppermute | solution.py:46
  155.6 17.6 %attn_forward.3 = (f32[576,768]{1,0:T(8,128)}, bf16[6,576,256]{2,1,0:T(8,128)(2,1)}, bf16[576,768]{1,0:T(8,128)(2,1)}) custom-call(s32[1]{0:T(128)} %bitcast.refs_0_, f32[576,768]{1,0:T(8,128)} %maximum_select_fusion.refs_1_, f32[2,768]{1,0:T(2,128)} %get-tuple-element.571.refs_2_.refs_7_.norm, s32[576,1]{1,0:T(8,128)} %broadcast_in_dim.27.refs_3_.refs_5_.refs_8_, ...), custom_call_target="tpu_custom_call" | custom-call | flops 1000000 | bytes 10000 | tf_op jit(solution)/shard_map/attn_forward/pallas_call | solution.py:245
  185.3 12.4 %ff_forward.3 = (f32[576,768]{1,0:T(8,128)}, bf16[576,768]{1,0:T(8,128)(2,1)}) custom-call(s32[1]{0:T(128)} %bitcast.refs_0_, f32[576,768]{1,0:T(8,128)} %get-tuple-element.202.refs_1_.refs_6_.value, bf16[576,768]{1,0:T(8,128)(2,1)} %get-tuple-element.201.refs_2_, bf16[576,768]{1,0:T(8,128)(2,1)} %copy-done.57, ...), custom_call_target="tpu_custom_call" | custom-call | flops 1000000 | bytes 10000 | tf_op jit(solution)/shard_map/ff_forward/pallas_call | solution.py:300
  201.3 11.2 %collective-permute-done.25.refs_10_.refs_14_ = bf16[384,768]{1,0:T(8,128)(2,1)S(1)} collective-permute-done((bf16[384,768]{1,0:T(8,128)(2,1)S(1)}, bf16[384,768]{1,0:T(8,128)(2,1)S(1)}, u32[]{:S(2)}, u32[]{:S(2)}) %collective-permute-start.25) | collective-permute-done | bytes 589856 | tf_op jit(solution)/shard_map/ppermute | solution.py:46
  220.9 18.3 %attn_forward.4 = (f32[576,768]{1,0:T(8,128)}, bf16[6,576,256]{2,1,0:T(8,128)(2,1)}, bf16[576,768]{1,0:T(8,128)(2,1)}) custom-call(s32[1]{0:T(128)} %bitcast.refs_0_, f32[576,768]{1,0:T(8,128)} %get-tuple-element.209.refs_1_.refs_6_.refs_2_, bf16[576,768]{1,0:T(8,128)(2,1)} %get-tuple-element.208.refs_2_, bf16[576,768]{1,0:T(8,128)(2,1)} %collective-permute-done.30.refs_3_, ...), custom_call_target="tpu_custom_call" | custom-call | flops 1000000 | bytes 10000 | tf_op jit(solution)/shard_map/attn_forward/pallas_call | solution.py:245
  250.7 12.3 %ff_forward.4 = (f32[576,768]{1,0:T(8,128)}, bf16[576,768]{1,0:T(8,128)(2,1)}) custom-call(s32[1]{0:T(128)} %bitcast.refs_0_, f32[576,768]{1,0:T(8,128)} %get-tuple-element.215.refs_1_.refs_6_.refs_2_, bf16[576,768]{1,0:T(8,128)(2,1)} %get-tuple-element.214.refs_2_, bf16[576,768]{1,0:T(8,128)(2,1)} %copy-done.59, ...), custom_call_target="tpu_custom_call" | custom-call | flops 1000000 | bytes 10000 | tf_op jit(solution)/shard_map/ff_forward/pallas_call | solution.py:300
  269.3 13.2 %collective-permute-done.36.refs_10_.refs_14_ = bf16[384,768]{1,0:T(8,128)(2,1)S(1)} collective-permute-done((bf16[384,768]{1,0:T(8,128)(2,1)S(1)}, bf16[384,768]{1,0:T(8,128)(2,1)S(1)}, u32[]{:S(2)}, u32[]{:S(2)}) %collective-permute-start.36) | collective-permute-done | bytes 589856 | tf_op jit(solution)/shard_map/ppermute | solution.py:46
  285.6 18.4 %attn_forward.5 = (f32[576,768]{1,0:T(8,128)}, bf16[6,576,256]{2,1,0:T(8,128)(2,1)}, bf16[576,768]{1,0:T(8,128)(2,1)}) custom-call(s32[1]{0:T(128)} %bitcast.refs_0_, f32[576,768]{1,0:T(8,128)} %get-tuple-element.221.refs_1_.refs_6_.refs_2_, bf16[576,768]{1,0:T(8,128)(2,1)} %get-tuple-element.220.refs_2_, bf16[576,768]{1,0:T(8,128)(2,1)} %collective-permute-done.40.refs_3_, ...), custom_call_target="tpu_custom_call" | custom-call | flops 1000000 | bytes 10000 | tf_op jit(solution)/shard_map/attn_forward/pallas_call | solution.py:245
  318.7 12.2 %ff_forward.5 = (f32[576,768]{1,0:T(8,128)}, bf16[576,768]{1,0:T(8,128)(2,1)}) custom-call(s32[1]{0:T(128)} %bitcast.refs_0_, f32[576,768]{1,0:T(8,128)} %get-tuple-element.227.refs_1_.refs_6_.refs_2_, bf16[576,768]{1,0:T(8,128)(2,1)} %get-tuple-element.226.refs_2_, bf16[576,768]{1,0:T(8,128)(2,1)} %copy-done.58, ...), custom_call_target="tpu_custom_call" | custom-call | flops 1000000 | bytes 10000 | tf_op jit(solution)/shard_map/ff_forward/pallas_call | solution.py:300
  355.7 17.1 %ff_backward.3 = (f32[576,768]{1,0:T(8,128)}, bf16[384,1536]{1,0:T(8,128)(2,1)}, bf16[384,1536]{1,0:T(8,128)(2,1)}, bf16[384,1536]{1,0:T(8,128)(2,1)}, bf16[384,...) custom-call(s32[1]{0:T(128)} %bitcast.refs_0_, f32[576,768]{1,0:T(8,128)} %fusion.43.refs_1_, ...), custom_call_target="tpu_custom_call" | custom-call | flops 1000000 | bytes 10000 | tf_op jit(solution)/shard_map/ff_backward/pallas_call | solution.py:381
  377.2 29.4 %attn_backward.3 = (f32[576,768]{1,0:T(8,128)}, bf16[384,768]{1,0:T(8,128)(2,1)}, bf16[384,768]{1,0:T(8,128)(2,1)}, bf16[384,768]{1,0:T(8,128)(2,1)}, bf16[384,7...) custom-call(s32[1]{0:T(128)} %bitcast.refs_0_, f32[576,768]{1,0:T(8,128)} %get-tuple-element.235.refs_1_, ...), custom_call_target="tpu_custom_call" | custom-call | flops 1000000 | bytes 10000 | tf_op jit(solution)/shard_map/attn_backward/pallas_call | solution.py:450
  412.8 19.5 %ff_backward.4 = (f32[576,768]{1,0:T(8,128)}, bf16[384,1536]{1,0:T(8,128)(2,1)}, bf16[384,1536]{1,0:T(8,128)(2,1)}, bf16[384,1536]{1,0:T(8,128)(2,1)}, bf16[384,...) custom-call(s32[1]{0:T(128)} %bitcast.refs_0_, f32[576,768]{1,0:T(8,128)} %get-tuple-element.244.refs_1_, ...), custom_call_target="tpu_custom_call" | custom-call | flops 1000000 | bytes 10000 | tf_op jit(solution)/shard_map/ff_backward/pallas_call | solution.py:381
  449.1 29.1 %attn_backward.4 = (f32[576,768]{1,0:T(8,128)}, bf16[384,768]{1,0:T(8,128)(2,1)}, bf16[384,768]{1,0:T(8,128)(2,1)}, bf16[384,768]{1,0:T(8,128)(2,1)}, bf16[384,7...) custom-call(s32[1]{0:T(128)} %bitcast.refs_0_, f32[576,768]{1,0:T(8,128)} %get-tuple-element.254.refs_1_, ...), custom_call_target="tpu_custom_call" | custom-call | flops 1000000 | bytes 10000 | tf_op jit(solution)/shard_map/attn_backward/pallas_call | solution.py:450
  492.6 19.6 %ff_backward.5 = (f32[576,768]{1,0:T(8,128)}, bf16[384,1536]{1,0:T(8,128)(2,1)}, bf16[384,1536]{1,0:T(8,128)(2,1)}, bf16[384,1536]{1,0:T(8,128)(2,1)}, bf16[384,...) custom-call(s32[1]{0:T(128)} %bitcast.refs_0_, f32[576,768]{1,0:T(8,128)} %get-tuple-element.266.refs_1_, ...), custom_call_target="tpu_custom_call" | custom-call | flops 1000000 | bytes 10000 | tf_op jit(solution)/shard_map/ff_backward/pallas_call | solution.py:381
  524.2 29.4 %attn_backward.5 = (f32[576,768]{1,0:T(8,128)}, bf16[384,768]{1,0:T(8,128)(2,1)}, bf16[384,768]{1,0:T(8,128)(2,1)}, bf16[384,768]{1,0:T(8,128)(2,1)}, bf16[384,7...) custom-call(s32[1]{0:T(128)} %bitcast.refs_0_, f32[576,768]{1,0:T(8,128)} %get-tuple-element.278.refs_1_, ...), custom_call_target="tpu_custom_call" | custom-call | flops 1000000 | bytes 10000 | tf_op jit(solution)/shard_map/attn_backward/pallas_call | solution.py:450
  577.0 7.6 %collective-permute-done.84 = bf16[2,96,768]{2,1,0:T(8,128)(2,1)} collective-permute-done((bf16[2,96,768]{2,1,0:T(8,128)(2,1)}, bf16[2,96,768]{2,1,0:T(8,128)(2,1)}, u32[]{:S(2)}, u32[]{:S(2)}) %collective-permute-start.84) | collective-permute-done | bytes 294944 | tf_op jit(solution)/shard_map/ppermute | solution.py:46
  594.9 8.2 %collective-permute-done.83 = bf16[384,1536]{1,0:T(8,128)(2,1)} collective-permute-done((bf16[384,1536]{1,0:T(8,128)(2,1)S(1)}, bf16[384,1536]{1,0:T(8,128)(2,1)}, u32[]{:S(2)}, u32[]{:S(2)}) %collective-permute-start.83) | collective-permute-done | bytes 1179680 | tf_op jit(solution)/shard_map/ppermute | solution.py:46
  611.7 12.2 %collective-permute-done.89 = bf16[1,96,768]{2,1,0:T(8,128)(2,1)S(1)} collective-permute-done((bf16[1,96,768]{2,1,0:T(8,128)(2,1)S(1)}, bf16[1,96,768]{2,1,0:T(8,128)(2,1)S(1)}, u32[]{:S(2)}, u32[]{:S(2)}) %collective-permute-start.89) | collective-permute-done | bytes 147488 | tf_op jit(solution)/shard_map/ppermute | solution.py:46
  654.1 9.3 %collective-permute-done.91 = bf16[4,96,768]{2,1,0:T(8,128)(2,1)} collective-permute-done((bf16[4,96,768]{2,1,0:T(8,128)(2,1)}, bf16[4,96,768]{2,1,0:T(8,128)(2,1)}, u32[]{:S(2)}, u32[]{:S(2)}) %collective-permute-start.91) | collective-permute-done | bytes 589856 | tf_op jit(solution)/shard_map/ppermute | solution.py:46
  (640 shorter events, 349.4 us)
Async XLA Ops:
  110.4 34.2 %collective-permute-start.15 = (bf16[384,1536]{1,0:T(8,128)(2,1)S(1)}, bf16[384,1536]{1,0:T(8,128)(2,1)S(1)}, u32[]{:S(2)}, u32[]{:S(2)}) collective-permute-start(bf16[384,1536]{1,0:T(8,128)(2,1)S(1)} %bitcast.316), channel_id=1, source_target_pairs={{0,2},{1,5},{2,0},{3,7},{4,6},{5,1},{6,4},{7,3},{8,10},{9,13},{10,... | collective-permute-start | bytes 3538952 | tf_op jit(solution)/shard_map/ppermute | solution.py:46
  110.9 33.7 %collective-permute-start.16 = (bf16[384,1536]{1,0:T(8,128)(2,1)S(1)}, bf16[384,1536]{1,0:T(8,128)(2,1)}, u32[]{:S(2)}, u32[]{:S(2)}) collective-permute-start(bf16[384,1536]{1,0:T(8,128)(2,1)S(1)} %bitcast.317), channel_id=1, source_target_pairs={{0,4},{1,3},{2,6},{3,1},{4,0},{5,7},{6,2},{7,5},{8,12},{9,11},{10,... | collective-permute-start | bytes 3538952 | tf_op jit(solution)/shard_map/ppermute | solution.py:46
  112.4 32.1 %collective-permute-start.14 = (bf16[384,768]{1,0:T(8,128)(2,1)}, bf16[384,768]{1,0:T(8,128)(2,1)}, u32[]{:S(2)}, u32[]{:S(2)}) collective-permute-start(bf16[384,768]{1,0:T(8,128)(2,1)} %collective-permute-done.10.refs_6_.refs_12_), channel_id=1, source_target_pairs={{0,4},{1,3},{2,6},{3,1},{4,0},{5,7},{6,2},{7,5},{8,12},{9,11},{10,... | collective-permute-start | bytes 1769480 | tf_op jit(solution)/shard_map/ppermute | solution.py:46
  144.6 32.4 %collective-permute-start.19 = (bf16[384,1536]{1,0:T(8,128)(2,1)S(1)}, bf16[384,1536]{1,0:T(8,128)(2,1)}, u32[]{:S(2)}, u32[]{:S(2)}) collective-permute-start(bf16[384,1536]{1,0:T(8,128)(2,1)S(1)} %collective-permute-done.15.refs_6_.refs_9_), channel_id=1, source_target_pairs={{0,4},{1,3},{2,6},{3,1},{4,0},{5,7},{6,2},{7,5},{8,12},{9,11},{10,... | collective-permute-start | bytes 3538952 | tf_op jit(solution)/shard_map/ppermute | solution.py:46
  177.9 34.7 %collective-permute-start.26 = (bf16[384,1536]{1,0:T(8,128)(2,1)S(1)}, bf16[384,1536]{1,0:T(8,128)(2,1)S(1)}, u32[]{:S(2)}, u32[]{:S(2)}) collective-permute-start(bf16[384,1536]{1,0:T(8,128)(2,1)S(1)} %bitcast.320), channel_id=1, source_target_pairs={{0,2},{1,5},{2,0},{3,7},{4,6},{5,1},{6,4},{7,3},{8,10},{9,13},{10,... | collective-permute-start | bytes 3538952 | tf_op jit(solution)/shard_map/ppermute | solution.py:46
  179.3 33.2 %collective-permute-start.27 = (bf16[384,1536]{1,0:T(8,128)(2,1)S(1)}, bf16[384,1536]{1,0:T(8,128)(2,1)S(1)}, u32[]{:S(2)}, u32[]{:S(2)}) collective-permute-start(bf16[384,1536]{1,0:T(8,128)(2,1)S(1)} %bitcast.321), channel_id=1, source_target_pairs={{0,4},{1,3},{2,6},{3,1},{4,0},{5,7},{6,2},{7,5},{8,12},{9,11},{10,... | collective-permute-start | bytes 3538952 | tf_op jit(solution)/shard_map/ppermute | solution.py:46
  179.9 32.6 %collective-permute-start.25 = (bf16[384,768]{1,0:T(8,128)(2,1)S(1)}, bf16[384,768]{1,0:T(8,128)(2,1)S(1)}, u32[]{:S(2)}, u32[]{:S(2)}) collective-permute-start(bf16[384,768]{1,0:T(8,128)(2,1)S(1)} %collective-permute-done.20.refs_8_.refs_12_), channel_id=1, source_target_pairs={{0,4},{1,3},{2,6},{3,1},{4,0},{5,7},{6,2},{7,5},{8,12},{9,11},{10,... | collective-permute-start | bytes 1769480 | tf_op jit(solution)/shard_map/ppermute | solution.py:46
  213.6 33.8 %collective-permute-start.31 = (bf16[384,1536]{1,0:T(8,128)(2,1)S(1)}, bf16[384,1536]{1,0:T(8,128)(2,1)}, u32[]{:S(2)}, u32[]{:S(2)}) collective-permute-start(bf16[384,1536]{1,0:T(8,128)(2,1)S(1)} %collective-permute-done.26.refs_6_.refs_9_), channel_id=1, source_target_pairs={{0,4},{1,3},{2,6},{3,1},{4,0},{5,7},{6,2},{7,5},{8,12},{9,11},{10,... | collective-permute-start | bytes 3538952 | tf_op jit(solution)/shard_map/ppermute | solution.py:46
  248.3 34.3 %collective-permute-start.37 = (bf16[384,1536]{1,0:T(8,128)(2,1)S(1)}, bf16[384,1536]{1,0:T(8,128)(2,1)S(1)}, u32[]{:S(2)}, u32[]{:S(2)}) collective-permute-start(bf16[384,1536]{1,0:T(8,128)(2,1)S(1)} %bitcast.324), channel_id=1, source_target_pairs={{0,2},{1,5},{2,0},{3,7},{4,6},{5,1},{6,4},{7,3},{8,10},{9,13},{10,... | collective-permute-start | bytes 3538952 | tf_op jit(solution)/shard_map/ppermute | solution.py:46
  249.0 34.4 %collective-permute-start.38 = (bf16[384,1536]{1,0:T(8,128)(2,1)S(1)}, bf16[384,1536]{1,0:T(8,128)(2,1)S(1)}, u32[]{:S(2)}, u32[]{:S(2)}) collective-permute-start(bf16[384,1536]{1,0:T(8,128)(2,1)S(1)} %bitcast.325), channel_id=1, source_target_pairs={{0,4},{1,3},{2,6},{3,1},{4,0},{5,7},{6,2},{7,5},{8,12},{9,11},{10,... | collective-permute-start | bytes 3538952 | tf_op jit(solution)/shard_map/ppermute | solution.py:46
  284.4 32.9 %collective-permute-start.41 = (bf16[384,1536]{1,0:T(8,128)(2,1)S(1)}, bf16[384,1536]{1,0:T(8,128)(2,1)S(1)}, u32[]{:S(2)}, u32[]{:S(2)}) collective-permute-start(bf16[384,1536]{1,0:T(8,128)(2,1)S(1)} %collective-permute-done.37.refs_6_.refs_5_), channel_id=1, source_target_pairs={{0,4},{1,3},{2,6},{3,1},{4,0},{5,7},{6,2},{7,5},{8,12},{9,11},{10,... | collective-permute-start | bytes 3538952 | tf_op jit(solution)/shard_map/ppermute | solution.py:46
  372.8 33.8 %collective-permute-start.53 = (bf16[384,1536]{1,0:T(8,128)(2,1)}, bf16[384,1536]{1,0:T(8,128)(2,1)S(1)}, u32[]{:S(2)}, u32[]{:S(2)}) collective-permute-start(bf16[384,1536]{1,0:T(8,128)(2,1)} %get-tuple-element.239), channel_id=1, source_target_pairs={{0,4},{1,3},{2,6},{3,1},{4,0},{5,7},{6,2},{7,5},{8,12},{9,11},{10,... | collective-permute-start | bytes 3538952 | tf_op jit(solution)/shard_map/ppermute | solution.py:46
  373.7 33.3 %collective-permute-start.54 = (bf16[384,1536]{1,0:T(8,128)(2,1)}, bf16[384,1536]{1,0:T(8,128)(2,1)S(1)}, u32[]{:S(2)}, u32[]{:S(2)}) collective-permute-start(bf16[384,1536]{1,0:T(8,128)(2,1)} %get-tuple-element.241), channel_id=1, source_target_pairs={{0,4},{1,3},{2,6},{3,1},{4,0},{5,7},{6,2},{7,5},{8,12},{9,11},{10,... | collective-permute-start | bytes 3538952 | tf_op jit(solution)/shard_map/ppermute | solution.py:46
  435.4 44.6 %collective-permute-start.62 = (bf16[384,1536]{1,0:T(8,128)(2,1)}, bf16[384,1536]{1,0:T(8,128)(2,1)}, u32[]{:S(2)}, u32[]{:S(2)}) collective-permute-start(bf16[384,1536]{1,0:T(8,128)(2,1)} %get-tuple-element.258), channel_id=1, source_target_pairs={{0,4},{1,3},{2,6},{3,1},{4,0},{5,7},{6,2},{7,5},{8,12},{9,11},{10,... | collective-permute-start | bytes 3538952 | tf_op jit(solution)/shard_map/ppermute | solution.py:46
  438.0 40.3 %collective-permute-start.65 = (bf16[2,96,1536]{2,1,0:T(8,128)(2,1)}, bf16[2,96,1536]{2,1,0:T(8,128)(2,1)}, u32[]{:S(2)}, u32[]{:S(2)}) collective-permute-start(bf16[2,96,1536]{2,1,0:T(8,128)(2,1)} %pad_maximum_fusion.15), channel_id=1, source_target_pairs={{0,16},{1,17},{2,18},{3,19},{4,20},{5,21},{6,22},{7,23},{8,24},{9,... | collective-permute-start | bytes 1769480 | tf_op jit(solution)/shard_map/ppermute | solution.py:46
  445.8 35.9 %collective-permute-start.63 = (bf16[384,1536]{1,0:T(8,128)(2,1)}, bf16[384,1536]{1,0:T(8,128)(2,1)S(1)}, u32[]{:S(2)}, u32[]{:S(2)}) collective-permute-start(bf16[384,1536]{1,0:T(8,128)(2,1)} %get-tuple-element.260), channel_id=1, source_target_pairs={{0,4},{1,3},{2,6},{3,1},{4,0},{5,7},{6,2},{7,5},{8,12},{9,11},{10,... | collective-permute-start | bytes 3538952 | tf_op jit(solution)/shard_map/ppermute | solution.py:46
  448.7 33.0 %collective-permute-start.64 = (bf16[384,768]{1,0:T(8,128)(2,1)S(1)}, bf16[384,768]{1,0:T(8,128)(2,1)}, u32[]{:S(2)}, u32[]{:S(2)}) collective-permute-start(bf16[384,768]{1,0:T(8,128)(2,1)S(1)} %add_convert_fusion.12), channel_id=1, source_target_pairs={{0,2},{1,5},{2,0},{3,7},{4,6},{5,1},{6,4},{7,3},{8,10},{9,13},{10,... | collective-permute-start | bytes 1769480 | tf_op jit(solution)/shard_map/ppermute | solution.py:46
  481.7 32.7 %collective-permute-start.69 = (bf16[384,1536]{1,0:T(8,128)(2,1)S(1)}, bf16[384,1536]{1,0:T(8,128)(2,1)S(1)}, u32[]{:S(2)}, u32[]{:S(2)}) collective-permute-start(bf16[384,1536]{1,0:T(8,128)(2,1)S(1)} %add_convert_fusion.3), channel_id=1, source_target_pairs={{0,2},{1,5},{2,0},{3,7},{4,6},{5,1},{6,4},{7,3},{8,10},{9,13},{10,... | collective-permute-start | bytes 3538952 | tf_op jit(solution)/shard_map/ppermute | solution.py:46
  514.5 39.1 %collective-permute-start.75 = (bf16[384,768]{1,0:T(8,128)(2,1)}, bf16[384,768]{1,0:T(8,128)(2,1)}, u32[]{:S(2)}, u32[]{:S(2)}) collective-permute-start(bf16[384,768]{1,0:T(8,128)(2,1)} %add_convert_fusion.10), channel_id=1, source_target_pairs={{0,2},{1,5},{2,0},{3,7},{4,6},{5,1},{6,4},{7,3},{8,10},{9,13},{10,... | collective-permute-start | bytes 1769480 | tf_op jit(solution)/shard_map/ppermute | solution.py:46
  517.4 37.9 %collective-permute-start.76 = (bf16[2,96,1536]{2,1,0:T(8,128)(2,1)S(1)}, bf16[2,96,1536]{2,1,0:T(8,128)(2,1)S(1)}, u32[]{:S(2)}, u32[]{:S(2)}) collective-permute-start(bf16[2,96,1536]{2,1,0:T(8,128)(2,1)S(1)} %pad_maximum_fusion.16), channel_id=1, source_target_pairs={{0,16},{1,17},{2,18},{3,19},{4,20},{5,21},{6,22},{7,23},{8,24},{9,... | collective-permute-start | bytes 1769480 | tf_op jit(solution)/shard_map/ppermute | solution.py:46
  519.6 37.4 %collective-permute-start.73 = (bf16[384,1536]{1,0:T(8,128)(2,1)}, bf16[384,1536]{1,0:T(8,128)(2,1)S(1)}, u32[]{:S(2)}, u32[]{:S(2)}) collective-permute-start(bf16[384,1536]{1,0:T(8,128)(2,1)} %get-tuple-element.282), channel_id=1, source_target_pairs={{0,4},{1,3},{2,6},{3,1},{4,0},{5,7},{6,2},{7,5},{8,12},{9,11},{10,... | collective-permute-start | bytes 3538952 | tf_op jit(solution)/shard_map/ppermute | solution.py:46
  520.9 36.1 %collective-permute-start.74 = (bf16[384,1536]{1,0:T(8,128)(2,1)}, bf16[384,1536]{1,0:T(8,128)(2,1)S(1)}, u32[]{:S(2)}, u32[]{:S(2)}) collective-permute-start(bf16[384,1536]{1,0:T(8,128)(2,1)} %get-tuple-element.284), channel_id=1, source_target_pairs={{0,4},{1,3},{2,6},{3,1},{4,0},{5,7},{6,2},{7,5},{8,12},{9,11},{10,... | collective-permute-start | bytes 3538952 | tf_op jit(solution)/shard_map/ppermute | solution.py:46
  523.3 33.7 %collective-permute-start.77 = (bf16[1,96,768]{2,1,0:T(8,128)(2,1)S(1)}, bf16[1,96,768]{2,1,0:T(8,128)(2,1)S(1)}, u32[]{:S(2)}, u32[]{:S(2)}) collective-permute-start(bf16[1,96,768]{2,1,0:T(8,128)(2,1)S(1)} %fusion.35), channel_id=1, source_target_pairs={{0,8},{1,9},{2,10},{3,11},{4,12},{5,13},{6,14},{7,15},{8,0},{9,1},... | collective-permute-start | bytes 442376 | tf_op jit(solution)/shard_map/ppermute | solution.py:46
  567.4 35.6 %collective-permute-start.83 = (bf16[384,1536]{1,0:T(8,128)(2,1)S(1)}, bf16[384,1536]{1,0:T(8,128)(2,1)}, u32[]{:S(2)}, u32[]{:S(2)}) collective-permute-start(bf16[384,1536]{1,0:T(8,128)(2,1)S(1)} %add_convert_fusion.1), channel_id=1, source_target_pairs={{0,2},{1,5},{2,0},{3,7},{4,6},{5,1},{6,4},{7,3},{8,10},{9,13},{10,... | collective-permute-start | bytes 3538952 | tf_op jit(solution)/shard_map/ppermute | solution.py:46
  (201 other events, 2368.0 us)

commit v4 on v3

--- a/solution.py
+++ b/solution.py
@@ -227,11 +227,15 @@
     load_weight(w, flag, *weight)
     mixed = nn(normed[...], w[...]).astype(BF)
     c = HEAD_DIM
+    width = w.shape[1] // 4
     keep = segq[...] == segk[...]
-    probs = masked_probs(mixed[:, :c] * HEAD_DIM ** (-0.5), mixed[:, c : 2 * c], keep)
-    out = nn(probs.astype(BF), mixed[:, 2 * c : 3 * c]).astype(BF)
-    mix_ref[0] = jnp.concatenate([mixed[:, : 3 * c], out], 1)
-    acc[...] += nt(out, w[:, 3 * c :])
+    outs = []
+    for at in range(0, width, c):
+        probs = masked_probs(mixed[:, at : at + c] * c ** (-0.5), mixed[:, width + at : width + at + c], keep)
+        outs.append(nn(probs.astype(BF), mixed[:, 2 * width + at : 2 * width + at + c]).astype(BF))
+    out = jnp.concatenate(outs, 1)
+    mix_ref[0] = jnp.concatenate([mixed[:, : 3 * width], out], 1)
+    acc[...] += nt(jnp.concatenate([jnp.zeros_like(outs[0]), out], 1), w[:, 3 * width - c :])
 
     @pl.when(step == pl.num_programs(0) - 1)
     def _():
@@ -240,7 +244,7 @@
 
 def attn_forward(adds, norm, segq, segk, pieces, flag):
     tokens, width = adds[0].shape
-    columns = 4 * HEAD_DIM
+    columns = pieces[0].shape[1]
     steps, quarters = quarter_specs(pieces[0], columns)
     return pl.pallas_call(
         functools.partial(attn_fwd_kernel, len(adds)),
@@ -403,7 +407,7 @@
     back = refs[1 : count + 1]
     value, norm, segq, segk, mix_ref = refs[count + 1 : count + 6]
     weight, d_ref, grad = refs[count + 6 : count + 10], refs[count + 10], refs[count + 11 : count + 15]
-    part_ref, g_ref, normed_t, dy, dy_t, w, acc = refs[count + 15 :]
+    part_ref, g_ref, normed_t, dy, dy_t, w, acc, d_mix = refs[count + 15 :]
     step = pl.program_id(0)
 
     @pl.when(step == 0)
@@ -412,29 +416,33 @@
         dy[...] = d_all.astype(BF)
         dy_t[...] = d_all.T.astype(BF)
         normed_t[...] = layer_norm(value[...], norm[...]).T.astype(BF)
+        d_mix[...] = jnp.zeros_like(d_mix)
         acc[...] = jnp.zeros_like(acc)
 
     load_weight(w, flag, *weight)
     c = HEAD_DIM
     scale = HEAD_DIM ** (-0.5)
-    query, key, val = (mix_ref[0, :, j * c : (j + 1) * c] for j in range(3))
-    query = query * scale
-    d_out = nn(dy[...], w[:, 3 * c :]).astype(BF)
+    width = w.shape[1] // 4
+    tokens = dy.shape[0]
+    d_outs = nn(dy[...], w[:, 3 * width - c :])[:, c:].astype(BF)
     keep = segq[...] == segk[...]
-    probs = masked_probs(query, key, keep)
-    d_probs = nt(d_out, val)
-    delta = jnp.sum(probs * d_probs, -1, keepdims=True)
-    d_scores = jnp.where(keep, probs * (d_probs - delta), 0.0).astype(BF)
-    d_query = (nn(d_scores, key) * scale).astype(BF)
-    d_key = tn(d_scores, query).astype(BF)
-    d_val = tn(probs.astype(BF), d_out).astype(BF)
-    d_left = jnp.concatenate([d_query, d_key], 1)
-    zero = jnp.zeros_like(d_val)
-    d_right = jnp.concatenate([d_val, zero], 1)
-    out = jnp.concatenate([zero, mix_ref[0, :, 3 * c :]], 1)
-    acc[...] += nt(d_left, w[:, : 2 * c]) + nt(d_right, w[:, 2 * c :])
-    left = nn(normed_t[...], d_left)
-    right = nn(normed_t[...], d_right) + nn(dy_t[...], out)
+    for at in range(0, width, c):
+        query = mix_ref[0, :, at : at + c] * scale
+        key = mix_ref[0, :, width + at : width + at + c]
+        val = mix_ref[0, :, 2 * width + at : 2 * width + at + c]
+        d_out = d_outs[:, at : at + c]
+        probs = masked_probs(query, key, keep)
+        d_probs = nt(d_out, val)
+        delta = jnp.sum(probs * d_probs, -1, keepdims=True)
+        d_scores = jnp.where(keep, probs * (d_probs - delta), 0.0).astype(BF)
+        d_mix[:, at : at + c] = (nn(d_scores, key) * scale).astype(BF)
+        d_mix[:, width + at : width + at + c] = nn(query.T, d_scores).T.astype(BF)
+        d_mix[:, 2 * width + at : 2 * width + at + c] = nn(d_out.T, probs.astype(BF)).T.astype(BF)
+    acc[...] += nt(d_mix[...], w[...])
+    wide = 4 * width - (3 * width - c)
+    out = jnp.concatenate([jnp.zeros((tokens, c), BF), mix_ref[0, :, 3 * width :]], 1)
+    left = nn(normed_t[...], d_mix[:, : 4 * width - wide])
+    right = nn(normed_t[...], d_mix[:, 4 * width - wide :]) + nn(dy_t[...], out)
     store_grad([left, right], flag, *grad)
 
     @pl.when(step == pl.num_programs(0) - 1)
@@ -444,7 +452,7 @@
 
 def attn_backward(back, value, norm, segq, segk, mix, pieces, flag):
     tokens, width = value.shape
-    columns = 4 * HEAD_DIM
+    columns = pieces[0].shape[1]
     steps, quarters = quarter_specs(pieces[0], columns)
     specs, shapes = back_out(tokens, width, pieces, quarters)
     return pl.pallas_call(
@@ -462,6 +470,7 @@
             pltpu.VMEM((width, tokens), BF),
             pltpu.VMEM((width, columns), BF),
             pltpu.VMEM((tokens, width), F32),
+            pltpu.VMEM((tokens, columns), BF),
         ],
         compiler_params=params(),
         cost_estimate=NO_COST,
@@ -491,40 +500,82 @@
     )(*back)
 
 
-def finish_kernel(token, *refs):
-    a_keep, a_got, f_keep, f_got, into, out, up, down, square = refs
-    c = HEAD_DIM
+def finish_kernel(count, *refs):
+    a_keep, a_got, f_keep, f_got, into, out, up, down, square = refs[1 + count :]
     g = a_keep[...].astype(F32) + a_got[...].astype(F32)
     total = jnp.sum(g * g, 0, keepdims=True).sum(1, keepdims=True)
-    heads = g.shape[1] // (4 * c)
-    parts = [[g[:, (4 * h + j) * c : (4 * h + j + 1) * c] for h in range(heads)] for j in range(4)]
+    width = g.shape[1] // 4
     for j in range(3):
-        into[j] = jnp.concatenate(parts[j], 1)
-    out[...] = jnp.concatenate(parts[3], 1).T
+        into[j] = g[:, j * width : (j + 1) * width]
+    out[...] = g[:, 3 * width :].T
     g = f_keep[...].astype(F32) + f_got[...].astype(F32)
     total = total + jnp.sum(g * g, 0, keepdims=True).sum(1, keepdims=True)
     for i in range(g.shape[1] // (2 * FF_BLOCK)):
         here = slice(i * FF_BLOCK, (i + 1) * FF_BLOCK)
         up[:, here] = g[:, 2 * i * FF_BLOCK : (2 * i + 1) * FF_BLOCK]
-        down[here] = g[:, (2 * i + 1) * FF_BLOCK : (2 * i + 2) * FF_BLOCK].T
+        down[:, here] = g[:, (2 * i + 1) * FF_BLOCK : (2 * i + 2) * FF_BLOCK]
     square[...] = total
 
 
-def finish(a_pair, f_pair, token):
+def finish(l, before, a_pair, f_pair, token):
     rows, width = a_pair[0].shape
     hidden = f_pair[0].shape[1] // 2
     values = (*a_pair, *f_pair)
-    outs = [(3, rows, width // 4), (width // 4, rows), (rows, hidden), (hidden, rows), (1, 1)]
+    outs = [(3, rows, width // 4), (width // 4, rows), (rows, hidden), (rows, hidden)]
+
+    def layer_spec(o):
+        return pl.BlockSpec((None, *o), lambda i: (l,) + (0,) * len(o))
+
+    anywhere = pl.BlockSpec(memory_space=pl.ANY)
     return pl.pallas_call(
-        finish_kernel,
+        functools.partial(finish_kernel, len(before)),
         grid=(1,),
-        in_specs=[pl.BlockSpec(memory_space=pl.ANY)] + [full(v) for v in values],
-        out_specs=[spec_of(o) for o in outs],
-        out_shape=[jax.ShapeDtypeStruct(o, F32) for o in outs],
+        in_specs=[anywhere] * (1 + len(before)) + [full(v) for v in values],
+        out_specs=[layer_spec(o) for o in outs] + [spec_of((1, 1))],
+        out_shape=[jax.ShapeDtypeStruct((LAYERS, *o), F32) for o in outs] + [jax.ShapeDtypeStruct((1, 1), F32)],
+        input_output_aliases={1 + i: i for i in range(len(before))},
         compiler_params=params(),
         cost_estimate=NO_COST,
         name="finish",
-    )(token, *values)
+    )(token, *before, *values)
+
+
+def adam_kernel(clip_ref, *refs):
+    clip = clip_ref[0]
+    for kind in range(7):
+        weight, grad, first, second = (refs[i * 7 + kind] for i in range(4))
+        new_first, new_second, new_weight = (refs[28 + i * 7 + kind] for i in range(3))
+
+        def update():
+            g = grad[...] * clip
+            new_first[...], new_second[...], new_weight[...] = adam(
+                weight[...], g, first[...], second[...], RATES[kind], DECAYS[kind]
+            )
+
+        if kind < 4:
+            update()
+        else:
+            pl.when(pl.program_id(0) == 0)(update)
+
+
+def adam_all(clip, masters, grads, firsts, seconds):
+    def spec(value, kind):
+        if kind < 4:
+            rest = value.shape[1:]
+            return pl.BlockSpec((None, *rest), lambda i: (i,) + (0,) * len(rest))
+        return full(value)
+
+    specs = [spec(value, kind) for kind, value in enumerate(masters)]
+    outs = pl.pallas_call(
+        adam_kernel,
+        grid=(LAYERS,),
+        in_specs=[FLAG] + specs * 4,
+        out_specs=specs * 3,
+        out_shape=[jax.ShapeDtypeStruct(v.shape, F32) for v in masters] * 3,
+        compiler_params=params(),
+        name="adam",
+    )(clip.reshape(1), *masters, *grads, *firsts, *seconds)
+    return tuple(outs)
 
 
 def adam(weight, grad, first, second, rate, decay):
@@ -547,14 +598,11 @@
     tokens = pixels.shape[0]
     total_images = images * lax.axis_size("dp")
 
-    heads = attend_in.shape[3] // HEAD_DIM
     hidden = hidden_up.shape[2]
     width = attend_out.shape[2] * lax.axis_size("dp")
 
     def attn_unit(l):
-        into = attend_in[l].astype(BF).reshape(3, rows, heads, HEAD_DIM)
-        out = attend_out[l].T.astype(BF).reshape(1, rows, heads, HEAD_DIM)
-        return jnp.concatenate([into, out], 0).transpose(1, 2, 0, 3).reshape(rows, -1)
+        return jnp.concatenate([attend_in[l, j].astype(BF) for j in range(3)] + [attend_out[l].astype(BF).T], 1)
 
     def ff_unit(l):
         up = hidden_up[l].astype(BF).reshape(rows, -1, 1, FF_BLOCK)
@@ -563,6 +611,10 @@
 
     half = class_head.shape[1] // 2
     head_unit = lax.dynamic_slice_in_dim(class_head.astype(BF), inner * half, half, 1)
+    teach = jax.nn.log_softmax(teacher_logits, -1)
+    teach = lax.dynamic_slice_in_dim(teach, inner * half, half, 1)
+    upper = lax.optimization_barrier(teach.astype(BF))
+    head_unit = jnp.concatenate([head_unit, upper, (teach - upper.astype(F32)).astype(BF)], 0)
 
     flag = inner.reshape(1)
 
@@ -618,8 +670,6 @@
         return jnp.where(inner == 0, jnp.concatenate([own, other], 1), jnp.concatenate([other, own], 1))
 
     dp_order = high + [low]
-    teach = jax.nn.log_softmax(teacher_logits, -1)
-    teach = lax.dynamic_slice_in_dim(teach, inner * half, half, 1)
     attn = [attn_unit(l) for l in range(LAYERS)]
     ff = [ff_unit(l) for l in range(LAYERS)]
 
@@ -646,9 +696,9 @@
     norms = patch[:, pixel_count:].T.astype(F32).reshape(7, 2, width)
     part = nt(jnp.concatenate(pix, 0), patch[:, :pixel_count]).astype(BF)
     part = of_inner(part, inner).astype(F32) + swap(of_inner(part, 1 - inner), INNER).astype(F32)
-    part, theirs = part[:MOST], steps.add(part[MOST:].astype(BF))
-    steps.next()
-    part = part + steps.swap(theirs, OUTER).astype(F32)
+    part, theirs = part[:MOST], steps.swap(part[MOST:].astype(BF), OUTER)
+    steps.next()
+    part = steps.tie(part) + theirs.astype(F32)
     attn[0] = across(attn[0])
     ff[0] = near(ff[0])
     attn[1] = flat(over(attn[1], two))
@@ -685,20 +735,20 @@
     ff[1] = across(ff[1])
     attn[2] = near(attn[2])
     ff[2] = flat(over(ff[2], two))
+    head = over(head_unit, one)
     adds = run_attn(1, adds)
     steps.next()
     attn[2] = across(attn[2])
     ff[2] = near(ff[2])
-    head = over(head_unit, one)
+    head = over(head, two)
     adds = run_ff(1, adds)
     steps.next()
     ff[2] = across(ff[2])
-    teach = over(teach, one)
-    head = over(head, two)
+    head = over(head, [low]).reshape(-1, rows + 2 * images, half)
     adds = run_attn(2, adds)
     steps.next()
-    teach = over(over(teach, two), [low])
-    head = over(head, [low]).reshape(width, half)
+    teach = head[:, rows : rows + images].astype(F32) + head[:, rows + images :].astype(F32)
+    head = head[:, :rows].reshape(width, half)
     adds = run_ff(2, adds)
     x = sum(v.astype(F32) for v in adds)
 
@@ -816,8 +866,7 @@
     steps.add(g_patch)
     g["patch"] = (g_patch[:mid], g_patch[mid:])
     token = g_norms[0]
-    done = [None] * LAYERS
-    done[2] = finish(g["attn", 2], g["ff", 2], token)
+    *done, square_two = finish(2, [], g["attn", 2], g["ff", 2], token)
     steps.next()
     near_low("patch")
     near_last(("attn", 0))
@@ -827,7 +876,7 @@
     g_head = g_head + steps.swap(g_head, OUTER)
     g_norm = steps.tie(jnp.concatenate([g_norms[i] for i in range(6)] + [g_final], 0))
     g_norm = 0.5 * (g_norm + swap(g_norm, INNER))
-    done[1] = finish(g["attn", 1], g["ff", 1], g_patch)
+    *done, square_one = finish(1, done, g["attn", 1], g["ff", 1], g_patch)
     steps.next()
     far_first(("attn", 0), "patch")
     far_last(("ff", 0))
@@ -841,12 +890,12 @@
     for bit in high[::-1]:
         g_norm = g_norm[0] + steps.swap(g_norm[1], bit)
     g_norm = g_norm.reshape(7, 2, rows)
-    done[0] = finish(g["attn", 0], g["ff", 0], g_patch)
+    *done, square_zero = finish(0, done, g["attn", 0], g["ff", 0], g_patch)
     g_patch = g["patch"][0].astype(F32) + g["patch"][1].astype(F32)
 
-    grads = tuple(jnp.stack([layer[i] for layer in done]) for i in range(4)) + (g_patch.T, g_head, g_norm)
+    grads = (*done, g_patch, g_head, g_norm)
     first_model = (lax.axis_index("mp") == 0).astype(F32)
-    squares = sum(layer[4][0, 0] for layer in done) + jnp.sum(g_patch * g_patch) + first_model * (
+    squares = (square_two + square_one + square_zero)[0, 0] + jnp.sum(g_patch * g_patch) + first_model * (
         jnp.sum(g_head * g_head) + jnp.sum(g_norm * g_norm)
     )
     sums = jnp.stack([squares, loss_local * (outer >= 0)])
@@ -862,12 +911,13 @@
     loss = sums[1]
     grad_norm = jnp.sqrt(sums[0])
     clip = jnp.minimum(1.0, CLIP / grad_norm)
-    results = []
-    for kind in range(7):
-        results.append(
-            adam(masters[kind], grads[kind] * clip, firsts[kind], seconds[kind], RATES[kind], DECAYS[kind])
-        )
-    return (loss, grad_norm) + tuple(r[i] for i in range(3) for r in results)
+
+    def turned(values):
+        return (*values[:3], values[3].swapaxes(1, 2), values[4].T, *values[5:])
+
+    masters, firsts, seconds = turned(masters), turned(firsts), turned(seconds)
+    outs = adam_all(clip, masters, grads, firsts, seconds)
+    return (loss, grad_norm) + turned(outs[:7]) + turned(outs[7:14]) + turned(outs[14:])
 
 
 def solution(mesh):

time: 734 us -> 662 us (0.902)
  other arithmetic: 99.6 us -> 69.2 us
  Pallas kernels: 248 us -> 228 us
  local copies, waits for them, and re-layouts: 57.8 us -> 37.9 us
    pallas_call x3, Pallas kernels: 88 us -> 69.3 us  [attn_backward(): pl.pallas_call(functools.partial(attn_back_kernel, len(back)), grid=(step...]
    sub x8 -> x0, other arithmetic: 16.3 us -> none  [the longest x7 16.2 us: adam(): return (first, second, weight - rate * (update + decay * weight))]
    pallas_call x3, Pallas kernels: 54.2 us -> 40.5 us  [attn_forward(): pl.pallas_call(functools.partial(attn_fwd_kernel, len(adds)), grid=(steps...]
    pallas_call x3 -> x4, Pallas kernels: 7.36 us -> 19.6 us  [the longest x1 12.5 us: adam_all(): pl.pallas_call(adam_kernel, grid=(LAYERS,), in_specs=[FLAG] + specs * 4,...]
    unnamed x247 -> x170, local copies, waits for them, and re-layouts: 26.6 us -> 15.3 us
    ppermute x106 -> x103, waiting for transfers between devices: 204 us -> 208 us  [swap(): return lax.ppermute(value, AXES, pairs)]
    ppermute x106 -> x103, starting transfers between devices: 93.8 us -> 91.1 us  [swap(): return lax.ppermute(value, AXES, pairs)]
  transfers between devices with their start and end apart: 106 -> 103, of which waited for: 38 -> 40; matrix products, arithmetic and copies ran while one was open for 16% -> 13% of each run, Pallas kernels for 31% -> 30%
where the time goes in v4:
time: 662 us; the launch traced here: 656 us
  Pallas kernels  228 us (34%)
  waiting for transfers between devices  208 us (31%)
  starting transfers between devices  91.1 us (14%)
  other arithmetic  69.2 us (10%)
  local copies, waits for them, and re-layouts  37.9 us (6%)
  between operations  13 us (2%)
  matrix products  9.47 us (1%)
    ppermute x103, waiting for transfers between devices, swap(): return lax.ppermute(value, AXES, pairs)  208 us
    ppermute x103, starting transfers between devices, swap(): return lax.ppermute(value, AXES, pairs)  91.1 us
    pallas_call x3, Pallas kernels, attn_backward(): pl.pallas_call(functools.partial(attn_back_kernel, len(back)), grid=(step...  69.3 us
    pallas_call x3, Pallas kernels, ff_backward(): pl.pallas_call(functools.partial(ff_back_kernel, len(back)), grid=(steps,...  57 us
    pallas_call x3, Pallas kernels, attn_forward(): pl.pallas_call(functools.partial(attn_fwd_kernel, len(adds)), grid=(steps...  40.5 us
    pallas_call x3, Pallas kernels, ff_forward(): pl.pallas_call(functools.partial(ff_fwd_kernel, len(adds)), grid=(steps,)...  36.8 us
    another operation x19, other arithmetic, over(): unit = jnp.stack([unit, steps.swap(unit, bit)])  16.6 us
    unnamed x170, local copies, waits for them, and re-layouts  15.3 us
  transfers between devices with their start and end apart: 103, of which 40 were waited for; matrix products, arithmetic and copies ran while one was open for 13% of the time, Pallas kernels for 30%

profile of v4, /device:TPU:0, one launch (start us, length us, event | category | flops | bytes accessed | tf_op | source)
XLA Modules:
  0.0 656.5 jit_solution(14922777979089375351)
XLA Ops:
  42.5 11.8 %collective-permute-done.5 = bf16[2,96,768]{1,2,0:T(8,128)(2,1)} collective-permute-done((bf16[2,96,768]{1,2,0:T(8,128)(2,1)}, bf16[2,96,768]{1,2,0:T(8,128)(2,1)}, u32[]{:S(2)}, u32[]{:S(2)}) %collective-permute-start.5) | collective-permute-done | bytes 294944 | tf_op jit(solution)/shard_map/ppermute | solution.py:46
  68.9 12.8 %collective-permute-done.9 = bf16[96,768]{0,1:T(8,128)(2,1)S(1)} collective-permute-done((bf16[96,768]{0,1:T(8,128)(2,1)S(1)}, bf16[96,768]{0,1:T(8,128)(2,1)S(1)}, u32[]{:S(2)}, u32[]{:S(2)}) %collective-permute-start.9) | collective-permute-done | bytes 147488 | tf_op jit(solution)/shard_map/ppermute | solution.py:46
  81.7 10.6 %collective-permute-done.8 = bf16[2,96,1536]{2,1,0:T(8,128)(2,1)S(1)} collective-permute-done((bf16[2,96,1536]{2,1,0:T(8,128)(2,1)S(1)}, bf16[2,96,1536]{2,1,0:T(8,128)(2,1)S(1)}, u32[]{:S(2)}, u32[]{:S(2)}) %collective-permute-start.8) | collective-permute-done | bytes 589856 | tf_op jit(solution)/shard_map/ppermute | solution.py:46
  105.1 11.9 %collective-permute-done.17 = bf16[2,96,768]{1,2,0:T(8,128)(2,1)} collective-permute-done((bf16[2,96,768]{1,2,0:T(8,128)(2,1)}, bf16[2,96,768]{1,2,0:T(8,128)(2,1)}, u32[]{:S(2)}, u32[]{:S(2)}) %collective-permute-start.17) | collective-permute-done | bytes 294944 | tf_op jit(solution)/shard_map/ppermute | solution.py:46
  117.0 10.5 %collective-permute-done.14.refs_8_.refs_14_ = bf16[384,768]{1,0:T(8,128)(2,1)} collective-permute-done((bf16[384,768]{1,0:T(8,128)(2,1)}, bf16[384,768]{1,0:T(8,128)(2,1)}, u32[]{:S(2)}, u32[]{:S(2)}) %collective-permute-start.14) | collective-permute-done | bytes 589856 | tf_op jit(solution)/shard_map/ppermute | solution.py:46
  139.1 13.0 %attn_forward.3 = (f32[576,768]{1,0:T(8,128)}, bf16[2,576,768]{2,1,0:T(8,128)(2,1)}, bf16[576,768]{1,0:T(8,128)(2,1)}) custom-call(s32[1]{0:T(128)} %bitcast.refs_0_, f32[576,768]{1,0:T(8,128)} %maximum_select_fusion.refs_1_, f32[2,768]{1,0:T(2,128)} %get-tuple-element.469.refs_2_.refs_7_.norm, s32[576,1]{1,0:T(8,128)} %broadcast_in_dim.27.refs_3_.refs_5_.refs_8_, ...), custom_call_target="tpu_custom_call" | custom-call | flops 1000000 | bytes 10000 | tf_op jit(solution)/shard_map/attn_forward/pallas_call | solution.py:249
  167.9 12.3 %ff_forward.3 = (f32[576,768]{1,0:T(8,128)}, bf16[576,768]{1,0:T(8,128)(2,1)}) custom-call(s32[1]{0:T(128)} %bitcast.refs_0_, f32[576,768]{1,0:T(8,128)} %get-tuple-element.222.refs_1_.refs_6_.value, bf16[576,768]{1,0:T(8,128)(2,1)} %get-tuple-element.221.refs_2_, bf16[576,768]{1,0:T(8,128)(2,1)} %copy-done.39, ...), custom_call_target="tpu_custom_call" | custom-call | flops 1000000 | bytes 10000 | tf_op jit(solution)/shard_map/ff_forward/pallas_call | solution.py:304
  184.1 11.8 %collective-permute-done.25.refs_10_.refs_14_ = bf16[384,768]{1,0:T(8,128)(2,1)S(1)} collective-permute-done((bf16[384,768]{1,0:T(8,128)(2,1)S(1)}, bf16[384,768]{1,0:T(8,128)(2,1)S(1)}, u32[]{:S(2)}, u32[]{:S(2)}) %collective-permute-start.25) | collective-permute-done | bytes 589856 | tf_op jit(solution)/shard_map/ppermute | solution.py:46
  204.1 13.6 %attn_forward.4 = (f32[576,768]{1,0:T(8,128)}, bf16[2,576,768]{2,1,0:T(8,128)(2,1)}, bf16[576,768]{1,0:T(8,128)(2,1)}) custom-call(s32[1]{0:T(128)} %bitcast.refs_0_, f32[576,768]{1,0:T(8,128)} %get-tuple-element.229.refs_1_.refs_6_.refs_2_, bf16[576,768]{1,0:T(8,128)(2,1)} %get-tuple-element.228.refs_2_, bf16[576,768]{1,0:T(8,128)(2,1)} %collective-permute-done.30.refs_3_, ...), custom_call_target="tpu_custom_call" | custom-call | flops 1000000 | bytes 10000 | tf_op jit(solution)/shard_map/attn_forward/pallas_call | solution.py:249
  217.9 10.9 %collective-permute-done.34 = bf16[2,96,1536]{2,1,0:T(8,128)(2,1)} collective-permute-done((bf16[2,96,1536]{2,1,0:T(8,128)(2,1)}, bf16[2,96,1536]{2,1,0:T(8,128)(2,1)}, u32[]{:S(2)}, u32[]{:S(2)}) %collective-permute-start.34) | collective-permute-done | bytes 589856 | tf_op jit(solution)/shard_map/ppermute | solution.py:46
  238.0 12.3 %ff_forward.4 = (f32[576,768]{1,0:T(8,128)}, bf16[576,768]{1,0:T(8,128)(2,1)}) custom-call(s32[1]{0:T(128)} %bitcast.refs_0_, f32[576,768]{1,0:T(8,128)} %get-tuple-element.236.refs_1_.refs_6_.refs_2_, bf16[576,768]{1,0:T(8,128)(2,1)} %get-tuple-element.235.refs_2_, bf16[576,768]{1,0:T(8,128)(2,1)} %copy-done.40, ...), custom_call_target="tpu_custom_call" | custom-call | flops 1000000 | bytes 10000 | tf_op jit(solution)/shard_map/ff_forward/pallas_call | solution.py:304
  251.5 12.6 %collective-permute-done.40 = bf16[2,112,500]{2,1,0:T(8,128)(2,1)S(1)} collective-permute-done((bf16[2,112,500]{2,1,0:T(8,128)(2,1)S(1)}, bf16[2,112,500]{2,1,0:T(8,128)(2,1)S(1)}, u32[]{:S(2)}, u32[]{:S(2)}) %collective-permute-start.40) | collective-permute-done | bytes 224032 | tf_op jit(solution)/shard_map/ppermute | solution.py:46
  269.9 13.8 %attn_forward.5 = (f32[576,768]{1,0:T(8,128)}, bf16[2,576,768]{2,1,0:T(8,128)(2,1)}, bf16[576,768]{1,0:T(8,128)(2,1)}) custom-call(s32[1]{0:T(128)} %bitcast.refs_0_, f32[576,768]{1,0:T(8,128)} %get-tuple-element.242.refs_1_.refs_6_.refs_2_, bf16[576,768]{1,0:T(8,128)(2,1)} %get-tuple-element.241.refs_2_, bf16[576,768]{1,0:T(8,128)(2,1)} %copy-done.44, ...), custom_call_target="tpu_custom_call" | custom-call | flops 1000000 | bytes 10000 | tf_op jit(solution)/shard_map/attn_forward/pallas_call | solution.py:249
  285.1 11.8 %collective-permute-done.43 = bf16[2,2,112,500]{3,2,1,0:T(8,128)(2,1)S(1)} collective-permute-done((bf16[2,2,112,500]{3,2,1,0:T(8,128)(2,1)S(1)}, bf16[2,2,112,500]{3,2,1,0:T(8,128)(2,1)S(1)}, u32[]{:S(2)}, u32[]{:S(2)}) %collective-permute-start.43) | collective-permute-done | bytes 448032 | tf_op jit(solution)/shard_map/ppermute | solution.py:46
  298.1 12.2 %ff_forward.5 = (f32[576,768]{1,0:T(8,128)}, bf16[576,768]{1,0:T(8,128)(2,1)}) custom-call(s32[1]{0:T(128)} %bitcast.refs_0_, f32[576,768]{1,0:T(8,128)} %get-tuple-element.247.refs_1_.refs_6_.refs_2_, bf16[576,768]{1,0:T(8,128)(2,1)} %get-tuple-element.246.refs_2_, bf16[576,768]{1,0:T(8,128)(2,1)} %copy-done.42, ...), custom_call_target="tpu_custom_call" | custom-call | flops 1000000 | bytes 10000 | tf_op jit(solution)/shard_map/ff_forward/pallas_call | solution.py:304
  323.1 17.6 %ff_backward.3 = (f32[576,768]{1,0:T(8,128)}, bf16[384,1536]{1,0:T(8,128)(2,1)}, bf16[384,1536]{1,0:T(8,128)(2,1)}, bf16[384,1536]{1,0:T(8,128)(2,1)}, bf16[384,...) custom-call(s32[1]{0:T(128)} %bitcast.refs_0_, f32[576,768]{1,0:T(8,128)} %fusion.35.refs_1_, ...), custom_call_target="tpu_custom_call" | custom-call | flops 1000000 | bytes 10000 | tf_op jit(solution)/shard_map/ff_backward/pallas_call | solution.py:385
  345.2 23.1 %attn_backward.3 = (f32[576,768]{1,0:T(8,128)}, bf16[384,768]{1,0:T(8,128)(2,1)}, bf16[384,768]{1,0:T(8,128)(2,1)}, bf16[384,768]{1,0:T(8,128)(2,1)}, bf16[384,7...) custom-call(s32[1]{0:T(128)} %bitcast.refs_0_, f32[576,768]{1,0:T(8,128)} %get-tuple-element.252.refs_1_, ...), custom_call_target="tpu_custom_call" | custom-call | flops 1000000 | bytes 10000 | tf_op jit(solution)/shard_map/attn_backward/pallas_call | solution.py:458
  374.2 19.6 %ff_backward.4 = (f32[576,768]{1,0:T(8,128)}, bf16[384,1536]{1,0:T(8,128)(2,1)}, bf16[384,1536]{1,0:T(8,128)(2,1)}, bf16[384,1536]{1,0:T(8,128)(2,1)}, bf16[384,...) custom-call(s32[1]{0:T(128)} %bitcast.refs_0_, f32[576,768]{1,0:T(8,128)} %get-tuple-element.261.refs_1_, ...), custom_call_target="tpu_custom_call" | custom-call | flops 1000000 | bytes 10000 | tf_op jit(solution)/shard_map/ff_backward/pallas_call | solution.py:385
  405.3 23.1 %attn_backward.4 = (f32[576,768]{1,0:T(8,128)}, bf16[384,768]{1,0:T(8,128)(2,1)}, bf16[384,768]{1,0:T(8,128)(2,1)}, bf16[384,768]{1,0:T(8,128)(2,1)}, bf16[384,7...) custom-call(s32[1]{0:T(128)} %bitcast.refs_0_, f32[576,768]{1,0:T(8,128)} %get-tuple-element.271.refs_1_, ...), custom_call_target="tpu_custom_call" | custom-call | flops 1000000 | bytes 10000 | tf_op jit(solution)/shard_map/attn_backward/pallas_call | solution.py:458
  442.5 19.8 %ff_backward.5 = (f32[576,768]{1,0:T(8,128)}, bf16[384,1536]{1,0:T(8,128)(2,1)}, bf16[384,1536]{1,0:T(8,128)(2,1)}, bf16[384,1536]{1,0:T(8,128)(2,1)}, bf16[384,...) custom-call(s32[1]{0:T(128)} %bitcast.refs_0_, f32[576,768]{1,0:T(8,128)} %get-tuple-element.283.refs_1_, ...), custom_call_target="tpu_custom_call" | custom-call | flops 1000000 | bytes 10000 | tf_op jit(solution)/shard_map/ff_backward/pallas_call | solution.py:385
  472.1 23.2 %attn_backward.5 = (f32[576,768]{1,0:T(8,128)}, bf16[384,768]{1,0:T(8,128)(2,1)}, bf16[384,768]{1,0:T(8,128)(2,1)}, bf16[384,768]{1,0:T(8,128)(2,1)}, bf16[384,7...) custom-call(s32[1]{0:T(128)} %bitcast.refs_0_, f32[576,768]{1,0:T(8,128)} %get-tuple-element.295.refs_1_, ...), custom_call_target="tpu_custom_call" | custom-call | flops 1000000 | bytes 10000 | tf_op jit(solution)/shard_map/attn_backward/pallas_call | solution.py:458
  564.1 12.8 %collective-permute-done.86 = bf16[2,96,1536]{2,1,0:T(8,128)(2,1)S(1)} collective-permute-done((bf16[2,96,1536]{2,1,0:T(8,128)(2,1)S(1)}, bf16[2,96,1536]{2,1,0:T(8,128)(2,1)S(1)}, u32[]{:S(2)}, u32[]{:S(2)}) %collective-permute-start.86) | collective-permute-done | bytes 589856 | tf_op jit(solution)/shard_map/ppermute | solution.py:46
  585.5 10.5 %collective-permute-done.89 = bf16[1,96,1536]{2,1,0:T(8,128)(2,1)S(1)} collective-permute-done((bf16[1,96,1536]{2,1,0:T(8,128)(2,1)}, bf16[1,96,1536]{2,1,0:T(8,128)(2,1)S(1)}, u32[]{:S(2)}, u32[]{:S(2)}) %collective-permute-start.89) | collective-permute-done | bytes 294944 | tf_op jit(solution)/shard_map/ppermute | solution.py:46
  642.7 12.5 %adam.1 = (f32[3,3,96,192]{3,2,1,0:T(8,128)}, f32[3,192,96]{2,1,0:T(8,128)}, f32[3,96,768]{2,1,0:T(8,128)}, f32[3,96,768]{2,1,0:T(8,128)}, f32[96,768]{1,0:T(8,1...) custom-call(f32[1]{0:T(128)} %bitcast.125.clip_ref, ...), custom_call_target="tpu_custom_call" | custom-call | tf_op jit(solution)/shard_map/adam/pallas_call | solution.py:569
  (548 shorter events, 299.3 us)
Async XLA Ops:
  62.4 29.9 %collective-permute-start.10 = (bf16[384,768]{1,0:T(8,128)(2,1)S(1)}, bf16[384,768]{1,0:T(8,128)(2,1)}, u32[]{:S(2)}, u32[]{:S(2)}) collective-permute-start(bf16[384,768]{1,0:T(8,128)(2,1)S(1)} %bitcast.311), channel_id=1, source_target_pairs={{0,2},{1,5},{2,0},{3,7},{4,6},{5,1},{6,4},{7,3},{8,10},{9,13},{10,... | collective-permute-start | bytes 1769480 | tf_op jit(solution)/shard_map/ppermute | solution.py:46
  93.1 34.4 %collective-permute-start.15 = (bf16[384,1536]{1,0:T(8,128)(2,1)S(1)}, bf16[384,1536]{1,0:T(8,128)(2,1)S(1)}, u32[]{:S(2)}, u32[]{:S(2)}) collective-permute-start(bf16[384,1536]{1,0:T(8,128)(2,1)S(1)} %bitcast.294), channel_id=1, source_target_pairs={{0,2},{1,5},{2,0},{3,7},{4,6},{5,1},{6,4},{7,3},{8,10},{9,13},{10,... | collective-permute-start | bytes 3538952 | tf_op jit(solution)/shard_map/ppermute | solution.py:46
  93.7 33.8 %collective-permute-start.16 = (bf16[384,1536]{1,0:T(8,128)(2,1)S(1)}, bf16[384,1536]{1,0:T(8,128)(2,1)}, u32[]{:S(2)}, u32[]{:S(2)}) collective-permute-start(bf16[384,1536]{1,0:T(8,128)(2,1)S(1)} %bitcast.295), channel_id=1, source_target_pairs={{0,4},{1,3},{2,6},{3,1},{4,0},{5,7},{6,2},{7,5},{8,12},{9,11},{10,... | collective-permute-start | bytes 3538952 | tf_op jit(solution)/shard_map/ppermute | solution.py:46
  95.2 32.3 %collective-permute-start.14 = (bf16[384,768]{1,0:T(8,128)(2,1)}, bf16[384,768]{1,0:T(8,128)(2,1)}, u32[]{:S(2)}, u32[]{:S(2)}) collective-permute-start(bf16[384,768]{1,0:T(8,128)(2,1)} %collective-permute-done.10.refs_6_.refs_12_), channel_id=1, source_target_pairs={{0,4},{1,3},{2,6},{3,1},{4,0},{5,7},{6,2},{7,5},{8,12},{9,11},{10,... | collective-permute-start | bytes 1769480 | tf_op jit(solution)/shard_map/ppermute | solution.py:46
  127.5 32.8 %collective-permute-start.19 = (bf16[384,1536]{1,0:T(8,128)(2,1)S(1)}, bf16[384,1536]{1,0:T(8,128)(2,1)}, u32[]{:S(2)}, u32[]{:S(2)}) collective-permute-start(bf16[384,1536]{1,0:T(8,128)(2,1)S(1)} %collective-permute-done.15.refs_6_.refs_9_), channel_id=1, source_target_pairs={{0,4},{1,3},{2,6},{3,1},{4,0},{5,7},{6,2},{7,5},{8,12},{9,11},{10,... | collective-permute-start | bytes 3538952 | tf_op jit(solution)/shard_map/ppermute | solution.py:46
  161.2 34.7 %collective-permute-start.26 = (bf16[384,1536]{1,0:T(8,128)(2,1)S(1)}, bf16[384,1536]{1,0:T(8,128)(2,1)S(1)}, u32[]{:S(2)}, u32[]{:S(2)}) collective-permute-start(bf16[384,1536]{1,0:T(8,128)(2,1)S(1)} %bitcast.298), channel_id=1, source_target_pairs={{0,2},{1,5},{2,0},{3,7},{4,6},{5,1},{6,4},{7,3},{8,10},{9,13},{10,... | collective-permute-start | bytes 3538952 | tf_op jit(solution)/shard_map/ppermute | solution.py:46
  162.6 33.2 %collective-permute-start.27 = (bf16[384,1536]{1,0:T(8,128)(2,1)S(1)}, bf16[384,1536]{1,0:T(8,128)(2,1)S(1)}, u32[]{:S(2)}, u32[]{:S(2)}) collective-permute-start(bf16[384,1536]{1,0:T(8,128)(2,1)S(1)} %bitcast.299), channel_id=1, source_target_pairs={{0,4},{1,3},{2,6},{3,1},{4,0},{5,7},{6,2},{7,5},{8,12},{9,11},{10,... | collective-permute-start | bytes 3538952 | tf_op jit(solution)/shard_map/ppermute | solution.py:46
  163.4 32.4 %collective-permute-start.25 = (bf16[384,768]{1,0:T(8,128)(2,1)S(1)}, bf16[384,768]{1,0:T(8,128)(2,1)S(1)}, u32[]{:S(2)}, u32[]{:S(2)}) collective-permute-start(bf16[384,768]{1,0:T(8,128)(2,1)S(1)} %collective-permute-done.20.refs_8_.refs_12_), channel_id=1, source_target_pairs={{0,4},{1,3},{2,6},{3,1},{4,0},{5,7},{6,2},{7,5},{8,12},{9,11},{10,... | collective-permute-start | bytes 1769480 | tf_op jit(solution)/shard_map/ppermute | solution.py:46
  197.0 36.9 %collective-permute-start.31 = (bf16[384,1536]{1,0:T(8,128)(2,1)S(1)}, bf16[384,1536]{1,0:T(8,128)(2,1)}, u32[]{:S(2)}, u32[]{:S(2)}) collective-permute-start(bf16[384,1536]{1,0:T(8,128)(2,1)S(1)} %collective-permute-done.26.refs_6_.refs_9_), channel_id=1, source_target_pairs={{0,4},{1,3},{2,6},{3,1},{4,0},{5,7},{6,2},{7,5},{8,12},{9,11},{10,... | collective-permute-start | bytes 3538952 | tf_op jit(solution)/shard_map/ppermute | solution.py:46
  201.5 32.4 %collective-permute-start.32 = (bf16[384,768]{1,0:T(8,128)(2,1)S(1)}, bf16[384,768]{1,0:T(8,128)(2,1)S(1)}, u32[]{:S(2)}, u32[]{:S(2)}) collective-permute-start(bf16[384,768]{1,0:T(8,128)(2,1)S(1)} %bitcast.319), channel_id=1, source_target_pairs={{0,2},{1,5},{2,0},{3,7},{4,6},{5,1},{6,4},{7,3},{8,10},{9,13},{10,... | collective-permute-start | bytes 1769480 | tf_op jit(solution)/shard_map/ppermute | solution.py:46
  202.9 31.1 %collective-permute-start.33 = (bf16[384,768]{1,0:T(8,128)(2,1)S(1)}, bf16[384,768]{1,0:T(8,128)(2,1)S(1)}, u32[]{:S(2)}, u32[]{:S(2)}) collective-permute-start(bf16[384,768]{1,0:T(8,128)(2,1)S(1)} %bitcast.320), channel_id=1, source_target_pairs={{0,4},{1,3},{2,6},{3,1},{4,0},{5,7},{6,2},{7,5},{8,12},{9,11},{10,... | collective-permute-start | bytes 1769480 | tf_op jit(solution)/shard_map/ppermute | solution.py:46
  234.6 33.4 %collective-permute-start.38 = (bf16[384,1536]{1,0:T(8,128)(2,1)S(1)}, bf16[384,1536]{1,0:T(8,128)(2,1)S(1)}, u32[]{:S(2)}, u32[]{:S(2)}) collective-permute-start(bf16[384,1536]{1,0:T(8,128)(2,1)S(1)} %bitcast.302), channel_id=1, source_target_pairs={{0,2},{1,5},{2,0},{3,7},{4,6},{5,1},{6,4},{7,3},{8,10},{9,13},{10,... | collective-permute-start | bytes 3538952 | tf_op jit(solution)/shard_map/ppermute | solution.py:46
  235.1 32.9 %collective-permute-start.39 = (bf16[384,1536]{1,0:T(8,128)(2,1)S(1)}, bf16[384,1536]{1,0:T(8,128)(2,1)S(1)}, u32[]{:S(2)}, u32[]{:S(2)}) collective-permute-start(bf16[384,1536]{1,0:T(8,128)(2,1)S(1)} %bitcast.303), channel_id=1, source_target_pairs={{0,4},{1,3},{2,6},{3,1},{4,0},{5,7},{6,2},{7,5},{8,12},{9,11},{10,... | collective-permute-start | bytes 3538952 | tf_op jit(solution)/shard_map/ppermute | solution.py:46
  236.0 32.0 %collective-permute-start.37 = (bf16[384,768]{1,0:T(8,128)(2,1)S(1)}, bf16[384,768]{1,0:T(8,128)(2,1)S(1)}, u32[]{:S(2)}, u32[]{:S(2)}) collective-permute-start(bf16[384,768]{1,0:T(8,128)(2,1)S(1)} %collective-permute-done.32.refs_8_.refs_12_), channel_id=1, source_target_pairs={{0,4},{1,3},{2,6},{3,1},{4,0},{5,7},{6,2},{7,5},{8,12},{9,11},{10,... | collective-permute-start | bytes 1769480 | tf_op jit(solution)/shard_map/ppermute | solution.py:46
  268.0 28.8 %collective-permute-start.42 = (bf16[384,1536]{1,0:T(8,128)(2,1)S(1)}, bf16[384,1536]{1,0:T(8,128)(2,1)S(1)}, u32[]{:S(2)}, u32[]{:S(2)}) collective-permute-start(bf16[384,1536]{1,0:T(8,128)(2,1)S(1)} %collective-permute-done.38.refs_6_.refs_5_), channel_id=1, source_target_pairs={{0,4},{1,3},{2,6},{3,1},{4,0},{5,7},{6,2},{7,5},{8,12},{9,11},{10,... | collective-permute-start | bytes 3538952 | tf_op jit(solution)/shard_map/ppermute | solution.py:46
  398.2 33.1 %collective-permute-start.59 = (bf16[384,1536]{1,0:T(8,128)(2,1)}, bf16[384,1536]{1,0:T(8,128)(2,1)S(1)}, u32[]{:S(2)}, u32[]{:S(2)}) collective-permute-start(bf16[384,1536]{1,0:T(8,128)(2,1)} %get-tuple-element.275), channel_id=1, source_target_pairs={{0,4},{1,3},{2,6},{3,1},{4,0},{5,7},{6,2},{7,5},{8,12},{9,11},{10,... | collective-permute-start | bytes 3538952 | tf_op jit(solution)/shard_map/ppermute | solution.py:46
  400.5 29.0 %collective-permute-start.62 = (bf16[2,96,1536]{2,1,0:T(8,128)(2,1)}, bf16[2,96,1536]{2,1,0:T(8,128)(2,1)}, u32[]{:S(2)}, u32[]{:S(2)}) collective-permute-start(bf16[2,96,1536]{2,1,0:T(8,128)(2,1)} %pad_maximum_fusion.15), channel_id=1, source_target_pairs={{0,16},{1,17},{2,18},{3,19},{4,20},{5,21},{6,22},{7,23},{8,24},{9,... | collective-permute-start | bytes 1769480 | tf_op jit(solution)/shard_map/ppermute | solution.py:46
  402.4 31.1 %collective-permute-start.60 = (bf16[384,1536]{1,0:T(8,128)(2,1)}, bf16[384,1536]{1,0:T(8,128)(2,1)S(1)}, u32[]{:S(2)}, u32[]{:S(2)}) collective-permute-start(bf16[384,1536]{1,0:T(8,128)(2,1)} %get-tuple-element.277), channel_id=1, source_target_pairs={{0,4},{1,3},{2,6},{3,1},{4,0},{5,7},{6,2},{7,5},{8,12},{9,11},{10,... | collective-permute-start | bytes 3538952 | tf_op jit(solution)/shard_map/ppermute | solution.py:46
  433.5 29.1 %collective-permute-start.66 = (bf16[384,1536]{1,0:T(8,128)(2,1)S(1)}, bf16[384,1536]{1,0:T(8,128)(2,1)S(1)}, u32[]{:S(2)}, u32[]{:S(2)}) collective-permute-start(bf16[384,1536]{1,0:T(8,128)(2,1)S(1)} %add_convert_fusion.3), channel_id=1, source_target_pairs={{0,2},{1,5},{2,0},{3,7},{4,6},{5,1},{6,4},{7,3},{8,10},{9,13},{10,... | collective-permute-start | bytes 3538952 | tf_op jit(solution)/shard_map/ppermute | solution.py:46
  462.7 32.6 %collective-permute-start.72 = (bf16[384,768]{1,0:T(8,128)(2,1)S(1)}, bf16[384,768]{1,0:T(8,128)(2,1)S(1)}, u32[]{:S(2)}, u32[]{:S(2)}) collective-permute-start(bf16[384,768]{1,0:T(8,128)(2,1)S(1)} %add_convert_fusion.10), channel_id=1, source_target_pairs={{0,2},{1,5},{2,0},{3,7},{4,6},{5,1},{6,4},{7,3},{8,10},{9,13},{10,... | collective-permute-start | bytes 1769480 | tf_op jit(solution)/shard_map/ppermute | solution.py:46
  465.0 32.7 %collective-permute-start.73 = (bf16[2,96,1536]{2,1,0:T(8,128)(2,1)S(1)}, bf16[2,96,1536]{2,1,0:T(8,128)(2,1)S(1)}, u32[]{:S(2)}, u32[]{:S(2)}) collective-permute-start(bf16[2,96,1536]{2,1,0:T(8,128)(2,1)S(1)} %pad_maximum_fusion.16), channel_id=1, source_target_pairs={{0,16},{1,17},{2,18},{3,19},{4,20},{5,21},{6,22},{7,23},{8,24},{9,... | collective-permute-start | bytes 1769480 | tf_op jit(solution)/shard_map/ppermute | solution.py:46
  466.9 32.4 %collective-permute-start.70 = (bf16[384,1536]{1,0:T(8,128)(2,1)}, bf16[384,1536]{1,0:T(8,128)(2,1)S(1)}, u32[]{:S(2)}, u32[]{:S(2)}) collective-permute-start(bf16[384,1536]{1,0:T(8,128)(2,1)} %get-tuple-element.299), channel_id=1, source_target_pairs={{0,4},{1,3},{2,6},{3,1},{4,0},{5,7},{6,2},{7,5},{8,12},{9,11},{10,... | collective-permute-start | bytes 3538952 | tf_op jit(solution)/shard_map/ppermute | solution.py:46
  468.0 31.3 %collective-permute-start.71 = (bf16[384,1536]{1,0:T(8,128)(2,1)}, bf16[384,1536]{1,0:T(8,128)(2,1)S(1)}, u32[]{:S(2)}, u32[]{:S(2)}) collective-permute-start(bf16[384,1536]{1,0:T(8,128)(2,1)} %get-tuple-element.301), channel_id=1, source_target_pairs={{0,4},{1,3},{2,6},{3,1},{4,0},{5,7},{6,2},{7,5},{8,12},{9,11},{10,... | collective-permute-start | bytes 3538952 | tf_op jit(solution)/shard_map/ppermute | solution.py:46
  510.2 34.2 %collective-permute-start.81 = (bf16[384,1536]{1,0:T(8,128)(2,1)S(1)}, bf16[384,1536]{1,0:T(8,128)(2,1)}, u32[]{:S(2)}, u32[]{:S(2)}) collective-permute-start(bf16[384,1536]{1,0:T(8,128)(2,1)S(1)} %add_convert_fusion.1), channel_id=1, source_target_pairs={{0,2},{1,5},{2,0},{3,7},{4,6},{5,1},{6,4},{7,3},{8,10},{9,13},{10,... | collective-permute-start | bytes 3538952 | tf_op jit(solution)/shard_map/ppermute | solution.py:46
  (163 other events, 1940.2 us)

commit v5 on v4

--- a/solution.py
+++ b/solution.py
@@ -11,6 +11,8 @@
 LAYERS = 3
 STEP = 10
 MOST = 576
+EXTRA = 16
+NEVER = -1e30
 FF_BLOCK = 256
 
 EPSILON = 1e-06
@@ -30,6 +32,7 @@
 AXES = ("dp", "mp")
 INNER = ("mp", 1)
 OUTER = ("mp", 2)
+DIAGONAL = ("mp", 3)
 LOW = ("dp", 1)
 FIRST = (LOW, OUTER)
 SECOND = (OUTER, LOW)
@@ -203,38 +206,78 @@
     return pltpu.CompilerParams(dimension_semantics=("arbitrary",), vmem_limit_bytes=56 * 1024 * 1024)
 
 
-def masked_probs(scaled_query, key, keep):
-    scores = jnp.where(keep, nt(scaled_query, key), MASKED)
-    weight = jnp.exp(scores - jnp.max(scores, -1, keepdims=True))
-    return weight * (1.0 / jnp.sum(weight, -1, keepdims=True))
-
-
-def attn_fwd_kernel(count, *refs):
-    flag = refs[0]
-    adds = refs[1 : count + 1]
-    norm, segq, segk, *weight, x_ref, mix_ref, part_ref, normed, w, acc = refs[count + 1 :]
+def masked_probs(scaled_query, key, keep, base, away):
+    scores = jnp.where(keep, nt(scaled_query, key), base)
+    top = jnp.maximum(jnp.max(scores, -1, keepdims=True), MASKED)
+    weight = jnp.exp(scores - top)
+    far = jnp.exp(MASKED - top)
+    part = 1.0 / (jnp.sum(weight, -1, keepdims=True) + away * far)
+    return weight * part, far * part
+
+
+def prepare_kernel(count, *refs):
+    adds = refs[:count]
+    norm, real, x_ref, normed_ref, sum_ref = refs[count:]
+    x = adds[0][...]
+    for other in adds[1:]:
+        x = x + other[...].astype(F32)
+    x_ref[...] = x
+    normed = layer_norm(x, norm[...]).astype(BF)
+    normed_ref[...] = normed
+    sum_ref[...] = jnp.sum(normed.astype(F32) * real[...], 0, keepdims=True)
+
+
+def prepare(adds, norm, real):
+    tokens, width = adds[0].shape
+    return pl.pallas_call(
+        functools.partial(prepare_kernel, len(adds)),
+        grid=(1,),
+        in_specs=[full(v) for v in adds] + [full(norm), full(real)],
+        out_specs=[spec_of((tokens, width)), spec_of((tokens, width)), spec_of((1, width))],
+        out_shape=[
+            jax.ShapeDtypeStruct((tokens, width), F32),
+            jax.ShapeDtypeStruct((tokens, width), BF),
+            jax.ShapeDtypeStruct((1, width), F32),
+        ],
+        compiler_params=params(),
+        cost_estimate=NO_COST,
+        name="prepare",
+    )(*adds, norm, real)
+
+
+def below(rows, count=EXTRA):
+    return jnp.concatenate([rows, jnp.zeros((count - rows.shape[0], rows.shape[1]), rows.dtype)], 0)
+
+
+def attn_fwd_kernel(flag, away, normed, others, segq, segk, base, *refs):
+    *weight, mix_ref, part_ref, normed_all, w, acc = refs
     step = pl.program_id(0)
+    tokens = normed.shape[0]
 
     @pl.when(step == 0)
     def _():
-        x = adds[0][...]
-        for other in adds[1:]:
-            x = x + other[...].astype(F32)
-        x_ref[...] = x
-        normed[...] = layer_norm(x, norm[...]).astype(BF)
+        normed_all[:tokens] = normed[...]
+        normed_all[tokens:] = below(others[...]).astype(BF)
         acc[...] = jnp.zeros_like(acc)
 
     load_weight(w, flag, *weight)
-    mixed = nn(normed[...], w[...]).astype(BF)
+    wide = nn(normed_all[...], w[...])
+    mixed = wide.astype(BF)
     c = HEAD_DIM
     width = w.shape[1] // 4
     keep = segq[...] == segk[...]
     outs = []
     for at in range(0, width, c):
-        probs = masked_probs(mixed[:, at : at + c] * c ** (-0.5), mixed[:, width + at : width + at + c], keep)
-        outs.append(nn(probs.astype(BF), mixed[:, 2 * width + at : 2 * width + at + c]).astype(BF))
+        query = mixed[:tokens, at : at + c] * c ** (-0.5)
+        key = mixed[:tokens, width + at : width + at + c]
+        here = slice(2 * width + at, 2 * width + at + c)
+        probs, far = masked_probs(query, key, keep, base[...], away[0])
+        out = nn(probs.astype(BF), mixed[:tokens, here]) + far.astype(BF).astype(F32) * wide[tokens : tokens + 1, here]
+        outs.append(out.astype(BF))
     out = jnp.concatenate(outs, 1)
-    mix_ref[0] = jnp.concatenate([mixed[:, : 3 * width], out], 1)
+    mix_ref[0, :, : 3 * width] = mixed[:, : 3 * width]
+    mix_ref[0, :tokens, 3 * width :] = out
+    mix_ref[0, tokens:, 3 * width :] = jnp.zeros((EXTRA, width), BF)
     acc[...] += nt(jnp.concatenate([jnp.zeros_like(outs[0]), out], 1), w[:, 3 * width - c :])
 
     @pl.when(step == pl.num_programs(0) - 1)
@@ -242,33 +285,32 @@
         part_ref[...] = acc[...].astype(BF)
 
 
-def attn_forward(adds, norm, segq, segk, pieces, flag):
-    tokens, width = adds[0].shape
+def attn_forward(normed, others, segq, segk, base, away, pieces, flag):
+    tokens, width = normed.shape
     columns = pieces[0].shape[1]
     steps, quarters = quarter_specs(pieces[0], columns)
+    values = (normed, others, segq, segk, base)
     return pl.pallas_call(
-        functools.partial(attn_fwd_kernel, len(adds)),
+        attn_fwd_kernel,
         grid=(steps,),
-        in_specs=[FLAG] + [full(v) for v in adds] + [full(norm), full(segq), full(segk)] + quarters,
+        in_specs=[FLAG, FLAG] + [full(v) for v in values] + quarters,
         out_specs=[
-            spec_of((tokens, width)),
-            pl.BlockSpec((1, tokens, columns), lambda i: (i, 0, 0)),
+            pl.BlockSpec((1, tokens + EXTRA, columns), lambda i: (i, 0, 0)),
             spec_of((tokens, width)),
         ],
         out_shape=[
-            jax.ShapeDtypeStruct((tokens, width), F32),
-            jax.ShapeDtypeStruct((steps, tokens, columns), BF),
+            jax.ShapeDtypeStruct((steps, tokens + EXTRA, columns), BF),
             jax.ShapeDtypeStruct((tokens, width), BF),
         ],
         scratch_shapes=[
-            pltpu.VMEM((tokens, width), BF),
+            pltpu.VMEM((tokens + EXTRA, width), BF),
             pltpu.VMEM((width, columns), BF),
             pltpu.VMEM((tokens, width), F32),
         ],
         compiler_params=params(),
         cost_estimate=NO_COST,
         name="attn_forward",
-    )(flag, *adds, norm, segq, segk, *pieces)
+    )(flag, away, *values, *pieces)
 
 
 def ff_fwd_kernel(count, *refs):
@@ -321,13 +363,20 @@
     )(flag, *adds, norm, *pieces)
 
 
+def past_norm(own, other, *rest):
+    total = own[...].astype(F32) + other[...].astype(F32)
+    if rest:
+        one, two, real = rest
+        total = total + real[...] * (one[:1] + two[:1])
+    return total
+
+
 def back_prologue(back, d_ref, g_ref):
     d_base = back[0][...]
     if len(back) == 1:
         d_ref[...] = d_base
         return d_base
-    value, norm, own, other = back[1:]
-    d_value, g_ref[...] = norm_back(value[...], norm[...], own[...].astype(F32) + other[...].astype(F32))
+    d_value, g_ref[...] = norm_back(back[1][...], back[2][...], past_norm(*back[3:]))
     d_all = d_base + d_value
     d_ref[...] = d_all
     return d_all
@@ -403,19 +452,21 @@
 
 
 def attn_back_kernel(count, *refs):
-    flag = refs[0]
-    back = refs[1 : count + 1]
-    value, norm, segq, segk, mix_ref = refs[count + 1 : count + 6]
-    weight, d_ref, grad = refs[count + 6 : count + 10], refs[count + 10], refs[count + 11 : count + 15]
-    part_ref, g_ref, normed_t, dy, dy_t, w, acc, d_mix = refs[count + 15 :]
+    flag, away = refs[:2]
+    back = refs[2 : count + 2]
+    value, norm, others, segq, segk, base, mix_ref = refs[count + 2 : count + 9]
+    weight, d_ref, grad = refs[count + 9 : count + 13], refs[count + 13], refs[count + 14 : count + 18]
+    part_ref, g_ref, row_ref, normed_t, dy, dy_t, w, acc, d_mix = refs[count + 18 :]
     step = pl.program_id(0)
+    tokens = dy.shape[0]
 
     @pl.when(step == 0)
     def _():
         d_all = back_prologue(back, d_ref, g_ref)
         dy[...] = d_all.astype(BF)
         dy_t[...] = d_all.T.astype(BF)
-        normed_t[...] = layer_norm(value[...], norm[...]).T.astype(BF)
+        here = jnp.concatenate([layer_norm(value[...], norm[...]), below(others[...])], 0)
+        normed_t[...] = here.T.astype(BF)
         d_mix[...] = jnp.zeros_like(d_mix)
         acc[...] = jnp.zeros_like(acc)
 
@@ -423,63 +474,70 @@
     c = HEAD_DIM
     scale = HEAD_DIM ** (-0.5)
     width = w.shape[1] // 4
-    tokens = dy.shape[0]
     d_outs = nn(dy[...], w[:, 3 * width - c :])[:, c:].astype(BF)
     keep = segq[...] == segk[...]
     for at in range(0, width, c):
-        query = mix_ref[0, :, at : at + c] * scale
-        key = mix_ref[0, :, width + at : width + at + c]
-        val = mix_ref[0, :, 2 * width + at : 2 * width + at + c]
+        query = mix_ref[0, :tokens, at : at + c] * scale
+        key = mix_ref[0, :tokens, width + at : width + at + c]
+        here = slice(2 * width + at, 2 * width + at + c)
+        val = mix_ref[0, :tokens, here]
+        val_sum = mix_ref[0, tokens:, here][:1].astype(F32)
         d_out = d_outs[:, at : at + c]
-        probs = masked_probs(query, key, keep)
+        d_wide = d_out.astype(F32)
+        probs, far = masked_probs(query, key, keep, base[...], away[0])
         d_probs = nt(d_out, val)
-        delta = jnp.sum(probs * d_probs, -1, keepdims=True)
+        delta = jnp.sum(probs * d_probs, -1, keepdims=True) + far * jnp.sum(d_wide * val_sum, -1, keepdims=True)
         d_scores = jnp.where(keep, probs * (d_probs - delta), 0.0).astype(BF)
-        d_mix[:, at : at + c] = (nn(d_scores, key) * scale).astype(BF)
-        d_mix[:, width + at : width + at + c] = nn(query.T, d_scores).T.astype(BF)
-        d_mix[:, 2 * width + at : 2 * width + at + c] = nn(d_out.T, probs.astype(BF)).T.astype(BF)
+        d_mix[:tokens, at : at + c] = (nn(d_scores, key) * scale).astype(BF)
+        d_mix[:tokens, width + at : width + at + c] = nn(query.T, d_scores).T.astype(BF)
+        d_mix[:tokens, here] = nn(d_out.T, probs.astype(BF)).T.astype(BF)
+        row = jnp.sum(far.astype(BF).astype(F32) * d_wide, 0, keepdims=True)
+        d_mix[tokens:, here] = below(row).astype(BF)
     acc[...] += nt(d_mix[...], w[...])
     wide = 4 * width - (3 * width - c)
-    out = jnp.concatenate([jnp.zeros((tokens, c), BF), mix_ref[0, :, 3 * width :]], 1)
+    out = jnp.concatenate([jnp.zeros((tokens, c), BF), mix_ref[0, :tokens, 3 * width :]], 1)
     left = nn(normed_t[...], d_mix[:, : 4 * width - wide])
     right = nn(normed_t[...], d_mix[:, 4 * width - wide :]) + nn(dy_t[...], out)
     store_grad([left, right], flag, *grad)
 
     @pl.when(step == pl.num_programs(0) - 1)
     def _():
-        part_ref[...] = acc[...].astype(BF)
-
-
-def attn_backward(back, value, norm, segq, segk, mix, pieces, flag):
+        part_ref[...] = acc[:tokens].astype(BF)
+        row_ref[...] = acc[tokens:]
+
+
+def attn_backward(back, value, norm, others, segq, segk, base, away, mix, pieces, flag):
     tokens, width = value.shape
     columns = pieces[0].shape[1]
     steps, quarters = quarter_specs(pieces[0], columns)
     specs, shapes = back_out(tokens, width, pieces, quarters)
+    values = (*back, value, norm, others, segq, segk, base)
     return pl.pallas_call(
         functools.partial(attn_back_kernel, len(back)),
         grid=(steps,),
-        in_specs=[FLAG] + [full(v) for v in back]
-        + [full(value), full(norm), full(segq), full(segk)]
-        + [pl.BlockSpec((1, tokens, columns), lambda i: (i, 0, 0))]
+        in_specs=[FLAG, FLAG]
+        + [full(v) for v in values]
+        + [pl.BlockSpec((1, tokens + EXTRA, columns), lambda i: (i, 0, 0))]
         + quarters,
-        out_specs=specs,
-        out_shape=shapes,
+        out_specs=specs + [spec_of((EXTRA, width))],
+        out_shape=shapes + [jax.ShapeDtypeStruct((EXTRA, width), F32)],
         scratch_shapes=[
-            pltpu.VMEM((width, tokens), BF),
+            pltpu.VMEM((width, tokens + EXTRA), BF),
             pltpu.VMEM((tokens, width), BF),
             pltpu.VMEM((width, tokens), BF),
             pltpu.VMEM((width, columns), BF),
-            pltpu.VMEM((tokens, width), F32),
-            pltpu.VMEM((tokens, columns), BF),
+            pltpu.VMEM((tokens + EXTRA, width), F32),
+            pltpu.VMEM((tokens + EXTRA, columns), BF),
         ],
         compiler_params=params(),
         cost_estimate=NO_COST,
         name="attn_backward",
-    )(flag, *back, value, norm, segq, segk, mix, *pieces)
-
-
-def last_kernel(base, value, norm, own, other, d_ref, g_ref):
-    d_value, g_ref[...] = norm_back(value[...], norm[...], own[...].astype(F32) + other[...].astype(F32))
+    )(flag, away, *values, mix, *pieces)
+
+
+def last_kernel(base, value, norm, *refs):
+    *parts, d_ref, g_ref = refs
+    d_value, g_ref[...] = norm_back(value[...], norm[...], past_norm(*parts))
     d_ref[...] = (base[...] + d_value).astype(BF)
 
 
@@ -656,6 +714,9 @@
     valid = jnp.where(place < held, mine(valid_mask, outer), 0) > 0
     segq = segment[:, None]
     segk = jnp.where(valid, segment, -1)[None, :]
+    real = (place < held).astype(F32)[:, None]
+    base = jnp.where(place < held, MASKED, NEVER)[None, :]
+    away = (tokens - held).astype(F32).reshape(1)
     image_ids = jnp.arange(images, dtype=jnp.int32)
     member = ((segment[None, :] == image_ids[:, None]) & valid[None, :]).astype(F32)
     owned = ((image_ids == longest) == (outer == 0)).astype(F32)[:, None]
@@ -675,8 +736,32 @@
 
     one, two = high[:1], high[1:]
 
+    def together(*units):
+        got = steps.swap(jnp.stack(units), high[0])
+        return [jnp.stack([unit, got[i]]) for i, unit in enumerate(units)]
+
     def flat(unit):
         return unit.reshape(-1, unit.shape[-1])
+
+    xs, middles, mixes, others = [], [], [], []
+
+    def run_prepare(l, adds):
+        x, normed, total = prepare(adds, norms[2 * l], real)
+        xs.append(x)
+        others.append(steps.swap(total, OUTER))
+        return x, steps.add(normed)
+
+    def run_attn(l, x, normed):
+        mix, own = attn_forward(steps.tie(normed), others[l], segq, segk, base, away, attn[l], flag)
+        mixes.append(mix)
+        steps.add(own)
+        return [x, own, swap(own, INNER)]
+
+    def run_ff(l, adds):
+        middle, own = ff_forward([steps.tie(adds[0])] + adds[1:], norms[2 * l + 1], ff[l], flag)
+        middles.append(middle)
+        steps.add(own)
+        return [middle, own, swap(own, INNER)]
 
     for unit in attn + ff + [head_unit]:
         steps.add(unit)
@@ -687,10 +772,11 @@
     steps.next()
     attn[0] = flat(over(attn[0], two))
     ff[0] = over(ff[0], one)
+    attn[1], attn[2] = together(attn[1], attn[2])
     patch = over(patch, [low]).reshape(width, -1)
     steps.next()
     ff[0] = flat(over(ff[0], two))
-    attn[1] = over(attn[1], one)
+    ff[1], ff[2] = together(ff[1], ff[2])
     attn[0] = near(attn[0])
     patch = steps.tie(patch)
     norms = patch[:, pixel_count:].T.astype(F32).reshape(7, 2, width)
@@ -702,51 +788,33 @@
     attn[0] = across(attn[0])
     ff[0] = near(ff[0])
     attn[1] = flat(over(attn[1], two))
-    ff[1] = over(ff[1], one)
-    x = steps.add(halves(part, swap(part, INNER)))
-    steps.next()
-    xs, middles, mixes = [], [], []
-
-    def run_attn(l, adds):
-        x, mix, own = attn_forward([steps.tie(adds[0])] + adds[1:], norms[2 * l], segq, segk, attn[l], flag)
-        xs.append(x)
-        mixes.append(mix)
-        steps.add(own)
-        return [x, own, swap(own, INNER)]
-
-    def run_ff(l, adds):
-        middle, own = ff_forward([steps.tie(adds[0])] + adds[1:], norms[2 * l + 1], ff[l], flag)
-        middles.append(middle)
-        steps.add(own)
-        return [middle, own, swap(own, INNER)]
-
+    prepared = run_prepare(0, [halves(part, swap(part, INNER))])
+    steps.next()
     ff[0] = across(ff[0])
     attn[1] = near(attn[1])
     ff[1] = flat(over(ff[1], two))
-    attn[2] = over(attn[2], one)
-    adds = run_attn(0, [x])
+    adds = run_attn(0, *prepared)
     steps.next()
     attn[1] = across(attn[1])
     ff[1] = near(ff[1])
     attn[2] = flat(over(attn[2], two))
-    ff[2] = over(ff[2], one)
-    adds = run_ff(0, adds)
+    prepared = run_prepare(1, run_ff(0, adds))
     steps.next()
     ff[1] = across(ff[1])
     attn[2] = near(attn[2])
     ff[2] = flat(over(ff[2], two))
-    head = over(head_unit, one)
-    adds = run_attn(1, adds)
+    adds = run_attn(1, *prepared)
     steps.next()
     attn[2] = across(attn[2])
     ff[2] = near(ff[2])
+    head = over(head_unit, one)
+    prepared = run_prepare(2, run_ff(1, adds))
+    steps.next()
+    ff[2] = across(ff[2])
     head = over(head, two)
-    adds = run_ff(1, adds)
-    steps.next()
-    ff[2] = across(ff[2])
+    adds = run_attn(2, *prepared)
+    steps.next()
     head = over(head, [low]).reshape(-1, rows + 2 * images, half)
-    adds = run_attn(2, adds)
-    steps.next()
     teach = head[:, rows : rows + images].astype(F32) + head[:, rows + images :].astype(F32)
     head = head[:, :rows].reshape(width, half)
     adds = run_ff(2, adds)
@@ -817,13 +885,15 @@
 
     def back_attn(l, back):
         back = [steps.tie(back[0])] + back[1:]
-        d_mid, *grad, own, g_above = attn_backward(
-            back, xs[l], norms[2 * l], segq, segk, mixes[l], attn[l], flag
+        d_mid, *grad, own, g_above, row = attn_backward(
+            back, xs[l], norms[2 * l], others[l], segq, segk, base, away, mixes[l], attn[l], flag
         )
         g["attn", l] = grad
         g_norms[2 * l + 1] = g_above
         steps.add(own)
-        return [d_mid, xs[l], norms[2 * l], own, swap(own, INNER)]
+        row = row[:8]
+        rows_in = [steps.add(swap(row, OUTER)), steps.add(swap(row, DIAGONAL))]
+        return [d_mid, xs[l], norms[2 * l], own, swap(own, INNER), *rows_in, real]
 
     g["head"] = (g_head[:mid], g_head[mid:])
     near_low("head")

time: 662 us -> 713 us (1.077)
  waiting for transfers between devices: 208 us -> 228 us
  Pallas kernels: 228 us -> 240 us
  starting transfers between devices: 91.1 us -> 99 us
    ppermute x103 -> x110, waiting for transfers between devices: 208 us -> 228 us  [swap(): return lax.ppermute(value, AXES, pairs)]
    ppermute x103 -> x110, starting transfers between devices: 91.1 us -> 99 us  [swap(): return lax.ppermute(value, AXES, pairs)]
    pallas_call x3 -> x6, Pallas kernels: 40.5 us -> 47.2 us  [the longest x3 36.1 us: attn_forward(): pl.pallas_call(attn_fwd_kernel, grid=(steps,), in_specs=[FLAG, FLAG] + [f...]
    unnamed x170 -> x204, local copies, waits for them, and re-layouts: 15.3 us -> 12.7 us
    another operation x19 -> x18, other arithmetic: 16.6 us -> 15.5 us  [over(): unit = jnp.stack([unit, steps.swap(unit, bit)])]
  transfers between devices with their start and end apart: 103 -> 110, of which waited for: 40 -> 43; matrix products, arithmetic and copies ran while one was open for 13% -> 13% of each run, Pallas kernels for 30% -> 30%
where the time goes in v5:
time: 713 us; the launch traced here: 702 us
  Pallas kernels  240 us (34%)
  waiting for transfers between devices  228 us (32%)
  starting transfers between devices  99 us (14%)
  other arithmetic  70.7 us (10%)
  local copies, waits for them, and re-layouts  41.7 us (6%)
  between operations  12.9 us (2%)
  matrix products  9.19 us (1%)
    ppermute x110, waiting for transfers between devices, swap(): return lax.ppermute(value, AXES, pairs)  228 us
    ppermute x110, starting transfers between devices, swap(): return lax.ppermute(value, AXES, pairs)  99 us
    pallas_call x3, Pallas kernels, attn_backward(): pl.pallas_call(functools.partial(attn_back_kernel, len(back)), grid=(step...  74.1 us
    pallas_call x3, Pallas kernels, ff_backward(): pl.pallas_call(functools.partial(ff_back_kernel, len(back)), grid=(steps,...  57 us
    pallas_call x3, Pallas kernels, ff_forward(): pl.pallas_call(functools.partial(ff_fwd_kernel, len(adds)), grid=(steps,)...  36.8 us
    pallas_call x3, Pallas kernels, attn_forward(): pl.pallas_call(attn_fwd_kernel, grid=(steps,), in_specs=[FLAG, FLAG] + [f...  36.1 us
    another operation x18, other arithmetic, over(): unit = jnp.stack([unit, steps.swap(unit, bit)])  15.5 us
  transfers between devices with their start and end apart: 110, of which 43 were waited for; matrix products, arithmetic and copies ran while one was open for 13% of the time, Pallas kernels for 30%

profile of v5, /device:TPU:0, one launch (start us, length us, event | category | flops | bytes accessed | tf_op | source)
XLA Modules:
  0.0 701.5 jit_solution(4455172379262123321)
XLA Ops:
  44.8 9.9 %collective-permute-done.5 = bf16[2,96,768]{1,2,0:T(8,128)(2,1)} collective-permute-done((bf16[2,96,768]{1,2,0:T(8,128)(2,1)}, bf16[2,96,768]{1,2,0:T(8,128)(2,1)}, u32[]{:S(2)}, u32[]{:S(2)}) %collective-permute-start.5) | collective-permute-done | bytes 294944 | tf_op jit(solution)/shard_map/ppermute | solution.py:49
  79.4 21.7 %collective-permute-done.10 = bf16[2,96,1536]{2,1,0:T(8,128)(2,1)} collective-permute-done((bf16[2,96,1536]{2,1,0:T(8,128)(2,1)}, bf16[2,96,1536]{2,1,0:T(8,128)(2,1)}, u32[]{:S(2)}, u32[]{:S(2)}) %collective-permute-start.10) | collective-permute-done | bytes 589856 | tf_op jit(solution)/shard_map/ppermute | solution.py:49
  120.8 11.4 %collective-permute-done.18 = bf16[2,96,768]{1,2,0:T(8,128)(2,1)S(1)} collective-permute-done((bf16[2,96,768]{1,2,0:T(8,128)(2,1)S(1)}, bf16[2,96,768]{1,2,0:T(8,128)(2,1)S(1)}, u32[]{:S(2)}, u32[]{:S(2)}) %collective-permute-start.18) | collective-permute-done | bytes 294944 | tf_op jit(solution)/shard_map/ppermute | solution.py:49
  132.2 10.2 %collective-permute-done.16.refs_3_.refs_17_ = bf16[384,768]{1,0:T(8,128)(2,1)S(1)} collective-permute-done((bf16[384,768]{1,0:T(8,128)(2,1)}, bf16[384,768]{1,0:T(8,128)(2,1)S(1)}, u32[]{:S(2)}, u32[]{:S(2)}) %collective-permute-start.16) | collective-permute-done | bytes 589856 | tf_op jit(solution)/shard_map/ppermute | solution.py:49
  148.5 12.2 %attn_forward.3 = (bf16[2,592,768]{2,1,0:T(8,128)(2,1)}, bf16[576,768]{1,0:T(8,128)(2,1)}) custom-call(s32[1]{0:T(128)} %bitcast.flag.refs_0_, f32[1]{0:T(128)} %bitcast.1.away.refs_1_, bf16[576,768]{1,0:T(8,128)(2,1)} %get-tuple-element.232.normed, f32[1,768]{1,0:T(1,128)} %copy-done.95, s32[576,1]{1,0:T(8,128)} %broadcast_in_dim.60.segq.refs_10_, ...), custom_call_target="tpu_custom_call" | custom-call | flops 1000000 | bytes 10000 | tf_op jit(solution)/shard_map/attn_forward/pallas_call | solution.py:293
  178.9 12.3 %ff_forward.3 = (f32[576,768]{1,0:T(8,128)}, bf16[576,768]{1,0:T(8,128)(2,1)}) custom-call(s32[1]{0:T(128)} %bitcast.flag.refs_0_, f32[576,768]{1,0:T(8,128)} %get-tuple-element.234.refs_1_.refs_7_.value, bf16[576,768]{1,0:T(8,128)(2,1)} %get-tuple-element.233.refs_2_, bf16[576,768]{1,0:T(8,128)(2,1)} %collective-permute-done.24.refs_3_, ...), custom_call_target="tpu_custom_call" | custom-call | flops 1000000 | bytes 10000 | tf_op jit(solution)/shard_map/ff_forward/pallas_call | solution.py:346
  201.5 11.2 %collective-permute-done.29 = bf16[2,96,768]{1,2,0:T(8,128)(2,1)S(1)} collective-permute-done((bf16[2,96,768]{1,2,0:T(8,128)(2,1)S(1)}, bf16[2,96,768]{1,2,0:T(8,128)(2,1)S(1)}, u32[]{:S(2)}, u32[]{:S(2)}) %collective-permute-start.29) | collective-permute-done | bytes 294944 | tf_op jit(solution)/shard_map/ppermute | solution.py:49
  215.7 11.9 %attn_forward.4 = (bf16[2,592,768]{2,1,0:T(8,128)(2,1)}, bf16[576,768]{1,0:T(8,128)(2,1)}) custom-call(s32[1]{0:T(128)} %bitcast.flag.refs_0_, f32[1]{0:T(128)} %bitcast.1.away.refs_1_, bf16[576,768]{1,0:T(8,128)(2,1)} %get-tuple-element.247.normed, f32[1,768]{1,0:T(1,128)} %copy-done.96, s32[576,1]{1,0:T(8,128)} %broadcast_in_dim.60.segq.refs_10_, ...), custom_call_target="tpu_custom_call" | custom-call | flops 1000000 | bytes 10000 | tf_op jit(solution)/shard_map/attn_forward/pallas_call | solution.py:293
  230.2 12.5 %collective-permute-done.34 = bf16[2,96,1536]{2,1,0:T(8,128)(2,1)} collective-permute-done((bf16[2,96,1536]{2,1,0:T(8,128)(2,1)S(1)}, bf16[2,96,1536]{2,1,0:T(8,128)(2,1)}, u32[]{:S(2)}, u32[]{:S(2)}) %collective-permute-start.34) | collective-permute-done | bytes 589856 | tf_op jit(solution)/shard_map/ppermute | solution.py:49
  246.7 12.3 %ff_forward.4 = (f32[576,768]{1,0:T(8,128)}, bf16[576,768]{1,0:T(8,128)(2,1)}) custom-call(s32[1]{0:T(128)} %bitcast.flag.refs_0_, f32[576,768]{1,0:T(8,128)} %get-tuple-element.249.refs_1_.refs_7_.refs_2_, bf16[576,768]{1,0:T(8,128)(2,1)} %get-tuple-element.248.refs_2_, bf16[576,768]{1,0:T(8,128)(2,1)} %collective-permute-done.35.refs_3_, ...), custom_call_target="tpu_custom_call" | custom-call | flops 1000000 | bytes 10000 | tf_op jit(solution)/shard_map/ff_forward/pallas_call | solution.py:346
  267.6 10.9 %collective-permute-done.38.refs_3_.refs_17_ = bf16[384,768]{1,0:T(8,128)(2,1)S(1)} collective-permute-done((bf16[384,768]{1,0:T(8,128)(2,1)S(1)}, bf16[384,768]{1,0:T(8,128)(2,1)S(1)}, u32[]{:S(2)}, u32[]{:S(2)}) %collective-permute-start.38) | collective-permute-done | bytes 589856 | tf_op jit(solution)/shard_map/ppermute | solution.py:49
  280.1 12.0 %attn_forward.5 = (bf16[2,592,768]{2,1,0:T(8,128)(2,1)}, bf16[576,768]{1,0:T(8,128)(2,1)}) custom-call(s32[1]{0:T(128)} %bitcast.flag.refs_0_, f32[1]{0:T(128)} %bitcast.1.away.refs_1_, bf16[576,768]{1,0:T(8,128)(2,1)} %get-tuple-element.261.normed, f32[1,768]{1,0:T(1,128)} %copy-done.97, s32[576,1]{1,0:T(8,128)} %broadcast_in_dim.60.segq.refs_10_, ...), custom_call_target="tpu_custom_call" | custom-call | flops 1000000 | bytes 10000 | tf_op jit(solution)/shard_map/attn_forward/pallas_call | solution.py:293
  295.0 12.0 %collective-permute-done.43 = bf16[2,112,500]{2,1,0:T(8,128)(2,1)} collective-permute-done((bf16[2,112,500]{2,1,0:T(8,128)(2,1)}, bf16[2,112,500]{2,1,0:T(8,128)(2,1)}, u32[]{:S(2)}, u32[]{:S(2)}) %collective-permute-start.43) | collective-permute-done | bytes 224032 | tf_op jit(solution)/shard_map/ppermute | solution.py:49
  308.3 12.3 %ff_forward.5 = (f32[576,768]{1,0:T(8,128)}, bf16[576,768]{1,0:T(8,128)(2,1)}) custom-call(s32[1]{0:T(128)} %bitcast.flag.refs_0_, f32[576,768]{1,0:T(8,128)} %get-tuple-element.263.refs_1_.refs_7_.refs_2_, bf16[576,768]{1,0:T(8,128)(2,1)} %get-tuple-element.262.refs_2_, bf16[576,768]{1,0:T(8,128)(2,1)} %copy-done.47, ...), custom_call_target="tpu_custom_call" | custom-call | flops 1000000 | bytes 10000 | tf_op jit(solution)/shard_map/ff_forward/pallas_call | solution.py:346
  325.2 10.8 %collective-permute-done.46 = bf16[2,2,112,500]{3,2,1,0:T(8,128)(2,1)S(1)} collective-permute-done((bf16[2,2,112,500]{3,2,1,0:T(8,128)(2,1)S(1)}, bf16[2,2,112,500]{3,2,1,0:T(8,128)(2,1)S(1)}, u32[]{:S(2)}, u32[]{:S(2)}) %collective-permute-start.46) | collective-permute-done | bytes 448032 | tf_op jit(solution)/shard_map/ppermute | solution.py:49
  345.7 17.1 %ff_backward.3 = (f32[576,768]{1,0:T(8,128)}, bf16[384,1536]{1,0:T(8,128)(2,1)}, bf16[384,1536]{1,0:T(8,128)(2,1)}, bf16[384,1536]{1,0:T(8,128)(2,1)}, bf16[384,...) custom-call(s32[1]{0:T(128)} %bitcast.flag.refs_0_, f32[576,768]{1,0:T(8,128)} %fusion.36.refs_1_, ...), custom_call_target="tpu_custom_call" | custom-call | flops 1000000 | bytes 10000 | tf_op jit(solution)/shard_map/ff_backward/pallas_call | solution.py:434
  367.8 24.9 %attn_backward.3 = (f32[576,768]{1,0:T(8,128)}, bf16[384,768]{1,0:T(8,128)(2,1)}, bf16[384,768]{1,0:T(8,128)(2,1)}, bf16[384,768]{1,0:T(8,128)(2,1)}, bf16[384,7...) custom-call(s32[1]{0:T(128)} %bitcast.flag.refs_0_, f32[1]{0:T(128)} %bitcast.1.away.refs_1_, ...), custom_call_target="tpu_custom_call" | custom-call | flops 1000000 | bytes 10000 | tf_op jit(solution)/shard_map/attn_backward/pallas_call | solution.py:515
  402.5 19.8 %ff_backward.4 = (f32[576,768]{1,0:T(8,128)}, bf16[384,1536]{1,0:T(8,128)(2,1)}, bf16[384,1536]{1,0:T(8,128)(2,1)}, bf16[384,1536]{1,0:T(8,128)(2,1)}, bf16[384,...) custom-call(s32[1]{0:T(128)} %bitcast.flag.refs_0_, f32[576,768]{1,0:T(8,128)} %get-tuple-element.279.refs_1_, ...), custom_call_target="tpu_custom_call" | custom-call | flops 1000000 | bytes 10000 | tf_op jit(solution)/shard_map/ff_backward/pallas_call | solution.py:434
  433.7 24.6 %attn_backward.4 = (f32[576,768]{1,0:T(8,128)}, bf16[384,768]{1,0:T(8,128)(2,1)}, bf16[384,768]{1,0:T(8,128)(2,1)}, bf16[384,768]{1,0:T(8,128)(2,1)}, bf16[384,7...) custom-call(s32[1]{0:T(128)} %bitcast.flag.refs_0_, f32[1]{0:T(128)} %bitcast.1.away.refs_1_, ...), custom_call_target="tpu_custom_call" | custom-call | flops 1000000 | bytes 10000 | tf_op jit(solution)/shard_map/attn_backward/pallas_call | solution.py:515
  478.8 20.1 %ff_backward.5 = (f32[576,768]{1,0:T(8,128)}, bf16[384,1536]{1,0:T(8,128)(2,1)}, bf16[384,1536]{1,0:T(8,128)(2,1)}, bf16[384,1536]{1,0:T(8,128)(2,1)}, bf16[384,...) custom-call(s32[1]{0:T(128)} %bitcast.flag.refs_0_, f32[576,768]{1,0:T(8,128)} %get-tuple-element.302.refs_1_, ...), custom_call_target="tpu_custom_call" | custom-call | flops 1000000 | bytes 10000 | tf_op jit(solution)/shard_map/ff_backward/pallas_call | solution.py:434
  508.9 24.7 %attn_backward.5 = (f32[576,768]{1,0:T(8,128)}, bf16[384,768]{1,0:T(8,128)(2,1)}, bf16[384,768]{1,0:T(8,128)(2,1)}, bf16[384,768]{1,0:T(8,128)(2,1)}, bf16[384,7...) custom-call(s32[1]{0:T(128)} %bitcast.flag.refs_0_, f32[1]{0:T(128)} %bitcast.1.away.refs_1_, ...), custom_call_target="tpu_custom_call" | custom-call | flops 1000000 | bytes 10000 | tf_op jit(solution)/shard_map/attn_backward/pallas_call | solution.py:515
  608.9 11.8 %collective-permute-done.93 = bf16[2,96,1536]{2,1,0:T(8,128)(2,1)S(1)} collective-permute-done((bf16[2,96,1536]{2,1,0:T(8,128)(2,1)S(1)}, bf16[2,96,1536]{2,1,0:T(8,128)(2,1)S(1)}, u32[]{:S(2)}, u32[]{:S(2)}) %collective-permute-start.93) | collective-permute-done | bytes 589856 | tf_op jit(solution)/shard_map/ppermute | solution.py:49
  629.1 10.7 %collective-permute-done.96 = bf16[1,96,1536]{2,1,0:T(8,128)(2,1)S(1)} collective-permute-done((bf16[1,96,1536]{2,1,0:T(8,128)(2,1)}, bf16[1,96,1536]{2,1,0:T(8,128)(2,1)S(1)}, u32[]{:S(2)}, u32[]{:S(2)}) %collective-permute-start.96) | collective-permute-done | bytes 294944 | tf_op jit(solution)/shard_map/ppermute | solution.py:49
  687.7 12.5 %adam.1 = (f32[3,3,96,192]{3,2,1,0:T(8,128)}, f32[3,192,96]{2,1,0:T(8,128)}, f32[3,96,768]{2,1,0:T(8,128)}, f32[3,96,768]{2,1,0:T(8,128)}, f32[96,768]{1,0:T(8,1...) custom-call(f32[1]{0:T(128)} %bitcast.122.clip_ref, ...), custom_call_target="tpu_custom_call" | custom-call | tf_op jit(solution)/shard_map/adam/pallas_call | solution.py:627
  (606 shorter events, 339.1 us)
Async XLA Ops:
  72.3 28.8 %collective-permute-start.11 = (bf16[384,768]{1,0:T(8,128)(2,1)}, bf16[384,768]{1,0:T(8,128)(2,1)}, u32[]{:S(2)}, u32[]{:S(2)}) collective-permute-start(bf16[384,768]{1,0:T(8,128)(2,1)} %bitcast.43.refs_0_.refs_14_), channel_id=1, source_target_pairs={{0,2},{1,5},{2,0},{3,7},{4,6},{5,1},{6,4},{7,3},{8,10},{9,13},{10,... | collective-permute-start | bytes 1769480 | tf_op jit(solution)/shard_map/ppermute | solution.py:49
  73.8 30.8 %collective-permute-start.12 = (bf16[384,768]{1,0:T(8,128)(2,1)}, bf16[384,768]{1,0:T(8,128)(2,1)}, u32[]{:S(2)}, u32[]{:S(2)}) collective-permute-start(bf16[384,768]{1,0:T(8,128)(2,1)} %bitcast.43.refs_0_.refs_14_), channel_id=1, source_target_pairs={{0,4},{1,3},{2,6},{3,1},{4,0},{5,7},{6,2},{7,5},{8,12},{9,11},{10,... | collective-permute-start | bytes 1769480 | tf_op jit(solution)/shard_map/ppermute | solution.py:49
  107.6 34.8 %collective-permute-start.15 = (bf16[384,1536]{1,0:T(8,128)(2,1)S(1)}, bf16[384,1536]{1,0:T(8,128)(2,1)S(1)}, u32[]{:S(2)}, u32[]{:S(2)}) collective-permute-start(bf16[384,1536]{1,0:T(8,128)(2,1)S(1)} %bitcast.291), channel_id=1, source_target_pairs={{0,2},{1,5},{2,0},{3,7},{4,6},{5,1},{6,4},{7,3},{8,10},{9,13},{10,... | collective-permute-start | bytes 3538952 | tf_op jit(solution)/shard_map/ppermute | solution.py:49
  108.2 34.2 %collective-permute-start.17 = (bf16[384,1536]{1,0:T(8,128)(2,1)S(1)}, bf16[384,1536]{1,0:T(8,128)(2,1)S(1)}, u32[]{:S(2)}, u32[]{:S(2)}) collective-permute-start(bf16[384,1536]{1,0:T(8,128)(2,1)S(1)} %bitcast.292), channel_id=1, source_target_pairs={{0,4},{1,3},{2,6},{3,1},{4,0},{5,7},{6,2},{7,5},{8,12},{9,11},{10,... | collective-permute-start | bytes 3538952 | tf_op jit(solution)/shard_map/ppermute | solution.py:49
  112.0 30.4 %collective-permute-start.16 = (bf16[384,768]{1,0:T(8,128)(2,1)}, bf16[384,768]{1,0:T(8,128)(2,1)S(1)}, u32[]{:S(2)}, u32[]{:S(2)}) collective-permute-start(bf16[384,768]{1,0:T(8,128)(2,1)} %collective-permute-done.11.refs_1_.refs_15_), channel_id=1, source_target_pairs={{0,4},{1,3},{2,6},{3,1},{4,0},{5,7},{6,2},{7,5},{8,12},{9,11},{10,... | collective-permute-start | bytes 1769480 | tf_op jit(solution)/shard_map/ppermute | solution.py:49
  143.6 33.7 %collective-permute-start.20 = (bf16[384,1536]{1,0:T(8,128)(2,1)S(1)}, bf16[384,1536]{1,0:T(8,128)(2,1)}, u32[]{:S(2)}, u32[]{:S(2)}) collective-permute-start(bf16[384,1536]{1,0:T(8,128)(2,1)S(1)} %collective-permute-done.15.refs_6_.refs_12_), channel_id=1, source_target_pairs={{0,4},{1,3},{2,6},{3,1},{4,0},{5,7},{6,2},{7,5},{8,12},{9,11},{10,... | collective-permute-start | bytes 3538952 | tf_op jit(solution)/shard_map/ppermute | solution.py:49
  177.3 35.4 %collective-permute-start.26 = (bf16[384,1536]{1,0:T(8,128)(2,1)S(1)}, bf16[384,1536]{1,0:T(8,128)(2,1)S(1)}, u32[]{:S(2)}, u32[]{:S(2)}) collective-permute-start(bf16[384,1536]{1,0:T(8,128)(2,1)S(1)} %bitcast.295), channel_id=1, source_target_pairs={{0,2},{1,5},{2,0},{3,7},{4,6},{5,1},{6,4},{7,3},{8,10},{9,13},{10,... | collective-permute-start | bytes 3538952 | tf_op jit(solution)/shard_map/ppermute | solution.py:49
  177.9 34.8 %collective-permute-start.28 = (bf16[384,1536]{1,0:T(8,128)(2,1)S(1)}, bf16[384,1536]{1,0:T(8,128)(2,1)S(1)}, u32[]{:S(2)}, u32[]{:S(2)}) collective-permute-start(bf16[384,1536]{1,0:T(8,128)(2,1)S(1)} %bitcast.296), channel_id=1, source_target_pairs={{0,4},{1,3},{2,6},{3,1},{4,0},{5,7},{6,2},{7,5},{8,12},{9,11},{10,... | collective-permute-start | bytes 3538952 | tf_op jit(solution)/shard_map/ppermute | solution.py:49
  212.8 31.4 %collective-permute-start.31 = (bf16[384,1536]{1,0:T(8,128)(2,1)S(1)}, bf16[384,1536]{1,0:T(8,128)(2,1)}, u32[]{:S(2)}, u32[]{:S(2)}) collective-permute-start(bf16[384,1536]{1,0:T(8,128)(2,1)S(1)} %collective-permute-done.26.refs_6_.refs_12_), channel_id=1, source_target_pairs={{0,4},{1,3},{2,6},{3,1},{4,0},{5,7},{6,2},{7,5},{8,12},{9,11},{10,... | collective-permute-start | bytes 3538952 | tf_op jit(solution)/shard_map/ppermute | solution.py:49
  244.2 34.4 %collective-permute-start.37 = (bf16[384,1536]{1,0:T(8,128)(2,1)S(1)}, bf16[384,1536]{1,0:T(8,128)(2,1)S(1)}, u32[]{:S(2)}, u32[]{:S(2)}) collective-permute-start(bf16[384,1536]{1,0:T(8,128)(2,1)S(1)} %bitcast.299), channel_id=1, source_target_pairs={{0,2},{1,5},{2,0},{3,7},{4,6},{5,1},{6,4},{7,3},{8,10},{9,13},{10,... | collective-permute-start | bytes 3538952 | tf_op jit(solution)/shard_map/ppermute | solution.py:49
  245.6 33.0 %collective-permute-start.39 = (bf16[384,1536]{1,0:T(8,128)(2,1)S(1)}, bf16[384,1536]{1,0:T(8,128)(2,1)S(1)}, u32[]{:S(2)}, u32[]{:S(2)}) collective-permute-start(bf16[384,1536]{1,0:T(8,128)(2,1)S(1)} %bitcast.300), channel_id=1, source_target_pairs={{0,4},{1,3},{2,6},{3,1},{4,0},{5,7},{6,2},{7,5},{8,12},{9,11},{10,... | collective-permute-start | bytes 3538952 | tf_op jit(solution)/shard_map/ppermute | solution.py:49
  362.8 32.1 %collective-permute-start.51 = (bf16[384,1536]{1,0:T(8,128)(2,1)}, bf16[384,1536]{1,0:T(8,128)(2,1)S(1)}, u32[]{:S(2)}, u32[]{:S(2)}) collective-permute-start(bf16[384,1536]{1,0:T(8,128)(2,1)} %get-tuple-element.273), channel_id=1, source_target_pairs={{0,4},{1,3},{2,6},{3,1},{4,0},{5,7},{6,2},{7,5},{8,12},{9,11},{10,... | collective-permute-start | bytes 3538952 | tf_op jit(solution)/shard_map/ppermute | solution.py:49
  364.2 33.6 %collective-permute-start.52 = (bf16[384,1536]{1,0:T(8,128)(2,1)}, bf16[384,1536]{1,0:T(8,128)(2,1)S(1)}, u32[]{:S(2)}, u32[]{:S(2)}) collective-permute-start(bf16[384,1536]{1,0:T(8,128)(2,1)} %get-tuple-element.275), channel_id=1, source_target_pairs={{0,4},{1,3},{2,6},{3,1},{4,0},{5,7},{6,2},{7,5},{8,12},{9,11},{10,... | collective-permute-start | bytes 3538952 | tf_op jit(solution)/shard_map/ppermute | solution.py:49
  365.1 30.1 %collective-permute-start.53 = (bf16[2,96,500]{2,1,0:T(8,128)(2,1)S(1)}, bf16[2,96,500]{2,1,0:T(8,128)(2,1)S(1)}, u32[]{:S(2)}, u32[]{:S(2)}) collective-permute-start(bf16[2,96,500]{2,1,0:T(8,128)(2,1)S(1)} %pad_maximum_fusion.35), channel_id=1, source_target_pairs={{0,16},{1,17},{2,18},{3,19},{4,20},{5,21},{6,22},{7,23},{8,24},{9,... | collective-permute-start | bytes 576008 | tf_op jit(solution)/shard_map/ppermute | solution.py:49
  425.9 36.1 %collective-permute-start.62 = (bf16[384,1536]{1,0:T(8,128)(2,1)}, bf16[384,1536]{1,0:T(8,128)(2,1)S(1)}, u32[]{:S(2)}, u32[]{:S(2)}) collective-permute-start(bf16[384,1536]{1,0:T(8,128)(2,1)} %get-tuple-element.293), channel_id=1, source_target_pairs={{0,4},{1,3},{2,6},{3,1},{4,0},{5,7},{6,2},{7,5},{8,12},{9,11},{10,... | collective-permute-start | bytes 3538952 | tf_op jit(solution)/shard_map/ppermute | solution.py:49
  428.5 31.4 %collective-permute-start.65 = (bf16[2,96,1536]{2,1,0:T(8,128)(2,1)}, bf16[2,96,1536]{2,1,0:T(8,128)(2,1)}, u32[]{:S(2)}, u32[]{:S(2)}) collective-permute-start(bf16[2,96,1536]{2,1,0:T(8,128)(2,1)} %pad_maximum_fusion.16), channel_id=1, source_target_pairs={{0,16},{1,17},{2,18},{3,19},{4,20},{5,21},{6,22},{7,23},{8,24},{9,... | collective-permute-start | bytes 1769480 | tf_op jit(solution)/shard_map/ppermute | solution.py:49
  431.2 38.6 %collective-permute-start.63 = (bf16[384,1536]{1,0:T(8,128)(2,1)}, bf16[384,1536]{1,0:T(8,128)(2,1)S(1)}, u32[]{:S(2)}, u32[]{:S(2)}) collective-permute-start(bf16[384,1536]{1,0:T(8,128)(2,1)} %get-tuple-element.295), channel_id=1, source_target_pairs={{0,4},{1,3},{2,6},{3,1},{4,0},{5,7},{6,2},{7,5},{8,12},{9,11},{10,... | collective-permute-start | bytes 3538952 | tf_op jit(solution)/shard_map/ppermute | solution.py:49
  469.8 30.2 %collective-permute-start.71 = (bf16[384,1536]{1,0:T(8,128)(2,1)S(1)}, bf16[384,1536]{1,0:T(8,128)(2,1)S(1)}, u32[]{:S(2)}, u32[]{:S(2)}) collective-permute-start(bf16[384,1536]{1,0:T(8,128)(2,1)S(1)} %add_convert_fusion.3), channel_id=1, source_target_pairs={{0,2},{1,5},{2,0},{3,7},{4,6},{5,1},{6,4},{7,3},{8,10},{9,13},{10,... | collective-permute-start | bytes 3538952 | tf_op jit(solution)/shard_map/ppermute | solution.py:49
  500.0 34.4 %collective-permute-start.77 = (bf16[384,768]{1,0:T(8,128)(2,1)}, bf16[384,768]{1,0:T(8,128)(2,1)S(1)}, u32[]{:S(2)}, u32[]{:S(2)}) collective-permute-start(bf16[384,768]{1,0:T(8,128)(2,1)} %add_convert_fusion.10), channel_id=1, source_target_pairs={{0,2},{1,5},{2,0},{3,7},{4,6},{5,1},{6,4},{7,3},{8,10},{9,13},{10,... | collective-permute-start | bytes 1769480 | tf_op jit(solution)/shard_map/ppermute | solution.py:49
  501.6 34.9 %collective-permute-start.78 = (bf16[2,96,1536]{2,1,0:T(8,128)(2,1)S(1)}, bf16[2,96,1536]{2,1,0:T(8,128)(2,1)S(1)}, u32[]{:S(2)}, u32[]{:S(2)}) collective-permute-start(bf16[2,96,1536]{2,1,0:T(8,128)(2,1)S(1)} %pad_maximum_fusion.17), channel_id=1, source_target_pairs={{0,16},{1,17},{2,18},{3,19},{4,20},{5,21},{6,22},{7,23},{8,24},{9,... | collective-permute-start | bytes 1769480 | tf_op jit(solution)/shard_map/ppermute | solution.py:49
  504.0 39.6 %collective-permute-start.75 = (bf16[384,1536]{1,0:T(8,128)(2,1)}, bf16[384,1536]{1,0:T(8,128)(2,1)S(1)}, u32[]{:S(2)}, u32[]{:S(2)}) collective-permute-start(bf16[384,1536]{1,0:T(8,128)(2,1)} %get-tuple-element.318), channel_id=1, source_target_pairs={{0,4},{1,3},{2,6},{3,1},{4,0},{5,7},{6,2},{7,5},{8,12},{9,11},{10,... | collective-permute-start | bytes 3538952 | tf_op jit(solution)/shard_map/ppermute | solution.py:49
  504.7 38.9 %collective-permute-start.76 = (bf16[384,1536]{1,0:T(8,128)(2,1)}, bf16[384,1536]{1,0:T(8,128)(2,1)S(1)}, u32[]{:S(2)}, u32[]{:S(2)}) collective-permute-start(bf16[384,1536]{1,0:T(8,128)(2,1)} %get-tuple-element.320), channel_id=1, source_target_pairs={{0,4},{1,3},{2,6},{3,1},{4,0},{5,7},{6,2},{7,5},{8,12},{9,11},{10,... | collective-permute-start | bytes 3538952 | tf_op jit(solution)/shard_map/ppermute | solution.py:49
  507.7 36.0 %collective-permute-start.79 = (bf16[1,96,768]{2,1,0:T(8,128)(2,1)}, bf16[1,96,768]{2,1,0:T(8,128)(2,1)}, u32[]{:S(2)}, u32[]{:S(2)}) collective-permute-start(bf16[1,96,768]{2,1,0:T(8,128)(2,1)} %fusion.29), channel_id=1, source_target_pairs={{0,8},{1,9},{2,10},{3,11},{4,12},{5,13},{6,14},{7,15},{8,0},{9,1},... | collective-permute-start | bytes 442376 | tf_op jit(solution)/shard_map/ppermute | solution.py:49
  555.9 33.4 %collective-permute-start.88 = (bf16[384,1536]{1,0:T(8,128)(2,1)S(1)}, bf16[384,1536]{1,0:T(8,128)(2,1)}, u32[]{:S(2)}, u32[]{:S(2)}) collective-permute-start(bf16[384,1536]{1,0:T(8,128)(2,1)S(1)} %add_convert_fusion.1), channel_id=1, source_target_pairs={{0,2},{1,5},{2,0},{3,7},{4,6},{5,1},{6,4},{7,3},{8,10},{9,13},{10,... | collective-permute-start | bytes 3538952 | tf_op jit(solution)/shard_map/ppermute | solution.py:49
  (187 other events, 2158.2 us)

commit v6 on v5

--- a/solution.py
+++ b/solution.py
@@ -769,10 +769,11 @@
     patch = jnp.concatenate([patch_embed.astype(BF), norm_params.astype(BF).reshape(-1, rows)], 0).T
     patch = far(patch)
     attn[0] = over(attn[0], one)
+    attn[1], attn[2] = together(attn[1], attn[2])
     steps.next()
     attn[0] = flat(over(attn[0], two))
     ff[0] = over(ff[0], one)
-    attn[1], attn[2] = together(attn[1], attn[2])
+    head = over(head_unit, one)
     patch = over(patch, [low]).reshape(width, -1)
     steps.next()
     ff[0] = flat(over(ff[0], two))
@@ -807,14 +808,13 @@
     steps.next()
     attn[2] = across(attn[2])
     ff[2] = near(ff[2])
-    head = over(head_unit, one)
+    head = over(head, two)
     prepared = run_prepare(2, run_ff(1, adds))
     steps.next()
     ff[2] = across(ff[2])
-    head = over(head, two)
+    head = over(head, [low]).reshape(-1, rows + 2 * images, half)
     adds = run_attn(2, *prepared)
     steps.next()
-    head = over(head, [low]).reshape(-1, rows + 2 * images, half)
     teach = head[:, rows : rows + images].astype(F32) + head[:, rows + images :].astype(F32)
     head = head[:, :rows].reshape(width, half)
     adds = run_ff(2, adds)

time: 713 us -> 696 us (0.976)
  waiting for transfers between devices: 228 us -> 214 us
    ppermute x110, waiting for transfers between devices: 228 us -> 214 us  [swap(): return lax.ppermute(value, AXES, pairs)]
  transfers between devices with their start and end apart: 110 -> 110, of which waited for: 43 -> 41; matrix products, arithmetic and copies ran while one was open for 13% -> 13% of each run, Pallas kernels for 30% -> 30%
where the time goes in v6:
time: 696 us; the launch traced here: 690 us
  Pallas kernels  240 us (34%)
  waiting for transfers between devices  214 us (31%)
  starting transfers between devices  102 us (15%)
  other arithmetic  69.7 us (10%)
  local copies, waits for them, and re-layouts  42.3 us (6%)
  between operations  12.9 us (2%)
  matrix products  9.2 us (1%)
    ppermute x110, waiting for transfers between devices, swap(): return lax.ppermute(value, AXES, pairs)  214 us
    ppermute x110, starting transfers between devices, swap(): return lax.ppermute(value, AXES, pairs)  102 us
    pallas_call x3, Pallas kernels, attn_backward(): pl.pallas_call(functools.partial(attn_back_kernel, len(back)), grid=(step...  74.1 us
    pallas_call x3, Pallas kernels, ff_backward(): pl.pallas_call(functools.partial(ff_back_kernel, len(back)), grid=(steps,...  56.9 us
    pallas_call x3, Pallas kernels, ff_forward(): pl.pallas_call(functools.partial(ff_fwd_kernel, len(adds)), grid=(steps,)...  36.9 us
    pallas_call x3, Pallas kernels, attn_forward(): pl.pallas_call(attn_fwd_kernel, grid=(steps,), in_specs=[FLAG, FLAG] + [f...  36.1 us
    another operation x18, other arithmetic, over(): unit = jnp.stack([unit, steps.swap(unit, bit)])  14.1 us
  transfers between devices with their start and end apart: 110, of which 41 were waited for; matrix products, arithmetic and copies ran while one was open for 13% of the time, Pallas kernels for 30%

profile of v6, /device:TPU:0, one launch (start us, length us, event | category | flops | bytes accessed | tf_op | source)
XLA Modules:
  0.0 689.6 jit_solution(7377461381004708970)
XLA Ops:
  50.6 10.5 %collective-permute-done.8 = bf16[112,500]{1,0:T(8,128)(2,1)S(1)} collective-permute-done((bf16[112,500]{1,0:T(8,128)(2,1)}, bf16[112,500]{1,0:T(8,128)(2,1)S(1)}, u32[]{:S(2)}, u32[]{:S(2)}) %collective-permute-start.8) | collective-permute-done | bytes 112032 | tf_op jit(solution)/shard_map/ppermute | solution.py:49
  80.7 20.9 %collective-permute-done.11 = bf16[2,96,1536]{2,1,0:T(8,128)(2,1)} collective-permute-done((bf16[2,96,1536]{2,1,0:T(8,128)(2,1)}, bf16[2,96,1536]{2,1,0:T(8,128)(2,1)}, u32[]{:S(2)}, u32[]{:S(2)}) %collective-permute-start.11) | collective-permute-done | bytes 589856 | tf_op jit(solution)/shard_map/ppermute | solution.py:49
  121.3 11.4 %collective-permute-done.19 = bf16[2,96,768]{1,2,0:T(8,128)(2,1)S(1)} collective-permute-done((bf16[2,96,768]{1,2,0:T(8,128)(2,1)S(1)}, bf16[2,96,768]{1,2,0:T(8,128)(2,1)S(1)}, u32[]{:S(2)}, u32[]{:S(2)}) %collective-permute-start.19) | collective-permute-done | bytes 294944 | tf_op jit(solution)/shard_map/ppermute | solution.py:49
  132.7 10.1 %collective-permute-done.17.refs_3_.refs_17_ = bf16[384,768]{1,0:T(8,128)(2,1)S(1)} collective-permute-done((bf16[384,768]{1,0:T(8,128)(2,1)}, bf16[384,768]{1,0:T(8,128)(2,1)S(1)}, u32[]{:S(2)}, u32[]{:S(2)}) %collective-permute-start.17) | collective-permute-done | bytes 589856 | tf_op jit(solution)/shard_map/ppermute | solution.py:49
  149.0 12.3 %attn_forward.3 = (bf16[2,592,768]{2,1,0:T(8,128)(2,1)}, bf16[576,768]{1,0:T(8,128)(2,1)}) custom-call(s32[1]{0:T(128)} %bitcast.flag.refs_0_, f32[1]{0:T(128)} %bitcast.1.away.refs_1_, bf16[576,768]{1,0:T(8,128)(2,1)} %get-tuple-element.231.normed, f32[1,768]{1,0:T(1,128)} %copy-done.96, s32[576,1]{1,0:T(8,128)} %broadcast_in_dim.60.segq.refs_10_, ...), custom_call_target="tpu_custom_call" | custom-call | flops 1000000 | bytes 10000 | tf_op jit(solution)/shard_map/attn_forward/pallas_call | solution.py:293
  163.4 9.8 %collective-permute-done.24 = bf16[2,96,1536]{2,1,0:T(8,128)(2,1)} collective-permute-done((bf16[2,96,1536]{2,1,0:T(8,128)(2,1)S(1)}, bf16[2,96,1536]{2,1,0:T(8,128)(2,1)}, u32[]{:S(2)}, u32[]{:S(2)}) %collective-permute-start.24) | collective-permute-done | bytes 589856 | tf_op jit(solution)/shard_map/ppermute | solution.py:49
  179.5 12.3 %ff_forward.3 = (f32[576,768]{1,0:T(8,128)}, bf16[576,768]{1,0:T(8,128)(2,1)}) custom-call(s32[1]{0:T(128)} %bitcast.flag.refs_0_, f32[576,768]{1,0:T(8,128)} %get-tuple-element.233.refs_1_.refs_7_.value, bf16[576,768]{1,0:T(8,128)(2,1)} %get-tuple-element.232.refs_2_, bf16[576,768]{1,0:T(8,128)(2,1)} %collective-permute-done.25.refs_3_, ...), custom_call_target="tpu_custom_call" | custom-call | flops 1000000 | bytes 10000 | tf_op jit(solution)/shard_map/ff_forward/pallas_call | solution.py:346
  202.0 11.2 %collective-permute-done.30 = bf16[2,96,768]{1,2,0:T(8,128)(2,1)S(1)} collective-permute-done((bf16[2,96,768]{1,2,0:T(8,128)(2,1)S(1)}, bf16[2,96,768]{1,2,0:T(8,128)(2,1)S(1)}, u32[]{:S(2)}, u32[]{:S(2)}) %collective-permute-start.30) | collective-permute-done | bytes 294944 | tf_op jit(solution)/shard_map/ppermute | solution.py:49
  216.2 11.9 %attn_forward.4 = (bf16[2,592,768]{2,1,0:T(8,128)(2,1)}, bf16[576,768]{1,0:T(8,128)(2,1)}) custom-call(s32[1]{0:T(128)} %bitcast.flag.refs_0_, f32[1]{0:T(128)} %bitcast.1.away.refs_1_, bf16[576,768]{1,0:T(8,128)(2,1)} %get-tuple-element.246.normed, f32[1,768]{1,0:T(1,128)} %copy-done.97, s32[576,1]{1,0:T(8,128)} %broadcast_in_dim.60.segq.refs_10_, ...), custom_call_target="tpu_custom_call" | custom-call | flops 1000000 | bytes 10000 | tf_op jit(solution)/shard_map/attn_forward/pallas_call | solution.py:293
  230.7 12.5 %collective-permute-done.35 = bf16[2,96,1536]{2,1,0:T(8,128)(2,1)} collective-permute-done((bf16[2,96,1536]{2,1,0:T(8,128)(2,1)S(1)}, bf16[2,96,1536]{2,1,0:T(8,128)(2,1)}, u32[]{:S(2)}, u32[]{:S(2)}) %collective-permute-start.35) | collective-permute-done | bytes 589856 | tf_op jit(solution)/shard_map/ppermute | solution.py:49
  247.3 12.3 %ff_forward.4 = (f32[576,768]{1,0:T(8,128)}, bf16[576,768]{1,0:T(8,128)(2,1)}) custom-call(s32[1]{0:T(128)} %bitcast.flag.refs_0_, f32[576,768]{1,0:T(8,128)} %get-tuple-element.248.refs_1_.refs_7_.refs_2_, bf16[576,768]{1,0:T(8,128)(2,1)} %get-tuple-element.247.refs_2_, bf16[576,768]{1,0:T(8,128)(2,1)} %collective-permute-done.36.refs_3_, ...), custom_call_target="tpu_custom_call" | custom-call | flops 1000000 | bytes 10000 | tf_op jit(solution)/shard_map/ff_forward/pallas_call | solution.py:346
  280.6 11.9 %attn_forward.5 = (bf16[2,592,768]{2,1,0:T(8,128)(2,1)}, bf16[576,768]{1,0:T(8,128)(2,1)}) custom-call(s32[1]{0:T(128)} %bitcast.flag.refs_0_, f32[1]{0:T(128)} %bitcast.1.away.refs_1_, bf16[576,768]{1,0:T(8,128)(2,1)} %get-tuple-element.260.normed, f32[1,768]{1,0:T(1,128)} %copy-done.98, s32[576,1]{1,0:T(8,128)} %broadcast_in_dim.60.segq.refs_10_, ...), custom_call_target="tpu_custom_call" | custom-call | flops 1000000 | bytes 10000 | tf_op jit(solution)/shard_map/attn_forward/pallas_call | solution.py:293
  294.0 11.7 %collective-permute-done.44 = bf16[2,2,112,500]{3,2,1,0:T(8,128)(2,1)S(1)} collective-permute-done((bf16[2,2,112,500]{3,2,1,0:T(8,128)(2,1)S(1)}, bf16[2,2,112,500]{3,2,1,0:T(8,128)(2,1)S(1)}, u32[]{:S(2)}, u32[]{:S(2)}) %collective-permute-start.44) | collective-permute-done | bytes 448032 | tf_op jit(solution)/shard_map/ppermute | solution.py:49
  307.1 12.3 %ff_forward.5 = (f32[576,768]{1,0:T(8,128)}, bf16[576,768]{1,0:T(8,128)(2,1)}) custom-call(s32[1]{0:T(128)} %bitcast.flag.refs_0_, f32[576,768]{1,0:T(8,128)} %get-tuple-element.262.refs_1_.refs_7_.refs_2_, bf16[576,768]{1,0:T(8,128)(2,1)} %get-tuple-element.261.refs_2_, bf16[576,768]{1,0:T(8,128)(2,1)} %copy-done.48, ...), custom_call_target="tpu_custom_call" | custom-call | flops 1000000 | bytes 10000 | tf_op jit(solution)/shard_map/ff_forward/pallas_call | solution.py:346
  333.4 17.1 %ff_backward.3 = (f32[576,768]{1,0:T(8,128)}, bf16[384,1536]{1,0:T(8,128)(2,1)}, bf16[384,1536]{1,0:T(8,128)(2,1)}, bf16[384,1536]{1,0:T(8,128)(2,1)}, bf16[384,...) custom-call(s32[1]{0:T(128)} %bitcast.flag.refs_0_, f32[576,768]{1,0:T(8,128)} %fusion.36.refs_1_, ...), custom_call_target="tpu_custom_call" | custom-call | flops 1000000 | bytes 10000 | tf_op jit(solution)/shard_map/ff_backward/pallas_call | solution.py:434
  356.1 24.9 %attn_backward.3 = (f32[576,768]{1,0:T(8,128)}, bf16[384,768]{1,0:T(8,128)(2,1)}, bf16[384,768]{1,0:T(8,128)(2,1)}, bf16[384,768]{1,0:T(8,128)(2,1)}, bf16[384,7...) custom-call(s32[1]{0:T(128)} %bitcast.flag.refs_0_, f32[1]{0:T(128)} %bitcast.1.away.refs_1_, ...), custom_call_target="tpu_custom_call" | custom-call | flops 1000000 | bytes 10000 | tf_op jit(solution)/shard_map/attn_backward/pallas_call | solution.py:515
  390.6 19.8 %ff_backward.4 = (f32[576,768]{1,0:T(8,128)}, bf16[384,1536]{1,0:T(8,128)(2,1)}, bf16[384,1536]{1,0:T(8,128)(2,1)}, bf16[384,1536]{1,0:T(8,128)(2,1)}, bf16[384,...) custom-call(s32[1]{0:T(128)} %bitcast.flag.refs_0_, f32[576,768]{1,0:T(8,128)} %get-tuple-element.277.refs_1_, ...), custom_call_target="tpu_custom_call" | custom-call | flops 1000000 | bytes 10000 | tf_op jit(solution)/shard_map/ff_backward/pallas_call | solution.py:434
  421.4 24.6 %attn_backward.4 = (f32[576,768]{1,0:T(8,128)}, bf16[384,768]{1,0:T(8,128)(2,1)}, bf16[384,768]{1,0:T(8,128)(2,1)}, bf16[384,768]{1,0:T(8,128)(2,1)}, bf16[384,7...) custom-call(s32[1]{0:T(128)} %bitcast.flag.refs_0_, f32[1]{0:T(128)} %bitcast.1.away.refs_1_, ...), custom_call_target="tpu_custom_call" | custom-call | flops 1000000 | bytes 10000 | tf_op jit(solution)/shard_map/attn_backward/pallas_call | solution.py:515
  466.9 20.0 %ff_backward.5 = (f32[576,768]{1,0:T(8,128)}, bf16[384,1536]{1,0:T(8,128)(2,1)}, bf16[384,1536]{1,0:T(8,128)(2,1)}, bf16[384,1536]{1,0:T(8,128)(2,1)}, bf16[384,...) custom-call(s32[1]{0:T(128)} %bitcast.flag.refs_0_, f32[576,768]{1,0:T(8,128)} %get-tuple-element.300.refs_1_, ...), custom_call_target="tpu_custom_call" | custom-call | flops 1000000 | bytes 10000 | tf_op jit(solution)/shard_map/ff_backward/pallas_call | solution.py:434
  497.3 24.7 %attn_backward.5 = (f32[576,768]{1,0:T(8,128)}, bf16[384,768]{1,0:T(8,128)(2,1)}, bf16[384,768]{1,0:T(8,128)(2,1)}, bf16[384,768]{1,0:T(8,128)(2,1)}, bf16[384,7...) custom-call(s32[1]{0:T(128)} %bitcast.flag.refs_0_, f32[1]{0:T(128)} %bitcast.1.away.refs_1_, ...), custom_call_target="tpu_custom_call" | custom-call | flops 1000000 | bytes 10000 | tf_op jit(solution)/shard_map/attn_backward/pallas_call | solution.py:515
  597.1 11.7 %collective-permute-done.93 = bf16[2,96,1536]{2,1,0:T(8,128)(2,1)S(1)} collective-permute-done((bf16[2,96,1536]{2,1,0:T(8,128)(2,1)S(1)}, bf16[2,96,1536]{2,1,0:T(8,128)(2,1)S(1)}, u32[]{:S(2)}, u32[]{:S(2)}) %collective-permute-start.93) | collective-permute-done | bytes 589856 | tf_op jit(solution)/shard_map/ppermute | solution.py:49
  617.1 10.8 %collective-permute-done.96 = bf16[1,96,1536]{2,1,0:T(8,128)(2,1)S(1)} collective-permute-done((bf16[1,96,1536]{2,1,0:T(8,128)(2,1)}, bf16[1,96,1536]{2,1,0:T(8,128)(2,1)S(1)}, u32[]{:S(2)}, u32[]{:S(2)}) %collective-permute-start.96) | collective-permute-done | bytes 294944 | tf_op jit(solution)/shard_map/ppermute | solution.py:49
  627.9 8.8 %collective-permute-done.95 = bf16[4,96,768]{2,1,0:T(8,128)(2,1)} collective-permute-done((bf16[4,96,768]{2,1,0:T(8,128)(2,1)}, bf16[4,96,768]{2,1,0:T(8,128)(2,1)}, u32[]{:S(2)}, u32[]{:S(2)}) %collective-permute-start.95) | collective-permute-done | bytes 589856 | tf_op jit(solution)/shard_map/ppermute | solution.py:49
  675.8 12.5 %adam.1 = (f32[3,3,96,192]{3,2,1,0:T(8,128)}, f32[3,192,96]{2,1,0:T(8,128)}, f32[3,96,768]{2,1,0:T(8,128)}, f32[3,96,768]{2,1,0:T(8,128)}, f32[96,768]{1,0:T(8,1...) custom-call(f32[1]{0:T(128)} %bitcast.122.clip_ref, ...), custom_call_target="tpu_custom_call" | custom-call | tf_op jit(solution)/shard_map/adam/pallas_call | solution.py:627
  (608 shorter events, 330.8 us)
Async XLA Ops:
  72.7 28.9 %collective-permute-start.12 = (bf16[384,768]{1,0:T(8,128)(2,1)}, bf16[384,768]{1,0:T(8,128)(2,1)}, u32[]{:S(2)}, u32[]{:S(2)}) collective-permute-start(bf16[384,768]{1,0:T(8,128)(2,1)} %bitcast.43.refs_0_.refs_14_), channel_id=1, source_target_pairs={{0,2},{1,5},{2,0},{3,7},{4,6},{5,1},{6,4},{7,3},{8,10},{9,13},{10,... | collective-permute-start | bytes 1769480 | tf_op jit(solution)/shard_map/ppermute | solution.py:49
  74.2 30.8 %collective-permute-start.13 = (bf16[384,768]{1,0:T(8,128)(2,1)}, bf16[384,768]{1,0:T(8,128)(2,1)}, u32[]{:S(2)}, u32[]{:S(2)}) collective-permute-start(bf16[384,768]{1,0:T(8,128)(2,1)} %bitcast.43.refs_0_.refs_14_), channel_id=1, source_target_pairs={{0,4},{1,3},{2,6},{3,1},{4,0},{5,7},{6,2},{7,5},{8,12},{9,11},{10,... | collective-permute-start | bytes 1769480 | tf_op jit(solution)/shard_map/ppermute | solution.py:49
  108.1 34.8 %collective-permute-start.16 = (bf16[384,1536]{1,0:T(8,128)(2,1)S(1)}, bf16[384,1536]{1,0:T(8,128)(2,1)S(1)}, u32[]{:S(2)}, u32[]{:S(2)}) collective-permute-start(bf16[384,1536]{1,0:T(8,128)(2,1)S(1)} %bitcast.291), channel_id=1, source_target_pairs={{0,2},{1,5},{2,0},{3,7},{4,6},{5,1},{6,4},{7,3},{8,10},{9,13},{10,... | collective-permute-start | bytes 3538952 | tf_op jit(solution)/shard_map/ppermute | solution.py:49
  108.7 34.2 %collective-permute-start.18 = (bf16[384,1536]{1,0:T(8,128)(2,1)S(1)}, bf16[384,1536]{1,0:T(8,128)(2,1)S(1)}, u32[]{:S(2)}, u32[]{:S(2)}) collective-permute-start(bf16[384,1536]{1,0:T(8,128)(2,1)S(1)} %bitcast.292), channel_id=1, source_target_pairs={{0,4},{1,3},{2,6},{3,1},{4,0},{5,7},{6,2},{7,5},{8,12},{9,11},{10,... | collective-permute-start | bytes 3538952 | tf_op jit(solution)/shard_map/ppermute | solution.py:49
  112.5 30.4 %collective-permute-start.17 = (bf16[384,768]{1,0:T(8,128)(2,1)}, bf16[384,768]{1,0:T(8,128)(2,1)S(1)}, u32[]{:S(2)}, u32[]{:S(2)}) collective-permute-start(bf16[384,768]{1,0:T(8,128)(2,1)} %collective-permute-done.12.refs_1_.refs_15_), channel_id=1, source_target_pairs={{0,4},{1,3},{2,6},{3,1},{4,0},{5,7},{6,2},{7,5},{8,12},{9,11},{10,... | collective-permute-start | bytes 1769480 | tf_op jit(solution)/shard_map/ppermute | solution.py:49
  144.0 33.8 %collective-permute-start.21 = (bf16[384,1536]{1,0:T(8,128)(2,1)S(1)}, bf16[384,1536]{1,0:T(8,128)(2,1)}, u32[]{:S(2)}, u32[]{:S(2)}) collective-permute-start(bf16[384,1536]{1,0:T(8,128)(2,1)S(1)} %collective-permute-done.16.refs_6_.refs_12_), channel_id=1, source_target_pairs={{0,4},{1,3},{2,6},{3,1},{4,0},{5,7},{6,2},{7,5},{8,12},{9,11},{10,... | collective-permute-start | bytes 3538952 | tf_op jit(solution)/shard_map/ppermute | solution.py:49
  177.8 35.4 %collective-permute-start.27 = (bf16[384,1536]{1,0:T(8,128)(2,1)S(1)}, bf16[384,1536]{1,0:T(8,128)(2,1)S(1)}, u32[]{:S(2)}, u32[]{:S(2)}) collective-permute-start(bf16[384,1536]{1,0:T(8,128)(2,1)S(1)} %bitcast.295), channel_id=1, source_target_pairs={{0,2},{1,5},{2,0},{3,7},{4,6},{5,1},{6,4},{7,3},{8,10},{9,13},{10,... | collective-permute-start | bytes 3538952 | tf_op jit(solution)/shard_map/ppermute | solution.py:49
  178.5 34.8 %collective-permute-start.29 = (bf16[384,1536]{1,0:T(8,128)(2,1)S(1)}, bf16[384,1536]{1,0:T(8,128)(2,1)S(1)}, u32[]{:S(2)}, u32[]{:S(2)}) collective-permute-start(bf16[384,1536]{1,0:T(8,128)(2,1)S(1)} %bitcast.296), channel_id=1, source_target_pairs={{0,4},{1,3},{2,6},{3,1},{4,0},{5,7},{6,2},{7,5},{8,12},{9,11},{10,... | collective-permute-start | bytes 3538952 | tf_op jit(solution)/shard_map/ppermute | solution.py:49
  213.3 31.4 %collective-permute-start.32 = (bf16[384,1536]{1,0:T(8,128)(2,1)S(1)}, bf16[384,1536]{1,0:T(8,128)(2,1)}, u32[]{:S(2)}, u32[]{:S(2)}) collective-permute-start(bf16[384,1536]{1,0:T(8,128)(2,1)S(1)} %collective-permute-done.27.refs_6_.refs_12_), channel_id=1, source_target_pairs={{0,4},{1,3},{2,6},{3,1},{4,0},{5,7},{6,2},{7,5},{8,12},{9,11},{10,... | collective-permute-start | bytes 3538952 | tf_op jit(solution)/shard_map/ppermute | solution.py:49
  244.7 34.4 %collective-permute-start.38 = (bf16[384,1536]{1,0:T(8,128)(2,1)S(1)}, bf16[384,1536]{1,0:T(8,128)(2,1)S(1)}, u32[]{:S(2)}, u32[]{:S(2)}) collective-permute-start(bf16[384,1536]{1,0:T(8,128)(2,1)S(1)} %bitcast.299), channel_id=1, source_target_pairs={{0,2},{1,5},{2,0},{3,7},{4,6},{5,1},{6,4},{7,3},{8,10},{9,13},{10,... | collective-permute-start | bytes 3538952 | tf_op jit(solution)/shard_map/ppermute | solution.py:49
  246.1 33.0 %collective-permute-start.40 = (bf16[384,1536]{1,0:T(8,128)(2,1)S(1)}, bf16[384,1536]{1,0:T(8,128)(2,1)S(1)}, u32[]{:S(2)}, u32[]{:S(2)}) collective-permute-start(bf16[384,1536]{1,0:T(8,128)(2,1)S(1)} %bitcast.300), channel_id=1, source_target_pairs={{0,4},{1,3},{2,6},{3,1},{4,0},{5,7},{6,2},{7,5},{8,12},{9,11},{10,... | collective-permute-start | bytes 3538952 | tf_op jit(solution)/shard_map/ppermute | solution.py:49
  350.6 32.1 %collective-permute-start.51 = (bf16[384,1536]{1,0:T(8,128)(2,1)}, bf16[384,1536]{1,0:T(8,128)(2,1)S(1)}, u32[]{:S(2)}, u32[]{:S(2)}) collective-permute-start(bf16[384,1536]{1,0:T(8,128)(2,1)} %get-tuple-element.271), channel_id=1, source_target_pairs={{0,4},{1,3},{2,6},{3,1},{4,0},{5,7},{6,2},{7,5},{8,12},{9,11},{10,... | collective-permute-start | bytes 3538952 | tf_op jit(solution)/shard_map/ppermute | solution.py:49
  351.7 34.3 %collective-permute-start.52 = (bf16[384,1536]{1,0:T(8,128)(2,1)}, bf16[384,1536]{1,0:T(8,128)(2,1)S(1)}, u32[]{:S(2)}, u32[]{:S(2)}) collective-permute-start(bf16[384,1536]{1,0:T(8,128)(2,1)} %get-tuple-element.273), channel_id=1, source_target_pairs={{0,4},{1,3},{2,6},{3,1},{4,0},{5,7},{6,2},{7,5},{8,12},{9,11},{10,... | collective-permute-start | bytes 3538952 | tf_op jit(solution)/shard_map/ppermute | solution.py:49
  352.8 30.2 %collective-permute-start.53 = (bf16[2,96,500]{2,1,0:T(8,128)(2,1)S(1)}, bf16[2,96,500]{2,1,0:T(8,128)(2,1)S(1)}, u32[]{:S(2)}, u32[]{:S(2)}) collective-permute-start(bf16[2,96,500]{2,1,0:T(8,128)(2,1)S(1)} %pad_maximum_fusion.35), channel_id=1, source_target_pairs={{0,16},{1,17},{2,18},{3,19},{4,20},{5,21},{6,22},{7,23},{8,24},{9,... | collective-permute-start | bytes 576008 | tf_op jit(solution)/shard_map/ppermute | solution.py:49
  414.1 36.1 %collective-permute-start.62 = (bf16[384,1536]{1,0:T(8,128)(2,1)}, bf16[384,1536]{1,0:T(8,128)(2,1)S(1)}, u32[]{:S(2)}, u32[]{:S(2)}) collective-permute-start(bf16[384,1536]{1,0:T(8,128)(2,1)} %get-tuple-element.291), channel_id=1, source_target_pairs={{0,4},{1,3},{2,6},{3,1},{4,0},{5,7},{6,2},{7,5},{8,12},{9,11},{10,... | collective-permute-start | bytes 3538952 | tf_op jit(solution)/shard_map/ppermute | solution.py:49
  416.4 31.9 %collective-permute-start.65 = (bf16[2,96,1536]{2,1,0:T(8,128)(2,1)}, bf16[2,96,1536]{2,1,0:T(8,128)(2,1)}, u32[]{:S(2)}, u32[]{:S(2)}) collective-permute-start(bf16[2,96,1536]{2,1,0:T(8,128)(2,1)} %pad_maximum_fusion.16), channel_id=1, source_target_pairs={{0,16},{1,17},{2,18},{3,19},{4,20},{5,21},{6,22},{7,23},{8,24},{9,... | collective-permute-start | bytes 1769480 | tf_op jit(solution)/shard_map/ppermute | solution.py:49
  419.2 39.0 %collective-permute-start.63 = (bf16[384,1536]{1,0:T(8,128)(2,1)}, bf16[384,1536]{1,0:T(8,128)(2,1)S(1)}, u32[]{:S(2)}, u32[]{:S(2)}) collective-permute-start(bf16[384,1536]{1,0:T(8,128)(2,1)} %get-tuple-element.293), channel_id=1, source_target_pairs={{0,4},{1,3},{2,6},{3,1},{4,0},{5,7},{6,2},{7,5},{8,12},{9,11},{10,... | collective-permute-start | bytes 3538952 | tf_op jit(solution)/shard_map/ppermute | solution.py:49
  458.2 29.8 %collective-permute-start.71 = (bf16[384,1536]{1,0:T(8,128)(2,1)S(1)}, bf16[384,1536]{1,0:T(8,128)(2,1)S(1)}, u32[]{:S(2)}, u32[]{:S(2)}) collective-permute-start(bf16[384,1536]{1,0:T(8,128)(2,1)S(1)} %add_convert_fusion.3), channel_id=1, source_target_pairs={{0,2},{1,5},{2,0},{3,7},{4,6},{5,1},{6,4},{7,3},{8,10},{9,13},{10,... | collective-permute-start | bytes 3538952 | tf_op jit(solution)/shard_map/ppermute | solution.py:49
  488.1 34.7 %collective-permute-start.77 = (bf16[384,768]{1,0:T(8,128)(2,1)}, bf16[384,768]{1,0:T(8,128)(2,1)S(1)}, u32[]{:S(2)}, u32[]{:S(2)}) collective-permute-start(bf16[384,768]{1,0:T(8,128)(2,1)} %add_convert_fusion.10), channel_id=1, source_target_pairs={{0,2},{1,5},{2,0},{3,7},{4,6},{5,1},{6,4},{7,3},{8,10},{9,13},{10,... | collective-permute-start | bytes 1769480 | tf_op jit(solution)/shard_map/ppermute | solution.py:49
  489.9 35.0 %collective-permute-start.78 = (bf16[2,96,1536]{2,1,0:T(8,128)(2,1)S(1)}, bf16[2,96,1536]{2,1,0:T(8,128)(2,1)S(1)}, u32[]{:S(2)}, u32[]{:S(2)}) collective-permute-start(bf16[2,96,1536]{2,1,0:T(8,128)(2,1)S(1)} %pad_maximum_fusion.17), channel_id=1, source_target_pairs={{0,16},{1,17},{2,18},{3,19},{4,20},{5,21},{6,22},{7,23},{8,24},{9,... | collective-permute-start | bytes 1769480 | tf_op jit(solution)/shard_map/ppermute | solution.py:49
  492.0 40.0 %collective-permute-start.75 = (bf16[384,1536]{1,0:T(8,128)(2,1)}, bf16[384,1536]{1,0:T(8,128)(2,1)S(1)}, u32[]{:S(2)}, u32[]{:S(2)}) collective-permute-start(bf16[384,1536]{1,0:T(8,128)(2,1)} %get-tuple-element.316), channel_id=1, source_target_pairs={{0,4},{1,3},{2,6},{3,1},{4,0},{5,7},{6,2},{7,5},{8,12},{9,11},{10,... | collective-permute-start | bytes 3538952 | tf_op jit(solution)/shard_map/ppermute | solution.py:49
  493.0 39.1 %collective-permute-start.76 = (bf16[384,1536]{1,0:T(8,128)(2,1)}, bf16[384,1536]{1,0:T(8,128)(2,1)S(1)}, u32[]{:S(2)}, u32[]{:S(2)}) collective-permute-start(bf16[384,1536]{1,0:T(8,128)(2,1)} %get-tuple-element.318), channel_id=1, source_target_pairs={{0,4},{1,3},{2,6},{3,1},{4,0},{5,7},{6,2},{7,5},{8,12},{9,11},{10,... | collective-permute-start | bytes 3538952 | tf_op jit(solution)/shard_map/ppermute | solution.py:49
  495.6 36.4 %collective-permute-start.79 = (bf16[1,96,768]{2,1,0:T(8,128)(2,1)}, bf16[1,96,768]{2,1,0:T(8,128)(2,1)}, u32[]{:S(2)}, u32[]{:S(2)}) collective-permute-start(bf16[1,96,768]{2,1,0:T(8,128)(2,1)} %fusion.29), channel_id=1, source_target_pairs={{0,8},{1,9},{2,10},{3,11},{4,12},{5,13},{6,14},{7,15},{8,0},{9,1},... | collective-permute-start | bytes 442376 | tf_op jit(solution)/shard_map/ppermute | solution.py:49
  544.0 33.6 %collective-permute-start.88 = (bf16[384,1536]{1,0:T(8,128)(2,1)S(1)}, bf16[384,1536]{1,0:T(8,128)(2,1)}, u32[]{:S(2)}, u32[]{:S(2)}) collective-permute-start(bf16[384,1536]{1,0:T(8,128)(2,1)S(1)} %add_convert_fusion.1), channel_id=1, source_target_pairs={{0,2},{1,5},{2,0},{3,7},{4,6},{5,1},{6,4},{7,3},{8,10},{9,13},{10,... | collective-permute-start | bytes 3538952 | tf_op jit(solution)/shard_map/ppermute | solution.py:49
  (188 other events, 2151.2 us)

commit v7 on v6

--- a/solution.py
+++ b/solution.py
@@ -32,7 +32,6 @@
 AXES = ("dp", "mp")
 INNER = ("mp", 1)
 OUTER = ("mp", 2)
-DIAGONAL = ("mp", 3)
 LOW = ("dp", 1)
 FIRST = (LOW, OUTER)
 SECOND = (OUTER, LOW)
@@ -892,7 +891,8 @@
         g_norms[2 * l + 1] = g_above
         steps.add(own)
         row = row[:8]
-        rows_in = [steps.add(swap(row, OUTER)), steps.add(swap(row, DIAGONAL))]
+        got = steps.add(swap(row, OUTER))
+        rows_in = [got, swap(got, INNER)]
         return [d_mid, xs[l], norms[2 * l], own, swap(own, INNER), *rows_in, real]
 
     g["head"] = (g_head[:mid], g_head[mid:])

time: 696 us -> 690 us (level)
    unnamed x206 -> x204, local copies, waits for them, and re-layouts: 13.5 us -> 15.4 us
  transfers between devices with their start and end apart: 110 -> 110, of which waited for: 41 -> 42; matrix products, arithmetic and copies ran while one was open for 13% -> 13% of each run, Pallas kernels for 30% -> 30%
where the time goes in v7:
time: 690 us; the launch traced here: 684 us
  Pallas kernels  240 us (35%)
  waiting for transfers between devices  208 us (30%)
  starting transfers between devices  102 us (15%)
  other arithmetic  67.4 us (10%)
  local copies, waits for them, and re-layouts  44.3 us (6%)
  between operations  12.8 us (2%)
  matrix products  9.2 us (1%)
    ppermute x110, waiting for transfers between devices, swap(): return lax.ppermute(value, AXES, pairs)  208 us
    ppermute x110, starting transfers between devices, swap(): return lax.ppermute(value, AXES, pairs)  102 us
    pallas_call x3, Pallas kernels, attn_backward(): pl.pallas_call(functools.partial(attn_back_kernel, len(back)), grid=(step...  74 us
    pallas_call x3, Pallas kernels, ff_backward(): pl.pallas_call(functools.partial(ff_back_kernel, len(back)), grid=(steps,...  57 us
    pallas_call x3, Pallas kernels, ff_forward(): pl.pallas_call(functools.partial(ff_fwd_kernel, len(adds)), grid=(steps,)...  36.9 us
    pallas_call x3, Pallas kernels, attn_forward(): pl.pallas_call(attn_fwd_kernel, grid=(steps,), in_specs=[FLAG, FLAG] + [f...  36.1 us
    unnamed x204, local copies, waits for them, and re-layouts  15.4 us
    another operation x18, other arithmetic, over(): unit = jnp.stack([unit, steps.swap(unit, bit)])  14.1 us
  transfers between devices with their start and end apart: 110, of which 42 were waited for; matrix products, arithmetic and copies ran while one was open for 13% of the time, Pallas kernels for 30%

profile of v7, /device:TPU:0, one launch (start us, length us, event | category | flops | bytes accessed | tf_op | source)
XLA Modules:
  0.0 683.7 jit_solution(14956906579369778338)
XLA Ops:
  50.5 10.5 %collective-permute-done.8 = bf16[112,500]{1,0:T(8,128)(2,1)S(1)} collective-permute-done((bf16[112,500]{1,0:T(8,128)(2,1)}, bf16[112,500]{1,0:T(8,128)(2,1)S(1)}, u32[]{:S(2)}, u32[]{:S(2)}) %collective-permute-start.8) | collective-permute-done | bytes 112032 | tf_op jit(solution)/shard_map/ppermute | solution.py:48
  80.6 20.9 %collective-permute-done.11 = bf16[2,96,1536]{2,1,0:T(8,128)(2,1)} collective-permute-done((bf16[2,96,1536]{2,1,0:T(8,128)(2,1)}, bf16[2,96,1536]{2,1,0:T(8,128)(2,1)}, u32[]{:S(2)}, u32[]{:S(2)}) %collective-permute-start.11) | collective-permute-done | bytes 589856 | tf_op jit(solution)/shard_map/ppermute | solution.py:48
  121.2 11.4 %collective-permute-done.19 = bf16[2,96,768]{1,2,0:T(8,128)(2,1)S(1)} collective-permute-done((bf16[2,96,768]{1,2,0:T(8,128)(2,1)S(1)}, bf16[2,96,768]{1,2,0:T(8,128)(2,1)S(1)}, u32[]{:S(2)}, u32[]{:S(2)}) %collective-permute-start.19) | collective-permute-done | bytes 294944 | tf_op jit(solution)/shard_map/ppermute | solution.py:48
  132.6 10.2 %collective-permute-done.17.refs_3_.refs_17_ = bf16[384,768]{1,0:T(8,128)(2,1)S(1)} collective-permute-done((bf16[384,768]{1,0:T(8,128)(2,1)}, bf16[384,768]{1,0:T(8,128)(2,1)S(1)}, u32[]{:S(2)}, u32[]{:S(2)}) %collective-permute-start.17) | collective-permute-done | bytes 589856 | tf_op jit(solution)/shard_map/ppermute | solution.py:48
  148.9 12.3 %attn_forward.3 = (bf16[2,592,768]{2,1,0:T(8,128)(2,1)}, bf16[576,768]{1,0:T(8,128)(2,1)}) custom-call(s32[1]{0:T(128)} %bitcast.flag.refs_0_, f32[1]{0:T(128)} %bitcast.1.away.refs_1_, bf16[576,768]{1,0:T(8,128)(2,1)} %get-tuple-element.231.normed, f32[1,768]{1,0:T(1,128)} %copy-done.95, s32[576,1]{1,0:T(8,128)} %broadcast_in_dim.60.segq.refs_10_, ...), custom_call_target="tpu_custom_call" | custom-call | flops 1000000 | bytes 10000 | tf_op jit(solution)/shard_map/attn_forward/pallas_call | solution.py:292
  163.3 9.8 %collective-permute-done.24 = bf16[2,96,1536]{2,1,0:T(8,128)(2,1)} collective-permute-done((bf16[2,96,1536]{2,1,0:T(8,128)(2,1)S(1)}, bf16[2,96,1536]{2,1,0:T(8,128)(2,1)}, u32[]{:S(2)}, u32[]{:S(2)}) %collective-permute-start.24) | collective-permute-done | bytes 589856 | tf_op jit(solution)/shard_map/ppermute | solution.py:48
  179.4 12.3 %ff_forward.3 = (f32[576,768]{1,0:T(8,128)}, bf16[576,768]{1,0:T(8,128)(2,1)}) custom-call(s32[1]{0:T(128)} %bitcast.flag.refs_0_, f32[576,768]{1,0:T(8,128)} %get-tuple-element.233.refs_1_.refs_7_.value, bf16[576,768]{1,0:T(8,128)(2,1)} %get-tuple-element.232.refs_2_, bf16[576,768]{1,0:T(8,128)(2,1)} %collective-permute-done.25.refs_3_, ...), custom_call_target="tpu_custom_call" | custom-call | flops 1000000 | bytes 10000 | tf_op jit(solution)/shard_map/ff_forward/pallas_call | solution.py:345
  202.0 11.2 %collective-permute-done.30 = bf16[2,96,768]{1,2,0:T(8,128)(2,1)S(1)} collective-permute-done((bf16[2,96,768]{1,2,0:T(8,128)(2,1)S(1)}, bf16[2,96,768]{1,2,0:T(8,128)(2,1)S(1)}, u32[]{:S(2)}, u32[]{:S(2)}) %collective-permute-start.30) | collective-permute-done | bytes 294944 | tf_op jit(solution)/shard_map/ppermute | solution.py:48
  216.2 11.9 %attn_forward.4 = (bf16[2,592,768]{2,1,0:T(8,128)(2,1)}, bf16[576,768]{1,0:T(8,128)(2,1)}) custom-call(s32[1]{0:T(128)} %bitcast.flag.refs_0_, f32[1]{0:T(128)} %bitcast.1.away.refs_1_, bf16[576,768]{1,0:T(8,128)(2,1)} %get-tuple-element.246.normed, f32[1,768]{1,0:T(1,128)} %copy-done.96, s32[576,1]{1,0:T(8,128)} %broadcast_in_dim.60.segq.refs_10_, ...), custom_call_target="tpu_custom_call" | custom-call | flops 1000000 | bytes 10000 | tf_op jit(solution)/shard_map/attn_forward/pallas_call | solution.py:292
  230.6 12.5 %collective-permute-done.35 = bf16[2,96,1536]{2,1,0:T(8,128)(2,1)} collective-permute-done((bf16[2,96,1536]{2,1,0:T(8,128)(2,1)S(1)}, bf16[2,96,1536]{2,1,0:T(8,128)(2,1)}, u32[]{:S(2)}, u32[]{:S(2)}) %collective-permute-start.35) | collective-permute-done | bytes 589856 | tf_op jit(solution)/shard_map/ppermute | solution.py:48
  247.2 12.3 %ff_forward.4 = (f32[576,768]{1,0:T(8,128)}, bf16[576,768]{1,0:T(8,128)(2,1)}) custom-call(s32[1]{0:T(128)} %bitcast.flag.refs_0_, f32[576,768]{1,0:T(8,128)} %get-tuple-element.248.refs_1_.refs_7_.refs_2_, bf16[576,768]{1,0:T(8,128)(2,1)} %get-tuple-element.247.refs_2_, bf16[576,768]{1,0:T(8,128)(2,1)} %collective-permute-done.36.refs_3_, ...), custom_call_target="tpu_custom_call" | custom-call | flops 1000000 | bytes 10000 | tf_op jit(solution)/shard_map/ff_forward/pallas_call | solution.py:345
  280.5 11.9 %attn_forward.5 = (bf16[2,592,768]{2,1,0:T(8,128)(2,1)}, bf16[576,768]{1,0:T(8,128)(2,1)}) custom-call(s32[1]{0:T(128)} %bitcast.flag.refs_0_, f32[1]{0:T(128)} %bitcast.1.away.refs_1_, bf16[576,768]{1,0:T(8,128)(2,1)} %get-tuple-element.260.normed, f32[1,768]{1,0:T(1,128)} %copy-done.97, s32[576,1]{1,0:T(8,128)} %broadcast_in_dim.60.segq.refs_10_, ...), custom_call_target="tpu_custom_call" | custom-call | flops 1000000 | bytes 10000 | tf_op jit(solution)/shard_map/attn_forward/pallas_call | solution.py:292
  293.9 11.7 %collective-permute-done.44 = bf16[2,2,112,500]{3,2,1,0:T(8,128)(2,1)S(1)} collective-permute-done((bf16[2,2,112,500]{3,2,1,0:T(8,128)(2,1)S(1)}, bf16[2,2,112,500]{3,2,1,0:T(8,128)(2,1)S(1)}, u32[]{:S(2)}, u32[]{:S(2)}) %collective-permute-start.44) | collective-permute-done | bytes 448032 | tf_op jit(solution)/shard_map/ppermute | solution.py:48
  307.0 12.3 %ff_forward.5 = (f32[576,768]{1,0:T(8,128)}, bf16[576,768]{1,0:T(8,128)(2,1)}) custom-call(s32[1]{0:T(128)} %bitcast.flag.refs_0_, f32[576,768]{1,0:T(8,128)} %get-tuple-element.262.refs_1_.refs_7_.refs_2_, bf16[576,768]{1,0:T(8,128)(2,1)} %get-tuple-element.261.refs_2_, bf16[576,768]{1,0:T(8,128)(2,1)} %copy-done.49, ...), custom_call_target="tpu_custom_call" | custom-call | flops 1000000 | bytes 10000 | tf_op jit(solution)/shard_map/ff_forward/pallas_call | solution.py:345
  333.3 17.1 %ff_backward.3 = (f32[576,768]{1,0:T(8,128)}, bf16[384,1536]{1,0:T(8,128)(2,1)}, bf16[384,1536]{1,0:T(8,128)(2,1)}, bf16[384,1536]{1,0:T(8,128)(2,1)}, bf16[384,...) custom-call(s32[1]{0:T(128)} %bitcast.flag.refs_0_, f32[576,768]{1,0:T(8,128)} %fusion.36.refs_1_, ...), custom_call_target="tpu_custom_call" | custom-call | flops 1000000 | bytes 10000 | tf_op jit(solution)/shard_map/ff_backward/pallas_call | solution.py:433
  356.0 24.9 %attn_backward.3 = (f32[576,768]{1,0:T(8,128)}, bf16[384,768]{1,0:T(8,128)(2,1)}, bf16[384,768]{1,0:T(8,128)(2,1)}, bf16[384,768]{1,0:T(8,128)(2,1)}, bf16[384,7...) custom-call(s32[1]{0:T(128)} %bitcast.flag.refs_0_, f32[1]{0:T(128)} %bitcast.1.away.refs_1_, ...), custom_call_target="tpu_custom_call" | custom-call | flops 1000000 | bytes 10000 | tf_op jit(solution)/shard_map/attn_backward/pallas_call | solution.py:514
  390.9 19.8 %ff_backward.4 = (f32[576,768]{1,0:T(8,128)}, bf16[384,1536]{1,0:T(8,128)(2,1)}, bf16[384,1536]{1,0:T(8,128)(2,1)}, bf16[384,1536]{1,0:T(8,128)(2,1)}, bf16[384,...) custom-call(s32[1]{0:T(128)} %bitcast.flag.refs_0_, f32[576,768]{1,0:T(8,128)} %get-tuple-element.277.refs_1_, ...), custom_call_target="tpu_custom_call" | custom-call | flops 1000000 | bytes 10000 | tf_op jit(solution)/shard_map/ff_backward/pallas_call | solution.py:433
  419.9 24.5 %attn_backward.4 = (f32[576,768]{1,0:T(8,128)}, bf16[384,768]{1,0:T(8,128)(2,1)}, bf16[384,768]{1,0:T(8,128)(2,1)}, bf16[384,768]{1,0:T(8,128)(2,1)}, bf16[384,7...) custom-call(s32[1]{0:T(128)} %bitcast.flag.refs_0_, f32[1]{0:T(128)} %bitcast.1.away.refs_1_, ...), custom_call_target="tpu_custom_call" | custom-call | flops 1000000 | bytes 10000 | tf_op jit(solution)/shard_map/attn_backward/pallas_call | solution.py:514
  465.2 20.1 %ff_backward.5 = (f32[576,768]{1,0:T(8,128)}, bf16[384,1536]{1,0:T(8,128)(2,1)}, bf16[384,1536]{1,0:T(8,128)(2,1)}, bf16[384,1536]{1,0:T(8,128)(2,1)}, bf16[384,...) custom-call(s32[1]{0:T(128)} %bitcast.flag.refs_0_, f32[576,768]{1,0:T(8,128)} %get-tuple-element.300.refs_1_, ...), custom_call_target="tpu_custom_call" | custom-call | flops 1000000 | bytes 10000 | tf_op jit(solution)/shard_map/ff_backward/pallas_call | solution.py:433
  493.7 24.6 %attn_backward.5 = (f32[576,768]{1,0:T(8,128)}, bf16[384,768]{1,0:T(8,128)(2,1)}, bf16[384,768]{1,0:T(8,128)(2,1)}, bf16[384,768]{1,0:T(8,128)(2,1)}, bf16[384,7...) custom-call(s32[1]{0:T(128)} %bitcast.flag.refs_0_, f32[1]{0:T(128)} %bitcast.1.away.refs_1_, ...), custom_call_target="tpu_custom_call" | custom-call | flops 1000000 | bytes 10000 | tf_op jit(solution)/shard_map/attn_backward/pallas_call | solution.py:514
  592.5 10.6 %collective-permute-done.93 = bf16[2,96,1536]{2,1,0:T(8,128)(2,1)S(1)} collective-permute-done((bf16[2,96,1536]{2,1,0:T(8,128)(2,1)S(1)}, bf16[2,96,1536]{2,1,0:T(8,128)(2,1)S(1)}, u32[]{:S(2)}, u32[]{:S(2)}) %collective-permute-start.93) | collective-permute-done | bytes 589856 | tf_op jit(solution)/shard_map/ppermute | solution.py:48
  611.7 10.3 %collective-permute-done.96 = bf16[1,96,1536]{2,1,0:T(8,128)(2,1)S(1)} collective-permute-done((bf16[1,96,1536]{2,1,0:T(8,128)(2,1)}, bf16[1,96,1536]{2,1,0:T(8,128)(2,1)S(1)}, u32[]{:S(2)}, u32[]{:S(2)}) %collective-permute-start.96) | collective-permute-done | bytes 294944 | tf_op jit(solution)/shard_map/ppermute | solution.py:48
  622.0 8.8 %collective-permute-done.95 = bf16[4,96,768]{2,1,0:T(8,128)(2,1)} collective-permute-done((bf16[4,96,768]{2,1,0:T(8,128)(2,1)}, bf16[4,96,768]{2,1,0:T(8,128)(2,1)}, u32[]{:S(2)}, u32[]{:S(2)}) %collective-permute-start.95) | collective-permute-done | bytes 589856 | tf_op jit(solution)/shard_map/ppermute | solution.py:48
  669.9 12.5 %adam.1 = (f32[3,3,96,192]{3,2,1,0:T(8,128)}, f32[3,192,96]{2,1,0:T(8,128)}, f32[3,96,768]{2,1,0:T(8,128)}, f32[3,96,768]{2,1,0:T(8,128)}, f32[96,768]{1,0:T(8,1...) custom-call(f32[1]{0:T(128)} %bitcast.122.clip_ref, ...), custom_call_target="tpu_custom_call" | custom-call | tf_op jit(solution)/shard_map/adam/pallas_call | solution.py:626
  (606 shorter events, 326.6 us)
Async XLA Ops:
  72.6 28.9 %collective-permute-start.12 = (bf16[384,768]{1,0:T(8,128)(2,1)}, bf16[384,768]{1,0:T(8,128)(2,1)}, u32[]{:S(2)}, u32[]{:S(2)}) collective-permute-start(bf16[384,768]{1,0:T(8,128)(2,1)} %bitcast.43.refs_0_.refs_14_), channel_id=1, source_target_pairs={{0,2},{1,5},{2,0},{3,7},{4,6},{5,1},{6,4},{7,3},{8,10},{9,13},{10,... | collective-permute-start | bytes 1769480 | tf_op jit(solution)/shard_map/ppermute | solution.py:48
  74.1 30.8 %collective-permute-start.13 = (bf16[384,768]{1,0:T(8,128)(2,1)}, bf16[384,768]{1,0:T(8,128)(2,1)}, u32[]{:S(2)}, u32[]{:S(2)}) collective-permute-start(bf16[384,768]{1,0:T(8,128)(2,1)} %bitcast.43.refs_0_.refs_14_), channel_id=1, source_target_pairs={{0,4},{1,3},{2,6},{3,1},{4,0},{5,7},{6,2},{7,5},{8,12},{9,11},{10,... | collective-permute-start | bytes 1769480 | tf_op jit(solution)/shard_map/ppermute | solution.py:48
  76.1 28.8 %collective-permute-start.10 = (bf16[2,96,1536]{2,1,0:T(8,128)(2,1)}, bf16[2,96,1536]{2,1,0:T(8,128)(2,1)}, u32[]{:S(2)}, u32[]{:S(2)}) collective-permute-start(bf16[2,96,1536]{2,1,0:T(8,128)(2,1)} %get-tuple-element.216), channel_id=1, source_target_pairs={{0,16},{1,17},{2,18},{3,19},{4,20},{5,21},{6,22},{7,23},{8,24},{9,... | collective-permute-start | bytes 1769480 | tf_op jit(solution)/shard_map/ppermute | solution.py:48
  108.0 34.8 %collective-permute-start.16 = (bf16[384,1536]{1,0:T(8,128)(2,1)S(1)}, bf16[384,1536]{1,0:T(8,128)(2,1)S(1)}, u32[]{:S(2)}, u32[]{:S(2)}) collective-permute-start(bf16[384,1536]{1,0:T(8,128)(2,1)S(1)} %bitcast.291), channel_id=1, source_target_pairs={{0,2},{1,5},{2,0},{3,7},{4,6},{5,1},{6,4},{7,3},{8,10},{9,13},{10,... | collective-permute-start | bytes 3538952 | tf_op jit(solution)/shard_map/ppermute | solution.py:48
  108.6 34.2 %collective-permute-start.18 = (bf16[384,1536]{1,0:T(8,128)(2,1)S(1)}, bf16[384,1536]{1,0:T(8,128)(2,1)S(1)}, u32[]{:S(2)}, u32[]{:S(2)}) collective-permute-start(bf16[384,1536]{1,0:T(8,128)(2,1)S(1)} %bitcast.292), channel_id=1, source_target_pairs={{0,4},{1,3},{2,6},{3,1},{4,0},{5,7},{6,2},{7,5},{8,12},{9,11},{10,... | collective-permute-start | bytes 3538952 | tf_op jit(solution)/shard_map/ppermute | solution.py:48
  112.4 30.4 %collective-permute-start.17 = (bf16[384,768]{1,0:T(8,128)(2,1)}, bf16[384,768]{1,0:T(8,128)(2,1)S(1)}, u32[]{:S(2)}, u32[]{:S(2)}) collective-permute-start(bf16[384,768]{1,0:T(8,128)(2,1)} %collective-permute-done.12.refs_1_.refs_15_), channel_id=1, source_target_pairs={{0,4},{1,3},{2,6},{3,1},{4,0},{5,7},{6,2},{7,5},{8,12},{9,11},{10,... | collective-permute-start | bytes 1769480 | tf_op jit(solution)/shard_map/ppermute | solution.py:48
  144.0 33.8 %collective-permute-start.21 = (bf16[384,1536]{1,0:T(8,128)(2,1)S(1)}, bf16[384,1536]{1,0:T(8,128)(2,1)}, u32[]{:S(2)}, u32[]{:S(2)}) collective-permute-start(bf16[384,1536]{1,0:T(8,128)(2,1)S(1)} %collective-permute-done.16.refs_6_.refs_12_), channel_id=1, source_target_pairs={{0,4},{1,3},{2,6},{3,1},{4,0},{5,7},{6,2},{7,5},{8,12},{9,11},{10,... | collective-permute-start | bytes 3538952 | tf_op jit(solution)/shard_map/ppermute | solution.py:48
  177.7 35.4 %collective-permute-start.27 = (bf16[384,1536]{1,0:T(8,128)(2,1)S(1)}, bf16[384,1536]{1,0:T(8,128)(2,1)S(1)}, u32[]{:S(2)}, u32[]{:S(2)}) collective-permute-start(bf16[384,1536]{1,0:T(8,128)(2,1)S(1)} %bitcast.295), channel_id=1, source_target_pairs={{0,2},{1,5},{2,0},{3,7},{4,6},{5,1},{6,4},{7,3},{8,10},{9,13},{10,... | collective-permute-start | bytes 3538952 | tf_op jit(solution)/shard_map/ppermute | solution.py:48
  178.4 34.8 %collective-permute-start.29 = (bf16[384,1536]{1,0:T(8,128)(2,1)S(1)}, bf16[384,1536]{1,0:T(8,128)(2,1)S(1)}, u32[]{:S(2)}, u32[]{:S(2)}) collective-permute-start(bf16[384,1536]{1,0:T(8,128)(2,1)S(1)} %bitcast.296), channel_id=1, source_target_pairs={{0,4},{1,3},{2,6},{3,1},{4,0},{5,7},{6,2},{7,5},{8,12},{9,11},{10,... | collective-permute-start | bytes 3538952 | tf_op jit(solution)/shard_map/ppermute | solution.py:48
  213.2 31.4 %collective-permute-start.32 = (bf16[384,1536]{1,0:T(8,128)(2,1)S(1)}, bf16[384,1536]{1,0:T(8,128)(2,1)}, u32[]{:S(2)}, u32[]{:S(2)}) collective-permute-start(bf16[384,1536]{1,0:T(8,128)(2,1)S(1)} %collective-permute-done.27.refs_6_.refs_12_), channel_id=1, source_target_pairs={{0,4},{1,3},{2,6},{3,1},{4,0},{5,7},{6,2},{7,5},{8,12},{9,11},{10,... | collective-permute-start | bytes 3538952 | tf_op jit(solution)/shard_map/ppermute | solution.py:48
  244.6 34.4 %collective-permute-start.38 = (bf16[384,1536]{1,0:T(8,128)(2,1)S(1)}, bf16[384,1536]{1,0:T(8,128)(2,1)S(1)}, u32[]{:S(2)}, u32[]{:S(2)}) collective-permute-start(bf16[384,1536]{1,0:T(8,128)(2,1)S(1)} %bitcast.299), channel_id=1, source_target_pairs={{0,2},{1,5},{2,0},{3,7},{4,6},{5,1},{6,4},{7,3},{8,10},{9,13},{10,... | collective-permute-start | bytes 3538952 | tf_op jit(solution)/shard_map/ppermute | solution.py:48
  246.0 33.0 %collective-permute-start.40 = (bf16[384,1536]{1,0:T(8,128)(2,1)S(1)}, bf16[384,1536]{1,0:T(8,128)(2,1)S(1)}, u32[]{:S(2)}, u32[]{:S(2)}) collective-permute-start(bf16[384,1536]{1,0:T(8,128)(2,1)S(1)} %bitcast.300), channel_id=1, source_target_pairs={{0,4},{1,3},{2,6},{3,1},{4,0},{5,7},{6,2},{7,5},{8,12},{9,11},{10,... | collective-permute-start | bytes 3538952 | tf_op jit(solution)/shard_map/ppermute | solution.py:48
  350.4 31.9 %collective-permute-start.51 = (bf16[384,1536]{1,0:T(8,128)(2,1)}, bf16[384,1536]{1,0:T(8,128)(2,1)S(1)}, u32[]{:S(2)}, u32[]{:S(2)}) collective-permute-start(bf16[384,1536]{1,0:T(8,128)(2,1)} %get-tuple-element.271), channel_id=1, source_target_pairs={{0,4},{1,3},{2,6},{3,1},{4,0},{5,7},{6,2},{7,5},{8,12},{9,11},{10,... | collective-permute-start | bytes 3538952 | tf_op jit(solution)/shard_map/ppermute | solution.py:48
  351.6 33.9 %collective-permute-start.52 = (bf16[384,1536]{1,0:T(8,128)(2,1)}, bf16[384,1536]{1,0:T(8,128)(2,1)S(1)}, u32[]{:S(2)}, u32[]{:S(2)}) collective-permute-start(bf16[384,1536]{1,0:T(8,128)(2,1)} %get-tuple-element.273), channel_id=1, source_target_pairs={{0,4},{1,3},{2,6},{3,1},{4,0},{5,7},{6,2},{7,5},{8,12},{9,11},{10,... | collective-permute-start | bytes 3538952 | tf_op jit(solution)/shard_map/ppermute | solution.py:48
  352.7 30.0 %collective-permute-start.53 = (bf16[2,96,500]{2,1,0:T(8,128)(2,1)S(1)}, bf16[2,96,500]{2,1,0:T(8,128)(2,1)S(1)}, u32[]{:S(2)}, u32[]{:S(2)}) collective-permute-start(bf16[2,96,500]{2,1,0:T(8,128)(2,1)S(1)} %pad_maximum_fusion.35), channel_id=1, source_target_pairs={{0,16},{1,17},{2,18},{3,19},{4,20},{5,21},{6,22},{7,23},{8,24},{9,... | collective-permute-start | bytes 576008 | tf_op jit(solution)/shard_map/ppermute | solution.py:48
  413.9 36.7 %collective-permute-start.62 = (bf16[384,1536]{1,0:T(8,128)(2,1)}, bf16[384,1536]{1,0:T(8,128)(2,1)S(1)}, u32[]{:S(2)}, u32[]{:S(2)}) collective-permute-start(bf16[384,1536]{1,0:T(8,128)(2,1)} %get-tuple-element.291), channel_id=1, source_target_pairs={{0,4},{1,3},{2,6},{3,1},{4,0},{5,7},{6,2},{7,5},{8,12},{9,11},{10,... | collective-permute-start | bytes 3538952 | tf_op jit(solution)/shard_map/ppermute | solution.py:48
  416.1 32.9 %collective-permute-start.65 = (bf16[2,96,1536]{2,1,0:T(8,128)(2,1)}, bf16[2,96,1536]{2,1,0:T(8,128)(2,1)}, u32[]{:S(2)}, u32[]{:S(2)}) collective-permute-start(bf16[2,96,1536]{2,1,0:T(8,128)(2,1)} %pad_maximum_fusion.16), channel_id=1, source_target_pairs={{0,16},{1,17},{2,18},{3,19},{4,20},{5,21},{6,22},{7,23},{8,24},{9,... | collective-permute-start | bytes 1769480 | tf_op jit(solution)/shard_map/ppermute | solution.py:48
  419.0 36.5 %collective-permute-start.63 = (bf16[384,1536]{1,0:T(8,128)(2,1)}, bf16[384,1536]{1,0:T(8,128)(2,1)S(1)}, u32[]{:S(2)}, u32[]{:S(2)}) collective-permute-start(bf16[384,1536]{1,0:T(8,128)(2,1)} %get-tuple-element.293), channel_id=1, source_target_pairs={{0,4},{1,3},{2,6},{3,1},{4,0},{5,7},{6,2},{7,5},{8,12},{9,11},{10,... | collective-permute-start | bytes 3538952 | tf_op jit(solution)/shard_map/ppermute | solution.py:48
  455.4 30.2 %collective-permute-start.71 = (bf16[384,1536]{1,0:T(8,128)(2,1)S(1)}, bf16[384,1536]{1,0:T(8,128)(2,1)S(1)}, u32[]{:S(2)}, u32[]{:S(2)}) collective-permute-start(bf16[384,1536]{1,0:T(8,128)(2,1)S(1)} %add_convert_fusion.3), channel_id=1, source_target_pairs={{0,2},{1,5},{2,0},{3,7},{4,6},{5,1},{6,4},{7,3},{8,10},{9,13},{10,... | collective-permute-start | bytes 3538952 | tf_op jit(solution)/shard_map/ppermute | solution.py:48
  485.6 34.3 %collective-permute-start.77 = (bf16[384,768]{1,0:T(8,128)(2,1)S(1)}, bf16[384,768]{1,0:T(8,128)(2,1)S(1)}, u32[]{:S(2)}, u32[]{:S(2)}) collective-permute-start(bf16[384,768]{1,0:T(8,128)(2,1)S(1)} %add_convert_fusion.10), channel_id=1, source_target_pairs={{0,2},{1,5},{2,0},{3,7},{4,6},{5,1},{6,4},{7,3},{8,10},{9,13},{10,... | collective-permute-start | bytes 1769480 | tf_op jit(solution)/shard_map/ppermute | solution.py:48
  487.3 36.9 %collective-permute-start.78 = (bf16[2,96,1536]{2,1,0:T(8,128)(2,1)S(1)}, bf16[2,96,1536]{2,1,0:T(8,128)(2,1)S(1)}, u32[]{:S(2)}, u32[]{:S(2)}) collective-permute-start(bf16[2,96,1536]{2,1,0:T(8,128)(2,1)S(1)} %pad_maximum_fusion.17), channel_id=1, source_target_pairs={{0,16},{1,17},{2,18},{3,19},{4,20},{5,21},{6,22},{7,23},{8,24},{9,... | collective-permute-start | bytes 1769480 | tf_op jit(solution)/shard_map/ppermute | solution.py:48
  489.0 38.9 %collective-permute-start.75 = (bf16[384,1536]{1,0:T(8,128)(2,1)}, bf16[384,1536]{1,0:T(8,128)(2,1)S(1)}, u32[]{:S(2)}, u32[]{:S(2)}) collective-permute-start(bf16[384,1536]{1,0:T(8,128)(2,1)} %get-tuple-element.316), channel_id=1, source_target_pairs={{0,4},{1,3},{2,6},{3,1},{4,0},{5,7},{6,2},{7,5},{8,12},{9,11},{10,... | collective-permute-start | bytes 3538952 | tf_op jit(solution)/shard_map/ppermute | solution.py:48
  490.1 37.9 %collective-permute-start.76 = (bf16[384,1536]{1,0:T(8,128)(2,1)}, bf16[384,1536]{1,0:T(8,128)(2,1)S(1)}, u32[]{:S(2)}, u32[]{:S(2)}) collective-permute-start(bf16[384,1536]{1,0:T(8,128)(2,1)} %get-tuple-element.318), channel_id=1, source_target_pairs={{0,4},{1,3},{2,6},{3,1},{4,0},{5,7},{6,2},{7,5},{8,12},{9,11},{10,... | collective-permute-start | bytes 3538952 | tf_op jit(solution)/shard_map/ppermute | solution.py:48
  540.3 32.2 %collective-permute-start.88 = (bf16[384,1536]{1,0:T(8,128)(2,1)S(1)}, bf16[384,1536]{1,0:T(8,128)(2,1)}, u32[]{:S(2)}, u32[]{:S(2)}) collective-permute-start(bf16[384,1536]{1,0:T(8,128)(2,1)S(1)} %add_convert_fusion.1), channel_id=1, source_target_pairs={{0,2},{1,5},{2,0},{3,7},{4,6},{5,1},{6,4},{7,3},{8,10},{9,13},{10,... | collective-permute-start | bytes 3538952 | tf_op jit(solution)/shard_map/ppermute | solution.py:48
  (187 other events, 2058.5 us)
